TPU v7x, 32 devices: a whole 2x2x4 slice. The times are simulated.
32 devices in a mesh: dp: 4 (over x, core), head: 4 (over z), tensor: 2 (over y).
Axes of the slice: x: 2, y: 2, z: 4, core: 2. Of those that a mesh axis runs over, the one named last changes fastest.
Arguments:
- residual: bfloat16 [16384, 1536], P(('dp', 'head', 'tensor')), may hold values from -6 to 6
- segment_ids: int32 [4, 4096], P('dp'), may hold values from 0 to 5, never falling along the last dimension, each value on 1 to 2000 neighbouring positions
- norm_in_gain: float32 [1536], replicated, may hold values from 0.5 to 1.5
- w_zx: bfloat16 [1536, 2, 3072], P('dp', None, ('head', 'tensor')), may hold values from -0.15625 to 0.15625
- w_bc: bfloat16 [1536, 256], P('dp'), may hold values from -0.15625 to 0.15625
- w_dt: bfloat16 [1536, 48], P('dp', ('head', 'tensor')), may hold values from -0.15625 to 0.15625
- conv_x_weight: float32 [4, 3072], P(None, ('head', 'tensor')), may hold values from -3 to 3
- conv_x_bias: float32 [3072], P(('head', 'tensor')), may hold values from -3 to 3
- conv_bc_weight: float32 [4, 256], replicated, may hold values from -3 to 3
- conv_bc_bias: float32 [256], replicated, may hold values from -3 to 3
- dt_bias: float32 [48], P(('head', 'tensor')), may hold values from -6 to -2
- a_log: float32 [48], P(('head', 'tensor')), may hold values from 0 to 2.7
- d_skip: float32 [48], P(('head', 'tensor')), may hold values from 0.5 to 1.5
- norm_gain: float32 [3072], P(('head', 'tensor')), may hold values from 0.5 to 1.5
- w_out: bfloat16 [1536, 3072], P('dp', ('head', 'tensor')), may hold values from -0.109375 to 0.109375
- cotangent: bfloat16 [16384, 1536], P(('dp', 'head', 'tensor')), may hold values from -6 to 6
Outputs:
- block_out: bfloat16 [16384, 1536], P(('dp', 'head', 'tensor'))
- residual_grad: float32 [16384, 1536], P(('dp', 'head', 'tensor'))
- norm_in_gain_grad: float32 [1536], replicated
- w_zx_grad: float32 [1536, 2, 3072], P('dp', None, ('head', 'tensor'))
- w_bc_grad: float32 [1536, 256], P('dp')
- w_dt_grad: float32 [1536, 48], P('dp', ('head', 'tensor'))
- conv_x_weight_grad: float32 [4, 3072], P(None, ('head', 'tensor'))
- conv_x_bias_grad: float32 [3072], P(('head', 'tensor'))
- conv_bc_weight_grad: float32 [4, 256], replicated
- conv_bc_bias_grad: float32 [256], replicated
- dt_bias_grad: float32 [48], P(('head', 'tensor'))
- a_log_grad: float32 [48], P(('head', 'tensor'))
- d_skip_grad: float32 [48], P(('head', 'tensor'))
- norm_gain_grad: float32 [3072], P(('head', 'tensor'))
- w_out_grad: float32 [1536, 3072], P('dp', ('head', 'tensor'))
Inputs may be any that keep to these rules, and one draw needn't show every extreme that they name: `segment_ids`: along each sequence the numbers never fall; a document holds at most 2000 tokens.
All inputs are finite; a program needn't handle non-finite values.
Results may differ from a plain program's by a relative error of at most 0.0078.
Values may be sent and summed in bfloat16 or wider, within the bound.
A program may use at most 256 MiB of HBM per device.

v0:
```python
import jax
import jax.numpy as jnp
from jax import lax
from jax.sharding import PartitionSpec as P

HEADS = 48
BLOCK = 256
INNER = 3072


EPSILON = 1e-05
HIGHEST = lax.Precision.HIGHEST


def causal_conv(values, taps, offset_bias, segments):
    tap_count = taps.shape[0]
    summed = offset_bias + taps[tap_count - 1] * values
    for offset in range(1, tap_count):
        earlier = jnp.pad(values, ((0, 0), (offset, 0), (0, 0)))[:, :-offset]
        earlier_seg = jnp.pad(segments, ((0, 0), (offset, 0)), constant_values=-1)[:, :-offset]
        same_doc = (earlier_seg == segments).astype(jnp.float32)[..., None]
        summed = summed + taps[tap_count - 1 - offset] * earlier * same_doc
    return jax.nn.silu(summed)


def scan_blocks(x_heads, steps_dt, decay_rate, b_proj, c_proj, segments):
    seq_count, length, head_count, head_width = x_heads.shape
    state_size = b_proj.shape[-1]
    block_count = length // BLOCK

    def to_blocks(values):
        return jnp.moveaxis(
            values.reshape((seq_count, block_count, BLOCK) + values.shape[2:]), 1, 0
        )

    seg_blocks = to_blocks(segments)
    prev_end = jnp.concatenate([jnp.full((1, seq_count), -1, jnp.int32), seg_blocks[:-1, :, -1]], 0)
    lower_part = jnp.tril(jnp.ones((BLOCK, BLOCK), jnp.bool_))

    @jax.checkpoint
    def block_step(carried, inputs):
        x_block, dt_block, b_block, c_block, seg_block, end_before = inputs
        cumulative = jnp.cumsum(dt_block * decay_rate, axis=1)
        same_doc = ((seg_block[:, :, None] == seg_block[:, None, :]) & lower_part)[..., None]
        coupling = jnp.einsum("nls,nms->nlm", c_block, b_block, precision=HIGHEST)
        spread = cumulative[:, :, None, :] - cumulative[:, None, :, :]
        kernel = (
            jnp.where(same_doc, jnp.exp(jnp.where(same_doc, spread, 0.0)), 0.0)
            * coupling[..., None]
            * dt_block[:, None, :, :]
        )
        within = jnp.einsum("nlmh,nmhp->nlhp", kernel, x_block, precision=HIGHEST)
        carry_in = (seg_block == end_before[:, None]).astype(jnp.float32)[..., None] * jnp.exp(
            cumulative
        )
        from_state = (
            jnp.einsum("nls,nhps->nlhp", c_block, carried, precision=HIGHEST) * carry_in[..., None]
        )
        end_seg = seg_block[:, -1]
        tail_weight = (
            jnp.exp(cumulative[:, -1:, :] - cumulative)
            * dt_block
            * (seg_block == end_seg[:, None]).astype(jnp.float32)[..., None]
        )
        added_state = jnp.einsum(
            "nmh,nmhp,nms->nhps", tail_weight, x_block, b_block, precision=HIGHEST
        )
        keep_all = (end_before == end_seg).astype(jnp.float32)[:, None] * jnp.exp(
            cumulative[:, -1, :]
        )
        carried = carried * keep_all[:, :, None, None] + added_state
        return (carried, within + from_state)

    initial = jnp.zeros((seq_count, head_count, head_width, state_size), jnp.float32)
    _, outputs = lax.scan(
        block_step,
        initial,
        (
            to_blocks(x_heads),
            to_blocks(steps_dt),
            to_blocks(b_proj),
            to_blocks(c_proj),
            seg_blocks,
            prev_end,
        ),
    )
    return jnp.moveaxis(outputs, 0, 1).reshape(seq_count, length, head_count, head_width)


def mixer(
    z_and_x,
    b_and_c,
    dt_raw,
    segments,
    conv_weight,
    conv_bias,
    bc_weight,
    bc_bias,
    dt_shift,
    log_decay,
    skip_gain,
):
    seq_count, length = segments.shape
    head_count = dt_shift.shape[0]
    inner_width = z_and_x.shape[-1]
    head_width = inner_width // head_count
    state_size = b_and_c.shape[-1] // 2
    x_conv = causal_conv(z_and_x[:, :, 1], conv_weight, conv_bias, segments)
    bc_conv = causal_conv(b_and_c, bc_weight, bc_bias, segments)
    steps_dt = jax.nn.softplus(dt_raw + dt_shift)
    decay_rate = -jnp.exp(log_decay)
    x_heads = x_conv.reshape(seq_count, length, head_count, head_width)
    scanned = scan_blocks(
        x_heads,
        steps_dt,
        decay_rate,
        bc_conv[..., :state_size],
        bc_conv[..., state_size:],
        segments,
    )
    scanned = scanned + skip_gain[:, None] * x_heads
    return scanned.reshape(seq_count, length, inner_width) * jax.nn.silu(z_and_x[:, :, 0])


def body(
    residual,
    segment_ids,
    norm_in_gain,
    w_zx,
    w_bc,
    w_dt,
    conv_x_weight,
    conv_x_bias,
    conv_bc_weight,
    conv_bc_bias,
    dt_bias,
    a_log,
    d_skip,
    norm_gain,
    w_out,
    cotangent,
):
    own_rows, model_width = residual.shape
    seq_count, length = segment_ids.shape
    group_rows = seq_count * length
    inner_local = w_zx.shape[2]
    heads_local = w_dt.shape[1]
    state_cols = w_bc.shape[1]
    dp_rows = w_bc.shape[0]
    rows_in = residual.astype(jnp.float32)
    inv_rms = lax.rsqrt(jnp.mean(rows_in * rows_in, axis=1, keepdims=True) + EPSILON)
    normed = (rows_in * inv_rms * norm_in_gain).astype(jnp.bfloat16)
    zx_full, bc_full, dt_full, out_full = (
        lax.all_gather(w_zx, "dp", axis=0, tiled=True),
        lax.all_gather(w_bc, "dp", axis=0, tiled=True),
        lax.all_gather(w_dt, "dp", axis=0, tiled=True),
        lax.all_gather(w_out, "dp", axis=0, tiled=True),
    )
    zx_cols = zx_full.reshape(model_width, 2 * inner_local)
    proj_cols = jnp.concatenate([zx_cols, bc_full, dt_full], 1)
    projected = jnp.dot(
        lax.all_gather(normed, ("head", "tensor"), axis=0, tiled=True),
        proj_cols,
        preferred_element_type=jnp.float32,
    )
    z_and_x = projected[:, : 2 * inner_local].reshape(group_rows, 2, inner_local)
    b_and_c = projected[:, 2 * inner_local : 2 * inner_local + state_cols]
    dt_raw = projected[:, 2 * inner_local + state_cols :]

    def local_mix(
        zx_in,
        bc_in,
        dt_in,
        conv_weight,
        conv_bias,
        bc_weight,
        bc_bias,
        dt_shift,
        log_decay,
        skip_gain,
    ):
        mixed_seq = mixer(
            zx_in.reshape(seq_count, length, 2, inner_local),
            bc_in.reshape(seq_count, length, state_cols),
            dt_in.reshape(seq_count, length, heads_local),
            segment_ids,
            conv_weight,
            conv_bias,
            bc_weight,
            bc_bias,
            dt_shift,
            log_decay,
            skip_gain,
        )
        return mixed_seq.reshape(group_rows, inner_local)

    gated, mix_back = jax.vjp(
        local_mix,
        z_and_x,
        b_and_c,
        dt_raw,
        conv_x_weight,
        conv_x_bias,
        conv_bc_weight,
        conv_bc_bias,
        dt_bias,
        a_log,
        d_skip,
    )
    square_sum = lax.psum(jnp.sum(gated * gated, axis=1), ("head", "tensor"))
    inv_gate = lax.rsqrt(square_sum / INNER + EPSILON)[:, None]
    gated_out = (gated * inv_gate * norm_gain).astype(jnp.bfloat16)
    row_block = gated_out
    mixed_rows = lax.psum_scatter(
        jnp.einsum("ti,di->td", row_block, out_full, preferred_element_type=jnp.float32),
        ("head", "tensor"),
        scatter_dimension=0,
        tiled=True,
    )
    block_out = (rows_in + mixed_rows).astype(jnp.bfloat16)
    row_piece = lax.all_gather(cotangent, ("head", "tensor"), axis=0, tiled=True)
    row_block = gated_out
    grad_part = jnp.dot(row_piece, out_full, preferred_element_type=jnp.float32)
    grad_weight = jnp.einsum("td,ti->di", row_piece, row_block, preferred_element_type=jnp.float32)
    scaled_gate = grad_part * norm_gain
    cross_sum = lax.psum(jnp.sum(scaled_gate * gated, axis=1), ("head", "tensor"))
    grad_gated = (
        inv_gate * scaled_gate
        - gated * (inv_gate * inv_gate * inv_gate) * (cross_sum / INNER)[:, None]
    )
    grad_norm_gain = jnp.sum(grad_part * gated * inv_gate, axis=0)
    grads_mix = mix_back(grad_gated)
    low_zx = grads_mix[0].reshape(group_rows, 2 * inner_local).astype(jnp.bfloat16)
    grad_bc = grads_mix[1]
    low_dt = grads_mix[2].astype(jnp.bfloat16)
    low_both = jnp.concatenate([low_zx, low_dt], 1)
    back_cols = jnp.concatenate([zx_cols, dt_full], 1)
    row_block = low_both
    through = jnp.einsum("tk,dk->td", row_block, back_cols, preferred_element_type=jnp.float32)
    summed_rows = lax.psum_scatter(
        jnp.concatenate([through, grad_bc], 1), ("head", "tensor"), scatter_dimension=0, tiled=True
    )
    bc_own = summed_rows[:, model_width:].astype(jnp.bfloat16)
    through_rows = summed_rows[:, :model_width]
    grad_normed = through_rows + jnp.einsum(
        "tk,dk->td", bc_own, bc_full, preferred_element_type=jnp.float32
    )
    scaled_in = grad_normed * norm_in_gain
    input_grad = (
        cotangent.astype(jnp.float32)
        + inv_rms * scaled_in
        - rows_in
        * (inv_rms * inv_rms * inv_rms)
        * jnp.mean(scaled_in * rows_in, axis=1, keepdims=True)
    )
    grad_in_gain = jnp.sum(grad_normed * rows_in * inv_rms, axis=0)
    row_block = low_both
    grad_cols = jnp.einsum(
        "td,tk->dk",
        lax.all_gather(normed, ("head", "tensor"), axis=0, tiled=True),
        row_block,
        preferred_element_type=jnp.float32,
    )
    grad_wzx = grad_cols[:, : 2 * inner_local].reshape(model_width, 2, inner_local)
    grad_wdt = grad_cols[:, 2 * inner_local :]
    grad_wbc = jnp.einsum("td,tk->dk", normed, bc_own, preferred_element_type=jnp.float32)
    grad_wzx, grad_wdt, grad_wout = (
        lax.psum_scatter(grad_wzx, "dp", scatter_dimension=0, tiled=True),
        lax.psum_scatter(grad_wdt, "dp", scatter_dimension=0, tiled=True),
        lax.psum_scatter(grad_weight, "dp", scatter_dimension=0, tiled=True),
    )
    ht_index = lax.axis_index(("head", "tensor"))
    channel_pack = jnp.concatenate([grads_mix[3], grads_mix[4][None], grad_norm_gain[None]], 0)
    head_pack = jnp.stack([grads_mix[7], grads_mix[8], grads_mix[9]], 0)
    channel_full = lax.dynamic_update_slice(
        jnp.zeros((channel_pack.shape[0], INNER), jnp.float32),
        channel_pack,
        (0, ht_index * inner_local),
    )
    head_full = lax.dynamic_update_slice(
        jnp.zeros((3, HEADS), jnp.float32), head_pack, (0, ht_index * heads_local)
    )
    gain_sum, wbc_sum, taps_sum, bias_sum, channel_sum, head_sum = lax.psum(
        (grad_in_gain, grad_wbc, grads_mix[5], grads_mix[6], channel_full, head_full),
        ("dp", "head", "tensor"),
    )
    wbc_own = lax.dynamic_slice_in_dim(wbc_sum, lax.axis_index("dp") * dp_rows, dp_rows, 0)
    channel_own = lax.dynamic_slice_in_dim(channel_sum, ht_index * inner_local, inner_local, 1)
    head_own = lax.dynamic_slice_in_dim(head_sum, ht_index * heads_local, heads_local, 1)
    conv_rows = conv_x_weight.shape[0]
    return (
        block_out,
        input_grad,
        gain_sum,
        grad_wzx,
        wbc_own,
        grad_wdt,
        channel_own[:conv_rows],
        channel_own[conv_rows],
        taps_sum,
        bias_sum,
        head_own[0],
        head_own[1],
        head_own[2],
        channel_own[conv_rows + 1],
        grad_wout,
    )


def solution(mesh):
    return jax.shard_map(
        body,
        mesh=mesh,
        in_specs=(
            P(("dp", "head", "tensor"), None),
            P("dp", None),
            P(),
            P("dp", None, ("head", "tensor")),
            P("dp", None),
            P("dp", ("head", "tensor")),
            P(None, ("head", "tensor")),
            P(("head", "tensor")),
            P(),
            P(),
            P(("head", "tensor")),
            P(("head", "tensor")),
            P(("head", "tensor")),
            P(("head", "tensor")),
            P("dp", ("head", "tensor")),
            P(("dp", "head", "tensor"), None),
        ),
        out_specs=(
            P(("dp", "head", "tensor"), None),
            P(("dp", "head", "tensor"), None),
            P(),
            P("dp", None, ("head", "tensor")),
            P("dp", None),
            P("dp", ("head", "tensor")),
            P(None, ("head", "tensor")),
            P(("head", "tensor")),
            P(),
            P(),
            P(("head", "tensor")),
            P(("head", "tensor")),
            P(("head", "tensor")),
            P(("head", "tensor")),
            P("dp", ("head", "tensor")),
        ),
        check_vma=False,
    )
```

profile of v0, /device:TPU:0, one launch (start us, length us, event | category | flops | bytes accessed | tf_op | source)
XLA Modules:
  0.0 2911.1 jit_solution(757828949911331417)
XLA Ops:
  23.4 13.5 all_gather.21
  42.8 177.2 %all-gather.5.cloned.1.call-done = bf16[4096,1536]{1,0:T(8,128)(2,1)} async-done(((bf16[512,1536]{1,0:T(8,128)(2,1)}), bf16[4096,1536]{1,0:T(8,128)(2,1)}) %all-gather.5.cloned.1.call-update) | async-done | bytes 12582928 | tf_op jit(solution)/shard_map/all_gather | solution.py:162
  220.0 19.9 fusion.158
  292.3 18.4 fusion.146
  332.9 397.8 %while.42 = (s32[]{:T(128)}, f32[1,6,64,128]{3,2,1,0:T(8,128)S(1)}, f32[16,1,256,6,64]{2,0,4,3,1:T(8,128)}, f32[16,1,6,64,128]{4,3,2,1,0:T(8,128)}, s32[16,1]{0,...) while((s32[]{:T(128)}, f32[1,6,64,128]{3,2,1,0:T(8,128)S(1)}, ...), condition=%wide.region_4.5_spmd.clone, body=%wide.region_1.4_spmd.clone.sunk | while | flops 707551744 | bytes 5887422 | solution.py:75
  778.9 33.2 %psum.56 = f32[4096]{0:T(1024)S(1)} all-reduce(f32[4096]{0:T(1024)S(1)} %get-tuple-element.952), channel_id=1, replica_groups=mesh['dp'=4,'head'=4,'tensor'=2] {'head','tensor'}, use_global_device_ids=true, to_apply=%region_6.7 | all-reduce | flops 4096 | bytes 32768 | tf_op jit(solution)/shard_map/psum | solution.py:210
  812.2 13.7 fusion.141
  825.9 33.0 %psum.57 = f32[4096]{0:T(1024)S(1)} all-reduce(f32[4096]{0:T(1024)S(1)} %get-tuple-element.866), channel_id=1, replica_groups=mesh['dp'=4,'head'=4,'tensor'=2] {'head','tensor'}, use_global_device_ids=true, to_apply=%region_9.10 | all-reduce | flops 4096 | bytes 32768 | tf_op jit(solution)/shard_map/psum | solution.py:226
  858.9 14.7 fusion.127
  873.6 12.4 fusion.124
  907.4 698.8 %while.43 = (s32[]{:T(128)}, f32[6]{0:T(128)S(1)}, f32[1,6,64,128]{3,2,1,0:T(8,128)S(1)}, f32[16,1,256,6,64]{2,0,4,3,1:T(8,128)}, f32[16,1,256,6]{2,3,1,0:T(8,12...) while((s32[]{:T(128)}, f32[6]{0:T(128)S(1)}, ...), condition=%wide.region_23.24_spmd.clone, body=%wide.region_10.23_spmd.clone.sunk | while | flops 1670571520 | bytes 15650670 | solution.py:75
  1630.8 22.5 multiply_reduce_fusion.5
  1701.9 20.4 fusion.157
  1722.4 19.3 pad_maximum_fusion
  1741.7 14.7 fusion.156
  1769.4 13.2 convolution_bitcast_fusion.7
  1782.7 15.3 fusion.185
  1798.9 404.2 %reduce-scatter.7.cloned.1.call-done = f32[512,1792]{1,0:T(8,128)} async-done(((f32[4096,1792]{1,0:T(8,128)}), f32[512,1792]{1,0:T(8,128)}) %reduce-scatter.7.cloned.1.call-update) | async-done | bytes 3670032 | tf_op jit(solution)/shard_map/reduce_scatter | solution.py:240
  2209.1 89.4 %all-reduce.35.cloned.1.call-done = f32[1536,2,384]{2,1,0:T(2,128)} async-done(((f32[1536,2,384]{2,1,0:T(2,128)}), f32[1536,2,384]{2,1,0:T(2,128)}) %all-reduce.35.cloned.1.call-update) | async-done | bytes 4718608
  2301.2 33.7 %reduce-scatter.11.cloned.1.call-done = f32[384,384]{0,1:T(8,128)} async-done(((f32[1536,384]{0,1:T(8,128)}), f32[384,384]{0,1:T(8,128)}) %reduce-scatter.11.cloned.1.call-update) | async-done | bytes 589840 | tf_op jit(solution)/shard_map/reduce_scatter | solution.py:270
  2342.0 44.2 %all-reduce.30 = (f32[1536]{0:T(1024)}, f32[4,256]{1,0:T(4,128)}, f32[256]{0:T(256)}, f32[3,48]{1,0:T(4,128)S(1)}) all-reduce(f32[1536]{0:T(1024)S(1)} %get-tuple-element.872, f32[4,256]{1,0:T(4,128)S(1)} %pad_add_fusion.1, f32[256]{0:T(256)S(1)} %get-tuple-element.874, ...), channel_id=1, replica_groups=mesh['dp'=4,'head'=4,'tensor'=2] {'dp','head','tensor'}, use_global_device_ids=true, to_apply=%region_27.28 | all-reduce | flops 2960 | bytes 23680 | tf_op jit(solution)/shard_map/psum | solution.py:283
  2386.8 357.3 %reduce-scatter.5.cloned.1.call-done = f32[512,1536]{1,0:T(8,128)} async-done(((f32[4096,1536]{1,0:T(8,128)}), f32[512,1536]{1,0:T(8,128)}) %reduce-scatter.5.cloned.1.call-update) | async-done | bytes 3145744 | tf_op jit(solution)/shard_map/reduce_scatter | solution.py:214
  2750.2 132.5 %all-reduce.37.cloned.1.call-done = (f32[1536,256]{1,0:T(8,128)}, f32[6,3072]{1,0:T(8,128)}) async-done(((f32[1536,256]{1,0:T(8,128)}, f32[6,3072]{1,0:T(8,128)}), (f32[1536,256]{1,0:T(8,128)}, f32[6,3072]{1,0:T(8,128)})) %all-reduce.37.cloned.1.call-update) | async-done | bytes 1646608 | tf_op jit(solution)/shard_map/psum | solution.py:283
  2887.2 16.8 reduce-scatter.9.cloned.1.call-done
  (1623 shorter events, 1329.4 us)
Async XLA Ops:
  7.3 33.4 %all-gather.7.cloned.1.call-start = ((), (), s32[]{:S(2)}) async-start(), calls=%async_computation.5 | async-start | bytes 2949120 | tf_op jit(solution)/shard_map/all_gather | solution.py:154
  8.0 212.0 %all-gather.5.cloned.1.call-start = ((), (), s32[]{:S(2)}) async-start(), calls=%async_computation.4 | async-start | bytes 14155776 | tf_op jit(solution)/shard_map/all_gather | solution.py:162
  13.4 798.7 %all-gather.9.cloned.1.call-start = ((), (), s32[]{:S(2)}) async-start(), calls=%async_computation.6 | async-start | bytes 1474560 | tf_op jit(solution)/shard_map/all_gather | solution.py:157
  14.2 798.0 %all-gather.11.cloned.1.call-start = ((), (), s32[]{:S(2)}) async-start(), calls=%async_computation.8 | async-start | bytes 14155776 | tf_op jit(solution)/shard_map/all_gather | solution.py:221
  14.7 2188.4 %reduce-scatter.7.cloned.1.call-start = ((), (), s32[]{:S(2)}) async-start(), calls=%async_computation.9 | async-start | bytes 33030144 | tf_op jit(solution)/shard_map/reduce_scatter | solution.py:240
  16.2 276.1 %copy-start.24 = (f32[384]{0:T(512)}, f32[384]{0:T(512)S(1)}, u32[]{:S(2)}) copy-start(f32[384]{0:T(512)S(1)} %get-tuple-element.878) | copy-start | bytes 4612
  907.4 700.6 %copy-start.56 = (f32[6]{0:T(128)S(1)}, f32[6]{0:T(128)}, u32[]{:S(2)}) copy-start(f32[6]{0:T(128)} %param.30) | copy-start | bytes 76
  1741.6 556.9 %all-reduce.35.cloned.1.call-start = ((), (), s32[]{:S(2)}) async-start(), calls=%async_computation.12 | async-start | bytes 9437184
  1769.3 565.5 %reduce-scatter.11.cloned.1.call-start = ((), (), s32[]{:S(2)}) async-start(), calls=%async_computation.11 | async-start | bytes 2949120 | tf_op jit(solution)/shard_map/reduce_scatter | solution.py:270
  1782.6 961.5 %reduce-scatter.5.cloned.1.call-start = ((), (), s32[]{:S(2)}) async-start(), calls=%async_computation.7 | async-start | bytes 28311552 | tf_op jit(solution)/shard_map/reduce_scatter | solution.py:214
  1798.1 405.0 %copy-start.5 = (bf16[512,1536]{1,0:T(8,128)(2,1)S(1)}, bf16[512,1536]{1,0:T(8,128)(2,1)}, u32[]{:S(2)}) copy-start(bf16[512,1536]{1,0:T(8,128)(2,1)} %fusion.166) | copy-start | bytes 4718596
  1798.1 407.9 %copy-start.64 = (u32[32]{0:T(128)S(1)}, u32[32]{0:T(128)}, u32[]{:S(2)}) copy-start(u32[32]{0:T(128)} %constant.242) | copy-start | bytes 388
  1798.1 410.6 %copy-start.45 = (f32[384]{0:T(512)S(1)}, f32[384]{0:T(512)}, u32[]{:S(2)}) copy-start(f32[384]{0:T(512)} %get-tuple-element.949) | copy-start | bytes 4612
  1798.1 410.8 %copy-start.36 = (f32[6]{0:T(128)S(1)}, f32[6]{0:T(128)}, u32[]{:S(2)}) copy-start(f32[6]{0:T(128)} %copy-done.35) | copy-start | bytes 76
  1798.1 410.8 %copy-start.63 = (f32[6]{0:T(128)S(1)}, f32[6]{0:T(128)}, u32[]{:S(2)}) copy-start(f32[6]{0:T(128)} %param.31) | copy-start | bytes 76
  1798.1 410.8 %copy-start.57 = (f32[6]{0:T(128)S(1)}, f32[6]{0:T(128)}, u32[]{:S(2)}) copy-start(f32[6]{0:T(128)} %get-tuple-element.947) | copy-start | bytes 76
  1798.2 538.8 %copy-start.6 = (bf16[512,1536]{1,0:T(8,128)(2,1)S(1)}, bf16[512,1536]{1,0:T(8,128)(2,1)}, u32[]{:S(2)}) copy-start(bf16[512,1536]{1,0:T(8,128)(2,1)} %param.20) | copy-start | bytes 4718596
  1798.2 538.8 %copy-start.23 = (f32[1536]{0:T(1024)S(1)}, f32[1536]{0:T(1024)}, u32[]{:S(2)}) copy-start(f32[1536]{0:T(1024)} %param.22) | copy-start | bytes 18436
  1798.2 538.8 %copy-start.33 = (f32[512]{0:T(512)S(1)}, f32[512]{0:T(512)}, u32[]{:S(2)}) copy-start(f32[512]{0:T(512)} %copy-done.32) | copy-start | bytes 6148
  1798.2 1084.5 %all-reduce.37.cloned.1.call-start = ((), (), s32[]{:S(2)}) async-start(), calls=%async_computation.13 | async-start | bytes 3342336 | tf_op jit(solution)/shard_map/psum | solution.py:283
  1798.8 407.1 %copy-start.17 = (f32[6,3072]{1,0:T(8,128)}, f32[6,3072]{1,0:T(8,128)S(1)}, u32[]{:S(2)}) copy-start(f32[6,3072]{1,0:T(8,128)S(1)} %maximum_dynamic-update-slice_fusion) | copy-start | bytes 221188
  2205.9 538.2 %copy-start.8 = (bf16[512,1536]{1,0:T(8,128)(2,1)S(1)}, bf16[512,1536]{1,0:T(8,128)(2,1)}, u32[]{:S(2)}) copy-start(bf16[512,1536]{1,0:T(8,128)(2,1)} %param.35) | copy-start | bytes 4718596
  2205.9 538.2 %copy-start.51 = (f32[512]{0:T(512)S(1)}, f32[512]{0:T(512)}, u32[]{:S(2)}) copy-start(f32[512]{0:T(512)} %get-tuple-element.998) | copy-start | bytes 6148
  2205.9 698.1 %reduce-scatter.9.cloned.1.call-start = ((), (), s32[]{:S(2)}) async-start(), calls=%async_computation.10 | async-start | bytes 61440 | tf_op jit(solution)/shard_map/reduce_scatter | solution.py:269
  (53 other events, 2668.8 us)
Sparse Core Ops, SparseCore 0:
  9.6 30.9 all-gather.6
  43.4 176.4 all-gather.4
  221.5 15.6 all-gather.8
  239.2 176.5 all-gather.10
  1741.8 461.2 reduce-scatter.6
  2205.3 93.1 all-reduce.34
  2301.6 33.2 reduce-scatter.10
  2339.2 404.8 reduce-scatter.4
  2751.0 131.6 all-reduce.36
  2885.5 18.4 reduce-scatter.8
where the time goes:
time: 2930 us; the launch traced here: 2910 us
  waiting for transfers between devices  1220 us (42%)
  local copies, waits for them, and re-layouts  730 us (25%)
  other arithmetic  412 us (14%)
  matrix products  361 us (12%)
  blocking collectives  130 us (4%)
  loops' own time  46.4 us (2%)
    reduce_scatter x1, waiting for transfers between devices, body(): lax.psum_scatter(jnp.concatenate([through, grad_bc], 1), ('head', 'tensor...  404 us
    dynamic_update_slice x96, local copies, waits for them, and re-layouts, scan_blocks(): lax.scan(block_step, initial, (to_blocks(x_heads), to_blocks(steps_dt), t...  397 us
    reduce_scatter x1, waiting for transfers between devices, body(): lax.psum_scatter(jnp.einsum('ti,di->td', row_block, out_full, preferred_e...  357 us
    another operation x144, other arithmetic  186 us
    all_gather x1, waiting for transfers between devices, body(): lax.all_gather(normed, ('head', 'tensor'), axis=0, tiled=True)  177 us
    psum x1, waiting for transfers between devices, body(): lax.psum((grad_in_gain, grad_wbc, grads_mix[5], grads_mix[6], channel_ful...  132 us
    dot_general x48, matrix products, block_step(): within = jnp.einsum('nlmh,nmhp->nlhp', kernel, x_block, precision=HIGHEST)  113 us
    unnamed x11, waiting for transfers between devices  91.4 us
  transfers between devices with their start and end apart: 10, of which 8 were waited for; matrix products, arithmetic and copies ran while one was open for 22% of the time, Pallas kernels for 0%

commit v1 on v0

v1 whole, which is shorter than its diff:
```python
import jax
import jax.numpy as jnp
from jax import lax
from jax.sharding import PartitionSpec as P

EPSILON = 1e-05
DOC_MOST = 2000
CHUNK = 128
HALO = 16
MASKED = -1e30
HIGHEST = lax.Precision.HIGHEST
SEQ = ("head", "tensor")
ALL = ("dp", "head", "tensor")
BF16 = jnp.bfloat16
F32 = jnp.float32


def dot16(pattern, left, right):
    return jnp.einsum(pattern, left.astype(BF16), right.astype(BF16), preferred_element_type=F32)


def rounded(v):
    return lax.optimization_barrier(v.astype(BF16))


def silu_grad(v):
    gate = jax.nn.sigmoid(v)
    return gate * (1.0 + v * (1.0 - gate))


def conv_before(ext, taps, bias, same):
    own = ext.shape[0] - HALO
    total = bias + taps[-1] * ext[HALO:]
    for back in range(1, taps.shape[0]):
        total = total + taps[-1 - back] * ext[HALO - back : HALO - back + own] * same[back - 1]
    return total


def conv_back(grad, ext, taps, same):
    own = grad.shape[0]
    width = taps.shape[0]
    below = jnp.zeros((HALO, grad.shape[1]), F32)
    total = jnp.concatenate([below, taps[-1] * grad], 0)
    rows = [jnp.sum(grad * ext[HALO:], axis=0)]
    for back in range(1, width):
        masked = grad * same[back - 1]
        rows.append(jnp.sum(masked * ext[HALO - back : HALO - back + own], axis=0))
        total = total + jnp.pad(
            taps[-1 - back] * masked, ((HALO - back, back), (0, 0))
        )
    return total, jnp.stack(rows[::-1], 0), jnp.sum(grad, axis=0)


def from_earlier(values, distance, size):
    return lax.ppermute(values, SEQ, [(i, i + distance) for i in range(size - distance)])


def from_later(values, distance, size):
    return lax.ppermute(values, SEQ, [(i + distance, i) for i in range(size - distance)])


def reach_over(shift, local, keep, size, need):
    total = shift(local.astype(BF16), 1, size).astype(F32)
    factor = shift(keep, 1, size)
    covered = 1
    while covered < min(need, size - 1):
        got = shift(total.astype(BF16), covered, size).astype(F32)
        total = total + factor[:, None, None] * got
        if covered * 2 < min(need, size - 1):
            factor = factor * shift(factor, covered, size)
        covered *= 2
    return total


def body(
    residual,
    segment_ids,
    norm_in_gain,
    w_zx,
    w_bc,
    w_dt,
    conv_x_weight,
    conv_x_bias,
    conv_bc_weight,
    conv_bc_bias,
    dt_bias,
    a_log,
    d_skip,
    norm_gain,
    w_out,
    cotangent,
):
    own, width = residual.shape
    dp_size = lax.axis_size("dp")
    size = lax.axis_size(SEQ)
    place = lax.axis_index(SEQ)
    dp_rows, _, cols = w_zx.shape
    heads_own = w_dt.shape[1]
    inner = cols * size
    heads = heads_own * size
    state2 = w_bc.shape[1]
    state = state2 // 2
    bc_cols = state2 // size
    chunks = own // CHUNK
    head_width = inner // heads

    bc_own = lax.dynamic_slice_in_dim(w_bc, place * bc_cols, bc_cols, 1)
    side = heads_own + bc_cols
    pack = jnp.concatenate([w_zx.reshape(dp_rows, 2 * cols), w_out, bc_own, w_dt], 1)
    full = lax.all_gather(pack, ALL, axis=0, tiled=False).reshape(dp_size, size, dp_rows, -1)
    full = jnp.moveaxis(full, 1, 2).reshape(width, size, -1)
    w_z = full[:, :, :cols].reshape(width, inner)
    w_x = full[:, :, cols : 2 * cols].reshape(width, inner)
    w_o = full[:, :, 2 * cols : 3 * cols].reshape(width, inner)
    w_b = full[:, :, 3 * cols : 3 * cols + bc_cols].reshape(width, state2)
    w_d = full[:, :, 3 * cols + bc_cols :].reshape(width, heads)
    per_head = jnp.concatenate(
        [dt_bias[None], a_log[None], d_skip[None]], 0
    )
    per_channel = jnp.concatenate([conv_x_weight, conv_x_bias[None], norm_gain[None]], 0)
    per_head = lax.all_gather(per_head, SEQ, axis=1, tiled=True)
    per_channel = lax.all_gather(per_channel, SEQ, axis=1, tiled=True)
    taps = conv_x_weight.shape[0]
    x_taps, x_bias, out_gain = per_channel[:taps], per_channel[taps], per_channel[taps + 1]
    dt_shift, log_rate, skip = per_head[0], per_head[1], per_head[2]
    rate = -jnp.exp(log_rate)
    skip_wide = jnp.repeat(skip, head_width)

    seg_all = jnp.pad(segment_ids[0], (HALO, 0), constant_values=-1)
    seg_ext = lax.dynamic_slice_in_dim(seg_all, place * own, own + HALO)
    seg = seg_ext[HALO:]
    same = [
        (seg_ext[HALO - back : HALO - back + own] == seg).astype(F32)[:, None]
        for back in range(1, taps)
    ]
    seg_chunk = seg.reshape(chunks, CHUNK)
    end_chunk = seg_chunk[:, -1]
    end_before = jnp.concatenate([seg_ext[HALO - 1 : HALO], end_chunk[:-1]])
    lower = jnp.tril(jnp.ones((CHUNK, CHUNK), F32))
    mask_bias = jnp.where(
        (seg_chunk[:, :, None] == seg_chunk[:, None, :]) & (lower > 0), 0.0, MASKED
    )

    rows_ext = jnp.concatenate([from_earlier(residual[-HALO:], 1, size), residual], 0).astype(F32)
    inv_ext = lax.rsqrt(jnp.mean(rows_ext * rows_ext, axis=1, keepdims=True) + EPSILON)
    normed = (rows_ext * inv_ext * norm_in_gain).astype(BF16)
    rows_in, inv_rms = rows_ext[HALO:], inv_ext[HALO:]
    x_ext = dot16("td,dk->tk", normed, w_x)
    z = dot16("td,dk->tk", normed[HALO:], w_z)
    bc_ext = dot16("td,dk->tk", normed, w_b)
    dt_raw = dot16("td,dk->tk", normed[HALO:], w_d)

    x_pre = conv_before(x_ext, x_taps, x_bias, same)
    bc_pre = conv_before(bc_ext, conv_bc_weight, conv_bc_bias, same)
    x = jax.nn.silu(x_pre)
    bc = jax.nn.silu(bc_pre).astype(BF16)
    dt = jax.nn.softplus(dt_raw + dt_shift)

    cum = jnp.einsum(
        "lm,cmh->clh", lower, (dt * rate).reshape(chunks, CHUNK, heads), precision=HIGHEST
    )
    b_chunk = bc[:, :state].reshape(chunks, CHUNK, state)
    c_chunk = bc[:, state:].reshape(chunks, CHUNK, state)

    def split(v):
        return v.reshape(chunks, CHUNK, heads, head_width)

    x4 = split(x)
    dt_chunk = dt.reshape(chunks, CHUNK, heads)
    xd = x4 * dt_chunk[..., None]
    xd16 = rounded(xd)
    coupling = dot16("cls,cms->clm", c_chunk, b_chunk)
    cum_t = jnp.moveaxis(cum, 2, 1)
    decay = jnp.exp(cum_t[:, :, :, None] - cum_t[:, :, None, :] + mask_bias[:, None])
    kernel = rounded(decay * coupling[:, None])
    y_within = dot16("chlm,cmhp->clhp", kernel, xd16)
    in_end = (seg_chunk == end_chunk[:, None]).astype(F32)[..., None]
    in_start = (seg_chunk == end_before[:, None]).astype(F32)[..., None]
    tail = jnp.exp(cum[:, -1:] - cum) * in_end
    entry = jnp.exp(cum) * in_start
    keep = jnp.exp(cum[:, -1]) * (end_before == end_chunk).astype(F32)[:, None]
    xt16 = rounded(xd * tail[..., None])
    added = dot16("cmhp,cms->chps", xt16, b_chunk)

    local, keep_local = added[0], keep[0]
    for c in range(1, chunks):
        local = added[c] + keep[c][:, None, None] * local
        keep_local = keep_local * keep[c]
    need = -(-(DOC_MOST - 1) // own)
    entering = [reach_over(from_earlier, local, keep_local, size, need)]
    for c in range(chunks - 1):
        entering.append(added[c] + keep[c][:, None, None] * entering[c])
    entering = jnp.stack(entering, 0)
    entering16 = entering.astype(BF16)
    y_entry = dot16("cls,chps->clhp", c_chunk, entering16)
    y = (y_within + y_entry * entry[..., None]).reshape(own, inner) + skip_wide * x

    z_gate = jax.nn.silu(z)
    gated = y * z_gate
    inv_gate = lax.rsqrt(jnp.mean(gated * gated, axis=1, keepdims=True) + EPSILON)
    gated_out = (gated * inv_gate * out_gain).astype(BF16)
    block_out = (rows_in + dot16("ti,di->td", gated_out, w_o)).astype(BF16)
    grad_gate = dot16("td,di->ti", cotangent, w_o)
    grad_wout = dot16("td,ti->di", cotangent, gated_out)
    grad_norm_gain = jnp.sum(grad_gate * gated * inv_gate, axis=0)
    scaled_gate = grad_gate * out_gain
    cross = jnp.sum(scaled_gate * gated, axis=1, keepdims=True)
    grad_gated = inv_gate * scaled_gate - gated * (inv_gate * inv_gate * inv_gate) * (cross / inner)

    dy = grad_gated * z_gate
    dz = grad_gated * y * silu_grad(z)
    grad_skip = jnp.sum((dy * x).reshape(own, heads, head_width), axis=(0, 2))

    dy4 = split(dy)
    dy16 = rounded(dy4)
    dye16 = rounded(dy4 * entry[..., None])
    back_added = dot16("clhp,cls->chps", dye16, c_chunk)
    back_local = back_added[-1]
    for c in range(chunks - 2, -1, -1):
        back_local = back_added[c] + keep[c][:, None, None] * back_local
    leaving = [reach_over(from_later, back_local, keep_local, size, need)]
    for c in range(chunks - 1, 0, -1):
        leaving.append(back_added[c] + keep[c][:, None, None] * leaving[-1])
    leaving = jnp.stack(leaving[::-1], 0)
    leaving16 = leaving.astype(BF16)
    dxd_within = dot16("chlm,clhp->cmhp", kernel, dy16)
    dxt = dot16("cms,chps->cmhp", b_chunk, leaving16)
    dxd = dxd_within + tail[..., None] * dxt
    dx = (dxd * dt_chunk[..., None]).reshape(own, inner) + skip_wide * dy
    dkernel = dot16("clhp,cmhp->chlm", dy16, xd16)
    dcoupling = jnp.sum(dkernel * decay, axis=1)
    dc = dot16("clm,cms->cls", dcoupling, b_chunk) + dot16("clhp,chps->cls", dye16, entering16)
    db = dot16("clm,cls->cms", dcoupling, c_chunk) + dot16("cmhp,chps->cms", xt16, leaving16)
    falls = jnp.sum(
        dy16.astype(F32) * y_within
        + dye16.astype(F32) * y_entry
        - xd16.astype(F32) * dxd_within,
        axis=3,
    )
    rises = jnp.sum(xt16.astype(F32) * dxt, axis=3)
    strict = lower - jnp.eye(CHUNK, dtype=F32)
    da = (
        jnp.einsum("lm,clh->cmh", lower, falls, precision=HIGHEST)
        + jnp.einsum("lm,cmh->clh", strict, rises, precision=HIGHEST)
        + (keep * jnp.sum(leaving * entering, axis=(2, 3)))[:, None]
    )
    ddt = jnp.sum(x4 * dxd, axis=3) + rate * da
    grad_log = rate * jnp.sum(dt_chunk * da, axis=(0, 1))
    ddt_raw = ddt.reshape(own, heads) * jax.nn.sigmoid(dt_raw + dt_shift)
    grad_shift = jnp.sum(ddt_raw, axis=0)

    gx, grad_taps, grad_bias = conv_back(dx * silu_grad(x_pre), x_ext, x_taps, same)
    dbc = jnp.concatenate([db, dc], 2).reshape(own, state2)
    gbc, grad_bc_taps, grad_bc_bias = conv_back(
        dbc * silu_grad(bc_pre), bc_ext, conv_bc_weight, same
    )
    low_x = gx.astype(BF16)
    low_bc = gbc.astype(BF16)
    above = jnp.zeros((HALO, 1), BF16)
    low_z = dz.astype(BF16)
    low_dt = ddt_raw.astype(BF16)
    normed_own = normed[HALO:]

    own_part = dot16("tk,dk->td", low_z, w_z) + dot16("tk,dk->td", low_dt, w_d)
    ext_part = dot16("tk,dk->td", low_x, w_x) + dot16("tk,dk->td", low_bc, w_b)
    last = from_later(ext_part[:HALO], 1, size)
    grad_normed = own_part + ext_part[HALO:]
    grad_normed = grad_normed.at[own - HALO :].add(last)
    scaled_in = grad_normed * norm_in_gain
    input_grad = (
        cotangent.astype(F32)
        + inv_rms * scaled_in
        - rows_in * (inv_rms * inv_rms * inv_rms) * jnp.mean(scaled_in * rows_in, axis=1, keepdims=True)
    )
    grad_in_gain = jnp.sum(grad_normed * rows_in * inv_rms, axis=0)

    grad_z = dot16("td,tk->dk", normed_own, low_z)
    grad_d = dot16("td,tk->dk", normed_own, low_dt)
    grad_x = dot16("td,tk->dk", normed, low_x)
    grad_b = dot16("td,tk->dk", normed, low_bc)

    def columns(v):
        return v.astype(BF16).reshape(width, size, -1)

    parts = jnp.concatenate([columns(v) for v in (grad_z, grad_x, grad_wout, grad_b, grad_d)], 2)
    parts = jnp.moveaxis(parts.reshape(dp_size, dp_rows, size, -1), 2, 1)
    mine = lax.psum_scatter(
        parts.reshape(dp_size * size * dp_rows, -1), ALL, scatter_dimension=0, tiled=True
    ).astype(F32)
    grad_wzx = mine[:, : 2 * cols].reshape(dp_rows, 2, cols)
    grad_wo = mine[:, 2 * cols : 3 * cols]
    grad_wbc = lax.all_gather(mine[:, 3 * cols : 3 * cols + bc_cols], SEQ, axis=1, tiled=True)
    grad_wdt = mine[:, 3 * cols + bc_cols :]

    channel_sum = jnp.concatenate([grad_taps, grad_bias[None], grad_norm_gain[None]], 0)
    head_sum = jnp.stack([grad_shift, grad_log, grad_skip], 0)
    gain_sum, taps_sum, bias_sum, channel_sum, head_sum = lax.psum(
        (grad_in_gain, grad_bc_taps, grad_bc_bias, channel_sum, head_sum), ALL
    )
    channel_own = lax.dynamic_slice_in_dim(channel_sum, place * cols, cols, 1)
    head_own = lax.dynamic_slice_in_dim(head_sum, place * heads_own, heads_own, 1)
    return (
        block_out,
        input_grad,
        gain_sum,
        grad_wzx,
        grad_wbc,
        grad_wdt,
        channel_own[:taps],
        channel_own[taps],
        taps_sum,
        bias_sum,
        head_own[0],
        head_own[1],
        head_own[2],
        channel_own[taps + 1],
        grad_wo,
    )


def solution(mesh):
    rows = P(ALL, None)
    in_specs = (
        rows,
        P("dp", None),
        P(),
        P("dp", None, SEQ),
        P("dp", None),
        P("dp", SEQ),
        P(None, SEQ),
        P(SEQ),
        P(),
        P(),
        P(SEQ),
        P(SEQ),
        P(SEQ),
        P(SEQ),
        P("dp", SEQ),
        rows,
    )
    out_specs = (
        rows,
        rows,
        P(),
        P("dp", None, SEQ),
        P("dp", None),
        P("dp", SEQ),
        P(None, SEQ),
        P(SEQ),
        P(),
        P(),
        P(SEQ),
        P(SEQ),
        P(SEQ),
        P(SEQ),
        P("dp", SEQ),
    )
    return jax.shard_map(
        body, mesh=mesh, in_specs=in_specs, out_specs=out_specs, check_vma=False
    )
```

time: 2930 us -> 1200 us (0.41)
  waiting for transfers between devices: 1220 us -> 419 us
  local copies, waits for them, and re-layouts: 730 us -> 332 us
  other arithmetic: 412 us -> 117 us
  matrix products: 361 us -> 139 us
  loops' own time: 46.4 us -> 0 us
  starting transfers between devices: 0.4 us -> 34.5 us
    reduce_scatter x4 -> x0, waiting for transfers between devices: 812 us -> none  [the longest x1 404 us: body(): lax.psum_scatter(jnp.concatenate([through, grad_bc], 1), ('head', 'tensor...]
    dynamic_update_slice x97 -> x0, local copies, waits for them, and re-layouts: 397 us -> none  [the longest x96 397 us: scan_blocks(): lax.scan(block_step, initial, (to_blocks(x_heads), to_blocks(steps_dt), t...]
    dot_general x232 -> x30, matrix products: 361 us -> 139 us  [the longest x27 138 us: dot16(): jnp.einsum(pattern, left.astype(BF16), right.astype(BF16), preferred_elem...]
    another operation x162 -> x6, other arithmetic: 186 us -> 9.91 us  [the longest x2 7.15 us: body(): entering = jnp.stack(entering, 0)]
    unnamed x11 -> x4, waiting for transfers between devices: 91.4 us -> 238 us
    psum x1, waiting for transfers between devices: 132 us -> 5.37 us  [body(): lax.psum((grad_in_gain, grad_bc_taps, grad_bc_bias, channel_sum, head_sum...]
    reshape x19 -> x11, local copies, waits for them, and re-layouts: 20 us -> 105 us  [the longest x4 41 us: split(): return v.reshape(chunks, CHUNK, heads, head_width)]
    concatenate x0 -> x8, local copies, waits for them, and re-layouts: none -> 79.3 us  [the longest x6 78.4 us: body(): jnp.concatenate([columns(v) for v in (grad_z, grad_x, grad_wout, grad_b,...]
  transfers between devices with their start and end apart: 10 -> 15, of which waited for: 8 -> 7; matrix products, arithmetic and copies ran while one was open for 22% -> 19% of each run, Pallas kernels for 0% -> 0%
where the time goes in v1:
time: 1200 us; the launch traced here: 1190 us
  waiting for transfers between devices  419 us (35%)
  local copies, waits for them, and re-layouts  332 us (28%)
  matrix products  139 us (12%)
  blocking collectives  130 us (11%)
  other arithmetic  117 us (10%)
  starting transfers between devices  34.5 us (3%)
  between operations  16.3 us (1%)
    unnamed x4, waiting for transfers between devices  238 us
    dot_general x27, matrix products, dot16(): jnp.einsum(pattern, left.astype(BF16), right.astype(BF16), preferred_elem...  138 us
    all_gather x1, waiting for transfers between devices, body(): lax.all_gather(pack, ALL, axis=0, tiled=False)  116 us
    unnamed x293, local copies, waits for them, and re-layouts  84 us
    concatenate x6, local copies, waits for them, and re-layouts, body(): jnp.concatenate([columns(v) for v in (grad_z, grad_x, grad_wout, grad_b,...  78.4 us
    psum x1, blocking collectives, body(): lax.psum((grad_in_gain, grad_bc_taps, grad_bc_bias, channel_sum, head_sum...  41.6 us
    reshape x4, local copies, waits for them, and re-layouts, split(): return v.reshape(chunks, CHUNK, heads, head_width)  41 us
    all_gather x1, blocking collectives, body(): per_channel = lax.all_gather(per_channel, SEQ, axis=1, tiled=True)  31.2 us
  transfers between devices with their start and end apart: 15, of which 7 were waited for; matrix products, arithmetic and copies ran while one was open for 19% of the time, Pallas kernels for 0%

profile of v1, /device:TPU:0, one launch (start us, length us, event | category | flops | bytes accessed | tf_op | source)
XLA Modules:
  0.0 1188.9 jit_solution(15713216331076574816)
XLA Ops:
  19.2 26.7 %all-gather.1 = f32[8,6,3]{1,2,0:T(4,128)S(1)} all-gather(f32[1,6,3]{1,2,0:T(4,128)S(1)} %maximum_bitcast_fusion), channel_id=1, replica_groups=mesh['dp'=4,'head'=4,'tensor'=2] {'head','tensor'}, dimensions={0}, use_global_device_ids=true | all-gather | bytes 648 | tf_op jit(solution)/shard_map/all_gather | solution.py:121
  46.0 31.2 %all_gather.15 = f32[6,3072]{1,0:T(8,128)S(1)} all-gather(f32[6,384]{1,0:T(8,128)S(1)} %pad_maximum_fusion.4), channel_id=1, replica_groups=mesh['dp'=4,'head'=4,'tensor'=2] {'head','tensor'}, dimensions={1}, use_global_device_ids=true | all-gather | bytes 82944 | tf_op jit(solution)/shard_map/all_gather | solution.py:122
  82.8 115.6 %all-gather.4.cloned.1.call-done = bf16[12288,1190]{0,1:T(8,128)(2,1)} async-done(((bf16[384,1190]{0,1:T(8,128)(2,1)}), bf16[12288,1190]{0,1:T(8,128)(2,1)}) %all-gather.4.cloned.1.call-update) | async-done | bytes 29245456 | tf_op jit(solution)/shard_map/all_gather | solution.py:110
  198.4 20.6 %copy.284 = bf16[149,8,32,384]{3,2,1,0:T(8,128)(2,1)} copy(bf16[149,8,32,384]{3,1,2,0:T(8,128)(2,1)} %bitcast.343) | data formatting | bytes 58589184
  219.0 20.1 %slice_bitcast_fusion = bf16[4,8,384,1190]{2,1,0,3:T(8,128)(2,1)} fusion(bf16[1192,32,384]{2,1,0:T(8,128)(2,1)} %bitcast.329), kind=kLoop, calls=%fused_computation | loop fusion | bytes 58490880 | tf_op jit(solution)/shard_map/reshape | solution.py:110
  239.2 20.0 %fusion.74 = (bf16[1536,8,384]{0,1,2:T(8,128)(2,1)}, bf16[1536,8,384]{0,1,2:T(8,128)(2,1)}, bf16[1536,8,384]{0,1,2:T(8,128)(2,1)}) fusion(bf16[1536,8,1190]{0,1,2:T(8,128)(2,1)} %bitcast.330), kind=kLoop, calls=%fused_computation.214 | loop fusion | bytes 56623104 | tf_op jit(solution)/shard_map/slice | solution.py:113
  328.3 17.2 %collective-permute-done.1 = bf16[48,64,128]{2,1,0:T(8,128)(2,1)S(1)} collective-permute-done((bf16[48,64,128]{2,1,0:T(8,128)(2,1)S(1)}, bf16[48,64,128]{2,1,0:T(8,128)(2,1)S(1)}, u32[]{:S(2)}, u32[]{:S(2)}) %collective-permute-start.1) | collective-permute-done | bytes 786464 | tf_op jit(solution)/shard_map/ppermute | solution.py:55
  353.0 13.3 %collective-permute-done.2 = f32[48]{0:T(128)S(1)} collective-permute-done((f32[48]{0:T(128)S(1)}, f32[48]{0:T(128)S(1)}, u32[]{:S(2)}, u32[]{:S(2)}) %collective-permute-start.2) | collective-permute-done | bytes 224 | tf_op jit(solution)/shard_map/ppermute | solution.py:55
  443.4 10.8 reshape.305
  454.1 14.0 %multiply_reduce_fusion.10 = (f32[512]{0:T(512)S(1)}, f32[512,3072]{1,0:T(8,128)S(1)}, f32[512,3072]{1,0:T(8,128)}) fusion(f32[512,3072]{1,0:T(8,128)} %reshape.305, f32[512,3072]{1,0:T(8,128)} %get-tuple-element.170, f32[3072]{0:T(1024)S(1)} %mul.824, bf16[1536,3072]{0,1:T(8,128)(2,1)} %bitcast.358, bf16[528,1536]{1,0:T(8,128)(2,1)S(1)} %copy-done.20), kind=kOutput, calls=%fused_computation.36 | convolution fusion | flops 4852284928 | bytes 36190208 | tf_op jit(solution)/shard_map/td,dk->tk/dot_general | solution.py:19
  478.5 12.5 %fusion.4 = (f32[3072]{0:T(1024)}, f32[512]{0:T(512)S(1)}, f32[3072,512]{0,1:T(8,128)}) fusion(f32[512,3072]{1,0:T(8,128)} %copy-done.37, f32[512]{0:T(512)S(1)} %get-tuple-element.217, f32[3072]{0:T(1024)S(1)} %bitcast.388, bf16[1536,3072]{0,1:T(8,128)(2,1)} %bitcast.356, bf16[512,1536]{1,0:T(8,128)(2,1)S(1)} %copy-done.45), kind=kOutput, calls=%fused_computation.18 | convolution fusion | flops 4841271808 | bytes 23621632 | tf_op jit(solution)/shard_map/td,di->ti/dot_general | solution.py:19
  491.1 13.2 %multiply_reduce_fusion.1 = (f32[3072]{0:T(1024)}, f32[512,3072]{1,0:T(8,128)}, bf16[512,3072]{1,0:T(8,128)(2,1)}) fusion(f32[512,3072]{1,0:T(8,128)S(1)} %bitcast.334, f32[512,3072]{1,0:T(8,128)} %get-tuple-element.229, f32[512]{0:T(512)S(1)} %broadcast_multiply_fusion.4, f32[512,3072]{1,0:T(8,128)} %copy-done.37, f32[512]{0:T(512)S(1)} %get-tuple-element.216, ...), kind=kLoop, calls=%fused_computation.22 | loop fusion | flops 39318528 | bytes 40937472 | tf_op jit(solution)/shard_map/reduce_sum | solution.py:212
  556.4 16.4 %concatenate.60 = bf16[4,384,8,384]{1,0,3,2:T(4,128)(2,1)} reshape(bf16[1536,3072]{0,1:T(8,128)(2,1)} %fusion) | data formatting | bytes 18874368 | tf_op jit(solution)/shard_map/concatenate | solution.py:285
  572.9 12.5 %copy.254 = bf16[4,384,8,384]{3,2,1,0:T(8,128)(2,1)} copy(bf16[4,384,8,384]{1,0,3,2:T(4,128)(2,1)} %concatenate.60) | data formatting | bytes 18874368 | tf_op jit(solution)/shard_map/concatenate | solution.py:285
  596.3 17.0 %collective-permute-done.8 = bf16[48,64,128]{2,1,0:T(8,128)(2,1)S(1)} collective-permute-done((bf16[48,64,128]{2,1,0:T(8,128)(2,1)}, bf16[48,64,128]{2,1,0:T(8,128)(2,1)S(1)}, u32[]{:S(2)}, u32[]{:S(2)}) %collective-permute-start.8) | collective-permute-done | bytes 786464 | tf_op jit(solution)/shard_map/ppermute | solution.py:59
  621.0 12.9 %collective-permute-done.10 = bf16[48,64,128]{2,1,0:T(8,128)(2,1)S(1)} collective-permute-done((bf16[48,64,128]{2,1,0:T(8,128)(2,1)S(1)}, bf16[48,64,128]{2,1,0:T(8,128)(2,1)S(1)}, u32[]{:S(2)}, u32[]{:S(2)}) %collective-permute-start.10) | collective-permute-done | bytes 786464 | tf_op jit(solution)/shard_map/ppermute | solution.py:59
  640.0 18.4 %multiply_reduce_fusion.7 = (f32[4,128,48]{1,2,0:T(8,128)}, f32[4,128,48]{1,2,0:T(8,128)}, f32[4,128,48]{1,2,0:T(8,128)}, f32[4,128,48,64]{1,3,2,0:T(8,128)}) fusion(bf16[4,128,48,64]{1,3,2,0:T(8,128)(2,1)S(1)} %copy-done.8, f32[4,128,48,64]{1,3,2,0:T(8,128)} %copy.231, f32[4,128,48]{1,2,0:T(8,128)S(1)} %copy-done.53, f32[4,48,64,128]{3,2,1,0:T(8,128)} %fusion.86, ...), kind=kOutput, calls=%fused_computation.29 | convolution fusion | flops 441901056 | bytes 50954240 | tf_op jit(solution)/shard_map/cms,chps->cmhp/dot_general | solution.py:19
  679.3 16.6 %multiply_reduce_fusion.2 = (f32[3072]{0:T(1024)S(1)}, f32[3072]{0:T(1024)S(1)}, f32[3072]{0:T(1024)S(1)}, f32[3072]{0:T(1024)S(1)}, f32[3072]{0:T(1024)S(1)}, /*index=5*/f32[512,3072]{1,0:T(8,128)S(1)}) fusion(f32[528,3072]{1,0:T(8,128)} %copy-done.2, f32[512]{0:T(512)S(1)} %copy-done.75, f32[512]{0:T(512)S(1)} %copy-done.80, f32[512]{0:T(512)S(1)} %copy-done.77, ...), kind=kLoop, calls=%fused_computation.23 | loop fusion | flops 34587648 | bytes 50411520 | tf_op jit(solution)/shard_map/reduce_sum | solution.py:44
  748.2 44.5 %concatenate.63 = bf16[4,384,8,1190]{3,2,1,0:T(8,128)(2,1)} concatenate(bf16[4,384,8,384]{3,2,1,0:T(8,128)(2,1)} %bitcast.341, bf16[4,384,8,384]{3,2,1,0:T(8,128)(2,1)} %bitcast.342, bf16[4,384,8,384]{3,2,1,0:T(8,128)(2,1)} %copy.254, bf16[4,384,8,32]{3,2,1,0:T(8,128)(2,1)} %reshape.307, bf16[4,384,8,6]{3,2,1,0:T(8,128)(2,1)S(1)} %copy.256), dimensions={3} | concatenate | bytes 58490880 | tf_op jit(solution)/shard_map/concatenate | solution.py:285
  792.7 22.1 %copy.279 = bf16[4,8,384,1190]{3,2,1,0:T(8,128)(2,1)} copy(bf16[4,8,384,1190]{3,1,2,0:T(8,128)(2,1)} %bitcast.328) | data formatting | bytes 58490880
  827.8 11.1 fusion.12
  858.9 41.6 %all-reduce.9 = (f32[1536]{0:T(1024)}, f32[4,256]{1,0:T(4,128)}, f32[256]{0:T(256)}, f32[3,48]{1,0:T(4,128)S(1)}) all-reduce(f32[1536]{0:T(1024)S(1)} %get-tuple-element.138, f32[4,256]{1,0:T(4,128)S(1)} %pad_maximum_fusion.5, f32[256]{0:T(256)S(1)} %copy-done.116, ...), channel_id=1, replica_groups=mesh['dp'=4,'head'=4,'tensor'=2] {'dp','head','tensor'}, use_global_device_ids=true, to_apply=%region_10.11 | all-reduce | flops 2960 | bytes 23680 | tf_op jit(solution)/shard_map/psum | solution.py:297
  906.6 237.7 %reduce-scatter.4.cloned.1.call-done = bf16[384,1190]{1,0:T(8,128)(2,1)} async-done(((bf16[12288,1190]{1,0:T(8,128)(2,1)}), bf16[384,1190]{1,0:T(8,128)(2,1)}) %reduce-scatter.4.cloned.1.call-update) | async-done | bytes 913936
  1147.9 31.0 %all_gather.19 = f32[384,256]{0,1:T(8,128)S(1)} all-gather(f32[384,32]{0,1:T(8,128)S(1)} %copy.298), channel_id=1, replica_groups=mesh['dp'=4,'head'=4,'tensor'=2] {'head','tensor'}, dimensions={1}, use_global_device_ids=true | all-gather | bytes 442368 | tf_op jit(solution)/shard_map/all_gather | solution.py:292
  (459 shorter events, 375.8 us)
Async XLA Ops:
  7.3 191.1 %all-gather.4.cloned.1.call-start = ((), (), s32[]{:S(2)}) async-start(), calls=%async_computation.2 | async-start | bytes 30210048 | tf_op jit(solution)/shard_map/all_gather | solution.py:110
  13.5 839.9 %all-reduce.12.cloned.1.call-start = ((), (), s32[]{:S(2)}) async-start(), calls=%async_computation.1 | async-start | bytes 196608 | tf_op jit(solution)/shard_map/psum | solution.py:297
  13.6 68.3 %collective-permute-start = (bf16[16,1536]{1,0:T(8,128)(2,1)S(1)}, bf16[16,1536]{1,0:T(8,128)(2,1)S(1)}, u32[]{:S(2)}, u32[]{:S(2)}) collective-permute-start(bf16[16,1536]{1,0:T(8,128)(2,1)S(1)} %slice.262), channel_id=1, source_target_pairs={{0,1},{1,2},{2,3},{3,4},{4,5},{5,6},{6,7},{8,9},{9,10},{10,11},{11... | collective-permute-start | bytes 147464 | tf_op jit(solution)/shard_map/ppermute | solution.py:55
  78.8 184.3 %copy-start.93 = (f32[1,256]{1,0:T(1,128)}, f32[1,256]{1,0:T(1,128)S(1)}, u32[]{:S(2)}) copy-start(f32[1,256]{1,0:T(1,128)S(1)} %get-tuple-element.206) | copy-start | bytes 3076
  78.9 184.3 %copy-start.95 = (f32[1,256]{1,0:T(1,128)}, f32[1,256]{1,0:T(1,128)S(1)}, u32[]{:S(2)}) copy-start(f32[1,256]{1,0:T(1,128)S(1)} %get-tuple-element.207) | copy-start | bytes 3076
  78.9 184.3 %copy-start.97 = (f32[1,256]{1,0:T(1,128)}, f32[1,256]{1,0:T(1,128)S(1)}, u32[]{:S(2)}) copy-start(f32[1,256]{1,0:T(1,128)S(1)} %get-tuple-element.208) | copy-start | bytes 3076
  78.9 184.3 %copy-start.99 = (f32[1,256]{1,0:T(1,128)}, f32[1,256]{1,0:T(1,128)S(1)}, u32[]{:S(2)}) copy-start(f32[1,256]{1,0:T(1,128)S(1)} %get-tuple-element.209) | copy-start | bytes 3076
  79.0 204.4 %copy-start.74 = (f32[512]{0:T(512)}, f32[512]{0:T(512)S(1)}, u32[]{:S(2)}) copy-start(f32[512]{0:T(512)S(1)} %get-tuple-element.210) | copy-start | bytes 6148
  79.0 204.4 %copy-start.76 = (f32[512]{0:T(512)}, f32[512]{0:T(512)S(1)}, u32[]{:S(2)}) copy-start(f32[512]{0:T(512)S(1)} %get-tuple-element.211) | copy-start | bytes 6148
  79.7 203.8 %copy-start.66 = (f32[1,3072]{1,0:T(1,128)}, f32[1,3072]{1,0:T(1,128)S(1)}, u32[]{:S(2)}) copy-start(f32[1,3072]{1,0:T(1,128)S(1)} %get-tuple-element.197) | copy-start | bytes 36868
  79.7 203.8 %copy-start.68 = (f32[1,3072]{1,0:T(1,128)}, f32[1,3072]{1,0:T(1,128)S(1)}, u32[]{:S(2)}) copy-start(f32[1,3072]{1,0:T(1,128)S(1)} %get-tuple-element.198) | copy-start | bytes 36868
  82.8 229.6 %copy-start.19 = (bf16[528,1536]{1,0:T(8,128)(2,1)}, bf16[528,1536]{1,0:T(8,128)(2,1)S(1)}, u32[]{:S(2)}) copy-start(bf16[528,1536]{1,0:T(8,128)(2,1)S(1)} %multiply_convert_fusion.6) | copy-start | bytes 4866052
  324.9 20.6 %collective-permute-start.1 = (bf16[48,64,128]{2,1,0:T(8,128)(2,1)S(1)}, bf16[48,64,128]{2,1,0:T(8,128)(2,1)S(1)}, u32[]{:S(2)}, u32[]{:S(2)}) collective-permute-start(bf16[48,64,128]{2,1,0:T(8,128)(2,1)S(1)} %fusion.17), channel_id=1, source_target_pairs={{0,1},{1,2},{2,3},{3,4},{4,5},{5,6},{6,7},{8,9},{9,10},{10,11},{11... | collective-permute-start | bytes 2359304 | tf_op jit(solution)/shard_map/ppermute | solution.py:55
  345.5 20.8 %collective-permute-start.3 = (bf16[48,64,128]{2,1,0:T(8,128)(2,1)S(1)}, bf16[48,64,128]{2,1,0:T(8,128)(2,1)S(1)}, u32[]{:S(2)}, u32[]{:S(2)}) collective-permute-start(bf16[48,64,128]{2,1,0:T(8,128)(2,1)S(1)} %collective-permute-done.1), channel_id=1, source_target_pairs={{0,1},{1,2},{2,3},{3,4},{4,5},{5,6},{6,7},{8,9},{9,10},{10,11},{11... | collective-permute-start | bytes 2359304 | tf_op jit(solution)/shard_map/ppermute | solution.py:55
  349.9 16.4 %collective-permute-start.2 = (f32[48]{0:T(128)S(1)}, f32[48]{0:T(128)S(1)}, u32[]{:S(2)}, u32[]{:S(2)}) collective-permute-start(f32[48]{0:T(128)S(1)} %multiply_multiply_fusion.9), channel_id=1, source_target_pairs={{0,1},{1,2},{2,3},{3,4},{4,5},{5,6},{6,7},{8,9},{9,10},{10,11},{11... | collective-permute-start | bytes 584 | tf_op jit(solution)/shard_map/ppermute | solution.py:55
  367.5 44.6 %collective-permute-start.5 = (bf16[48,64,128]{2,1,0:T(8,128)(2,1)}, bf16[48,64,128]{2,1,0:T(8,128)(2,1)}, u32[]{:S(2)}, u32[]{:S(2)}) collective-permute-start(bf16[48,64,128]{2,1,0:T(8,128)(2,1)} %fusion.18), channel_id=1, source_target_pairs={{0,2},{1,3},{2,4},{3,5},{4,6},{5,7},{8,10},{9,11},{10,12},{11,13},... | collective-permute-start | bytes 2359304 | tf_op jit(solution)/shard_map/ppermute | solution.py:55
  374.7 25.6 %collective-permute-start.7 = (f32[48]{0:T(128)S(1)}, f32[48]{0:T(128)S(1)}, u32[]{:S(2)}, u32[]{:S(2)}) collective-permute-start(f32[48]{0:T(128)S(1)} %multiply_multiply_fusion.9), channel_id=1, source_target_pairs={{1,0},{2,1},{3,2},{4,3},{5,4},{6,5},{7,6},{9,8},{10,9},{11,10},{12... | collective-permute-start | bytes 584 | tf_op jit(solution)/shard_map/ppermute | solution.py:59
  395.7 16.3 %collective-permute-start.4 = (f32[48]{0:T(128)S(1)}, f32[48]{0:T(128)S(1)}, u32[]{:S(2)}, u32[]{:S(2)}) collective-permute-start(f32[48]{0:T(128)S(1)} %collective-permute-done.2), channel_id=1, source_target_pairs={{0,1},{1,2},{2,3},{3,4},{4,5},{5,6},{6,7},{8,9},{9,10},{10,11},{11... | collective-permute-start | bytes 584 | tf_op jit(solution)/shard_map/ppermute | solution.py:55
  400.3 11.8 collective-permute-start.9
  537.5 55.1 %collective-permute-start.6 = (bf16[48,64,128]{2,1,0:T(8,128)(2,1)}, bf16[48,64,128]{2,1,0:T(8,128)(2,1)}, u32[]{:S(2)}, u32[]{:S(2)}) collective-permute-start(bf16[48,64,128]{2,1,0:T(8,128)(2,1)} %fusion.15), channel_id=1, source_target_pairs={{1,0},{2,1},{3,2},{4,3},{5,4},{6,5},{7,6},{9,8},{10,9},{11,10},{12... | collective-permute-start | bytes 2359304 | tf_op jit(solution)/shard_map/ppermute | solution.py:59
  592.5 20.8 %collective-permute-start.8 = (bf16[48,64,128]{2,1,0:T(8,128)(2,1)}, bf16[48,64,128]{2,1,0:T(8,128)(2,1)S(1)}, u32[]{:S(2)}, u32[]{:S(2)}) collective-permute-start(bf16[48,64,128]{2,1,0:T(8,128)(2,1)} %collective-permute-done.6), channel_id=1, source_target_pairs={{1,0},{2,1},{3,2},{4,3},{5,4},{6,5},{7,6},{9,8},{10,9},{11,10},{12... | collective-permute-start | bytes 2359304 | tf_op jit(solution)/shard_map/ppermute | solution.py:59
  614.9 19.0 %collective-permute-start.10 = (bf16[48,64,128]{2,1,0:T(8,128)(2,1)S(1)}, bf16[48,64,128]{2,1,0:T(8,128)(2,1)S(1)}, u32[]{:S(2)}, u32[]{:S(2)}) collective-permute-start(bf16[48,64,128]{2,1,0:T(8,128)(2,1)S(1)} %fusion.19), channel_id=1, source_target_pairs={{2,0},{3,1},{4,2},{5,3},{6,4},{7,5},{10,8},{11,9},{12,10},{13,11},... | collective-permute-start | bytes 2359304 | tf_op jit(solution)/shard_map/ppermute | solution.py:59
  733.2 411.0 %reduce-scatter.4.cloned.1.call-start = ((), (), s32[]{:S(2)}) async-start(), calls=%async_computation.3 | async-start | bytes 32440320
  844.8 11.4 collective-permute-start.11
  (131 other events, 1917.3 us)
Sparse Core Ops, SparseCore 0:
  13.6 184.7 all-gather.3
  733.3 120.0 all-reduce.11
  859.8 284.3 reduce-scatter.3

commit v2 on v1

--- a/solution.py
+++ b/solution.py
@@ -1,6 +1,10 @@
+import functools
+
 import jax
 import jax.numpy as jnp
 from jax import lax
+from jax.experimental import pallas as pl
+from jax.experimental.pallas import tpu as pltpu
 from jax.sharding import PartitionSpec as P
 
 EPSILON = 1e-05
@@ -13,6 +17,8 @@
 ALL = ("dp", "head", "tensor")
 BF16 = jnp.bfloat16
 F32 = jnp.float32
+MESH = pl.DeviceIdType.MESH
+VMEM_BYTES = 56 << 20
 
 
 def dot16(pattern, left, right):
@@ -26,6 +32,541 @@
 def silu_grad(v):
     gate = jax.nn.sigmoid(v)
     return gate * (1.0 + v * (1.0 - gate))
+
+
+def coordinates():
+    dp = lax.axis_index("dp")
+    return lax.div(dp, 2), lax.rem(dp, 2), lax.axis_index("head"), lax.axis_index("tensor")
+
+
+def enter_kernel(x, core, head, tensor, xs, hs, ts, sibling):
+    barrier = pltpu.get_barrier_semaphore()
+    count = 0
+    for step in range(1, hs):
+        pl.semaphore_signal(barrier, 1, device_id={"head": lax.rem(head + step, hs)}, device_id_type=MESH)
+        count += 1
+    for step in range(1, ts):
+        pl.semaphore_signal(barrier, 1, device_id={"tensor": lax.rem(tensor + step, ts)}, device_id_type=MESH)
+        count += 1
+    for step in range(1, xs):
+        other = 2 * lax.rem(x + step, xs) + core
+        pl.semaphore_signal(barrier, 1, device_id={"dp": other}, device_id_type=MESH)
+        count += 1
+    if sibling:
+        pl.semaphore_signal(barrier, 1, device_id={"dp": 2 * x + 1 - core}, device_id_type=MESH)
+        count += 1
+    pl.semaphore_wait(barrier, count)
+
+
+def gather_kernel(sizes, chunks, kinds, *refs):
+    xs, hs, ts = sizes
+    parts, small = refs[:kinds], refs[kinds]
+    fulls, small_full = refs[kinds + 1 : 2 * kinds + 1], refs[2 * kinds + 1]
+    send, recv, small_send, small_recv, own_sem = refs[2 * kinds + 2 :]
+    x, core, head, tensor = coordinates()
+    dp = 2 * x + core
+    for kind in range(kinds):
+        pltpu.make_async_copy(
+            parts[kind], fulls[kind].at[dp, head, tensor], own_sem.at[kind]
+        ).start()
+    pltpu.make_async_copy(small, small_full.at[head, tensor], own_sem.at[kinds]).start()
+    enter_kernel(x, core, head, tensor, xs, hs, ts, True)
+
+    def copy(src, dst, index, slot, device):
+        return pltpu.make_async_remote_copy(
+            src_ref=src,
+            dst_ref=dst,
+            send_sem=send.at[index, slot],
+            recv_sem=recv.at[index, slot],
+            device_id=device,
+            device_id_type=MESH,
+        )
+
+    def along_head(index):
+        kind, start, length, _ = chunks[index]
+        rows = pl.ds(start, length)
+        return [
+            copy(
+                parts[kind].at[rows],
+                fulls[kind].at[dp, head, tensor, rows],
+                index,
+                step - 1,
+                {"head": lax.rem(head + step, hs)},
+            )
+            for step in range(1, hs)
+        ]
+
+    def over(index, axis, second):
+        kind, start, length, _ = chunks[index]
+        rows = pl.ds(start, length)
+        base = hs - 1 if second else hs - 1 + max(xs, ts)
+        copies = []
+        if axis == "tensor":
+            homes = [dp] if second else [2 * home + core for home in range(xs)]
+            for step in range(1, ts):
+                for home in homes:
+                    view = fulls[kind].at[home, :, tensor, rows]
+                    device = {"tensor": lax.rem(tensor + step, ts)}
+                    copies.append(copy(view, view, index, base + len(copies), device))
+        else:
+            for step in range(1, xs):
+                view = fulls[kind].at[dp, :, tensor, rows] if second else fulls[kind].at[dp, :, :, rows]
+                device = {"dp": 2 * lax.rem(x + step, xs) + core}
+                copies.append(copy(view, view, index, base + len(copies), device))
+        return copies
+
+    def to_sibling(index):
+        kind, start, length, _ = chunks[index]
+        rows = pl.ds(start, length)
+        base = hs - 1 + max(xs, ts) + max(xs, xs * ts)
+        return [
+            copy(
+                fulls[kind].at[2 * home + core, :, :, rows],
+                fulls[kind].at[2 * home + core, :, :, rows],
+                index,
+                base + home,
+                {"dp": 2 * x + 1 - core},
+            )
+            for home in range(xs)
+        ]
+
+    def stage(index, number):
+        tensor_first = chunks[index][3]
+        if number == 0:
+            return along_head(index)
+        if number == 1:
+            return over(index, "tensor" if tensor_first else "x", True)
+        if number == 2:
+            return over(index, "x" if tensor_first else "tensor", False)
+        return to_sibling(index)
+
+    small_tensor = [
+        pltpu.make_async_remote_copy(
+            src_ref=small,
+            dst_ref=small_full.at[head, tensor],
+            send_sem=small_send.at[step - 1],
+            recv_sem=small_recv.at[step - 1],
+            device_id={"tensor": lax.rem(tensor + step, ts)},
+            device_id_type=MESH,
+        )
+        for step in range(1, ts)
+    ]
+    small_head = [
+        pltpu.make_async_remote_copy(
+            src_ref=small_full.at[head],
+            dst_ref=small_full.at[head],
+            send_sem=small_send.at[ts + step - 2],
+            recv_sem=small_recv.at[ts + step - 2],
+            device_id={"head": lax.rem(head + step, hs)},
+            device_id_type=MESH,
+        )
+        for step in range(1, hs)
+    ]
+    total = len(chunks)
+    ahead = 4
+    for one in small_tensor:
+        one.start()
+    for index in range(min(ahead, total)):
+        for one in stage(index, 0):
+            one.start()
+    for kind in range(kinds):
+        pltpu.make_async_copy(
+            parts[kind], fulls[kind].at[dp, head, tensor], own_sem.at[kind]
+        ).wait()
+    pltpu.make_async_copy(small, small_full.at[head, tensor], own_sem.at[kinds]).wait()
+    for one in small_tensor:
+        one.wait_recv()
+    for one in small_head:
+        one.start()
+    for tick in range(total + 6):
+        for number in range(4):
+            index = tick - 2 * number
+            if 0 <= index < total:
+                for one in stage(index, number):
+                    one.wait_recv()
+                if number < 3:
+                    for one in stage(index, number + 1):
+                        one.start()
+                if number == 0 and index + ahead < total:
+                    for one in stage(index + ahead, 0):
+                        one.start()
+    for one in small_head:
+        one.wait_recv()
+    for one in small_tensor + small_head:
+        one.wait_send()
+    for index in range(total):
+        for number in range(4):
+            for one in stage(index, number):
+                one.wait_send()
+
+
+def row_chunks(rows, kinds, pieces):
+    step = rows // pieces
+    return [
+        (kind, piece * step, step, piece % 2 == 0) for kind in range(kinds) for piece in range(pieces)
+    ]
+
+
+def gather_weights(parts, small, sizes):
+    xs, hs, ts = sizes
+    kinds = len(parts)
+    chunks = row_chunks(parts[0].shape[0], kinds, 4)
+    slots = hs - 1 + max(xs, ts) + max(xs, xs * ts) + xs
+    full = [jax.ShapeDtypeStruct((2 * xs, hs, ts) + part.shape, part.dtype) for part in parts]
+    full.append(jax.ShapeDtypeStruct((hs, ts) + small.shape, small.dtype))
+    anywhere = pl.BlockSpec(memory_space=pl.ANY)
+    return pl.pallas_call(
+        functools.partial(gather_kernel, sizes, chunks, kinds),
+        out_shape=full,
+        in_specs=[anywhere] * (kinds + 1),
+        out_specs=[anywhere] * (kinds + 1),
+        scratch_shapes=[
+            pltpu.SemaphoreType.DMA((len(chunks), slots)),
+            pltpu.SemaphoreType.DMA((len(chunks), slots)),
+            pltpu.SemaphoreType.DMA((hs + ts,)),
+            pltpu.SemaphoreType.DMA((hs + ts,)),
+            pltpu.SemaphoreType.DMA((kinds + 1,)),
+        ],
+        compiler_params=pltpu.CompilerParams(
+            collective_id=0, has_side_effects=True, vmem_limit_bytes=VMEM_BYTES
+        ),
+    )(*parts, small)
+
+
+def scatter_kernel(sizes, chunks, kinds, *refs):
+    xs, hs, ts = sizes
+    parts, small = refs[:kinds], refs[kinds]
+    outs, small_out = refs[kinds + 1 : 2 * kinds + 1], refs[2 * kinds + 1]
+    rest = refs[2 * kinds + 2 :]
+    bufs, rest = rest[: 4 * len(chunks)], rest[4 * len(chunks) :]
+    small_acc, small_in, send, recv, small_send, small_recv, own_sem = rest
+    x, core, head, tensor = coordinates()
+    dp = 2 * x + core
+    total = len(chunks)
+
+    def loads(index):
+        kind, start, length, x_first = chunks[index]
+        rows = pl.ds(start, length)
+        held = bufs[4 * index]
+        view = parts[kind].at[x, :, :, rows] if x_first else parts[kind].at[:, :, tensor, rows]
+        return pltpu.make_async_copy(view, held, own_sem.at[index])
+
+    def copy(src, dst, index, slot, device):
+        return pltpu.make_async_remote_copy(
+            src_ref=src,
+            dst_ref=dst,
+            send_sem=send.at[index, slot],
+            recv_sem=recv.at[index, slot],
+            device_id=device,
+            device_id_type=MESH,
+        )
+
+    def stage(index, number):
+        kind, start, length, x_first = chunks[index]
+        rows = pl.ds(start, length)
+        held, first, second, third = bufs[4 * index : 4 * index + 4]
+        most = max(xs, ts) - 1
+        if number == 0 and x_first:
+            return [
+                copy(
+                    parts[kind].at[lax.rem(x + step, xs), :, :, rows],
+                    first.at[step - 1],
+                    index,
+                    step - 1,
+                    {"dp": 2 * lax.rem(x + step, xs) + core},
+                )
+                for step in range(1, xs)
+            ]
+        if number == 0:
+            return [
+                copy(
+                    parts[kind].at[:, :, lax.rem(tensor + step, ts), rows],
+                    first.at[step - 1],
+                    index,
+                    step - 1,
+                    {"tensor": lax.rem(tensor + step, ts)},
+                )
+                for step in range(1, ts)
+            ]
+        if number == 1 and x_first:
+            return [
+                copy(
+                    held.at[:, lax.rem(tensor + step, ts)],
+                    second.at[step - 1],
+                    index,
+                    most + step - 1,
+                    {"tensor": lax.rem(tensor + step, ts)},
+                )
+                for step in range(1, ts)
+            ]
+        if number == 1:
+            return [
+                copy(
+                    held.at[lax.rem(x + step, xs)],
+                    second.at[step - 1],
+                    index,
+                    most + step - 1,
+                    {"dp": 2 * lax.rem(x + step, xs) + core},
+                )
+                for step in range(1, xs)
+            ]
+        copies = []
+        for step in range(1, hs):
+            other = lax.rem(head + step, hs)
+            view = held.at[other, tensor] if x_first else held.at[x, other]
+            copies.append(
+                copy(view, third.at[step - 1], index, 2 * most + step - 1, {"head": other})
+            )
+        return copies
+
+    def add(index, number):
+        kind, start, length, x_first = chunks[index]
+        held, first, second, third = bufs[4 * index : 4 * index + 4]
+        if number == 0:
+
+            @pl.loop(0, held.shape[0])
+            def _(one):
+                for two in range(held.shape[1]):
+                    value = held[one, two].astype(F32)
+                    for step in range(first.shape[0]):
+                        value = value + first[step, one, two].astype(F32)
+                    held[one, two] = value.astype(BF16)
+
+        elif number == 1:
+
+            @pl.loop(0, hs)
+            def _(one):
+                where = (one, tensor) if x_first else (x, one)
+                value = held[where].astype(F32)
+                for step in range(second.shape[0]):
+                    value = value + second[step, one].astype(F32)
+                held[where] = value.astype(BF16)
+
+        else:
+            where = (head, tensor) if x_first else (x, head)
+            value = held[where].astype(F32)
+            for step in range(third.shape[0]):
+                value = value + third[step].astype(F32)
+            outs[kind][start : start + length, :] = value
+
+    small_slots = [1, xs - 1, ts - 1, hs - 1]
+    small_base = [0, 1, xs, xs + ts - 1]
+
+    def small_stage(number):
+        copies = []
+        for step in range(1, small_slots[number] + 1):
+            slot = small_base[number] + step - 1
+            device = (
+                {"dp": 2 * x + 1 - core},
+                {"dp": 2 * lax.rem(x + step, xs) + core},
+                {"tensor": lax.rem(tensor + step, ts)},
+                {"head": lax.rem(head + step, hs)},
+            )[number]
+            copies.append(
+                pltpu.make_async_remote_copy(
+                    src_ref=small if number == 0 else small_acc.at[number - 1],
+                    dst_ref=small_in.at[slot],
+                    send_sem=small_send.at[slot],
+                    recv_sem=small_recv.at[slot],
+                    device_id=device,
+                    device_id_type=MESH,
+                )
+            )
+        return copies
+
+    def small_add(number):
+        mine = small[...] if number == 0 else small_acc[number - 1]
+        size = small_slots[number] + 1
+        place = (core, x, tensor, head)[number]
+        value = None
+        for at in range(size):
+            step = lax.rem(place - at + size, size)
+            slot = small_base[number] + jnp.maximum(step - 1, 0)
+            here = jnp.where(step == 0, mine, small_in[slot])
+            value = here if value is None else value + here
+        if number < 3:
+            small_acc[number] = value
+        else:
+            small_out[...] = value
+
+    for index in range(total):
+        loads(index).start()
+    enter_kernel(x, core, head, tensor, xs, hs, ts, True)
+    ahead = 4
+    for one in small_stage(0):
+        one.start()
+    for index in range(min(ahead, total)):
+        for one in stage(index, 0):
+            one.start()
+    for tick in range(total + 4):
+        for number in range(3):
+            index = tick - 2 * number
+            if 0 <= index < total:
+                for one in stage(index, number):
+                    one.wait_recv()
+                if number == 0:
+                    loads(index).wait()
+                    if index + ahead < total:
+                        for one in stage(index + ahead, 0):
+                            one.start()
+                add(index, number)
+                if number < 2:
+                    for one in stage(index, number + 1):
+                        one.start()
+        if tick < 4:
+            for one in small_stage(tick):
+                one.wait_recv()
+            small_add(tick)
+            if tick < 3:
+                for one in small_stage(tick + 1):
+                    one.start()
+    for number in range(4):
+        for one in small_stage(number):
+            one.wait_send()
+    for index in range(total):
+        for number in range(3):
+            for one in stage(index, number):
+                one.wait_send()
+
+
+def scatter_gradients(parts, small, sizes):
+    xs, hs, ts = sizes
+    kinds = len(parts)
+    chunks = row_chunks(parts[0].shape[3], kinds, 4)
+    scratch = []
+    for kind, _, length, x_first in chunks:
+        cols = parts[kind].shape[4]
+        held = (hs, ts) if x_first else (xs, hs)
+        near, far = (xs, ts) if x_first else (ts, xs)
+        scratch += [
+            pltpu.VMEM(held + (length, cols), BF16),
+            pltpu.VMEM((near - 1,) + held + (length, cols), BF16),
+            pltpu.VMEM((far - 1, hs, length, cols), BF16),
+            pltpu.VMEM((hs - 1, length, cols), BF16),
+        ]
+    slots = 2 * (max(xs, ts) - 1) + hs - 1
+    small_slots = xs + ts + hs - 2
+    anywhere = pl.BlockSpec(memory_space=pl.ANY)
+    whole = pl.BlockSpec(memory_space=pltpu.VMEM)
+    return pl.pallas_call(
+        functools.partial(scatter_kernel, sizes, chunks, kinds),
+        out_shape=[jax.ShapeDtypeStruct(part.shape[3:], F32) for part in parts]
+        + [jax.ShapeDtypeStruct(small.shape, F32)],
+        in_specs=[anywhere] * kinds + [whole],
+        out_specs=[whole] * (kinds + 1),
+        scratch_shapes=scratch
+        + [
+            pltpu.VMEM((3,) + small.shape, F32),
+            pltpu.VMEM((small_slots,) + small.shape, F32),
+            pltpu.SemaphoreType.DMA((len(chunks), slots)),
+            pltpu.SemaphoreType.DMA((len(chunks), slots)),
+            pltpu.SemaphoreType.DMA((small_slots,)),
+            pltpu.SemaphoreType.DMA((small_slots,)),
+            pltpu.SemaphoreType.DMA((len(chunks),)),
+        ],
+        compiler_params=pltpu.CompilerParams(
+            collective_id=1, has_side_effects=True, vmem_limit_bytes=VMEM_BYTES
+        ),
+    )(*parts, small)
+
+
+def group_of(cols):
+    return 1 if cols % 128 == 0 else 128 // cols if 128 % cols == 0 else 2
+
+
+def local_params():
+    return pltpu.CompilerParams(vmem_limit_bytes=VMEM_BYTES)
+
+
+def onto_columns(rows, pieces):
+    dps, hts, depth, cols = pieces.shape
+    group = group_of(cols)
+    count = rows.shape[0]
+
+    def kernel(rows_ref, piece_ref, out_ref):
+        for one in range(group):
+            weights = piece_ref[:, one].reshape(dps * depth, cols)
+            out_ref[:, one * cols : (one + 1) * cols] = jnp.dot(
+                rows_ref[...], weights, preferred_element_type=F32
+            )
+
+    return pl.pallas_call(
+        kernel,
+        grid=(hts // group,),
+        out_shape=jax.ShapeDtypeStruct((count, hts * cols), F32),
+        in_specs=[
+            pl.BlockSpec(rows.shape, lambda j: (0, 0)),
+            pl.BlockSpec((dps, group, depth, cols), lambda j: (0, j, 0, 0)),
+        ],
+        out_specs=pl.BlockSpec((count, group * cols), lambda j: (0, j)),
+        compiler_params=local_params(),
+        cost_estimate=pl.CostEstimate(
+            flops=2 * count * pieces.size, bytes_accessed=2 * pieces.size, transcendentals=0
+        ),
+    )(rows, pieces)
+
+
+def back_from_columns(values, pieces):
+    dps, hts, depth, cols = pieces.shape
+    group = group_of(cols)
+    count = values.shape[0]
+
+    def kernel(value_ref, piece_ref, out_ref):
+        @pl.when(pl.program_id(0) == 0)
+        def _():
+            out_ref[...] = jnp.zeros_like(out_ref)
+
+        for one in range(group):
+            weights = piece_ref[:, one].reshape(dps * depth, cols)
+            out_ref[...] += lax.dot_general(
+                value_ref[:, one * cols : (one + 1) * cols],
+                weights,
+                (((1,), (1,)), ((), ())),
+                preferred_element_type=F32,
+            )
+
+    return pl.pallas_call(
+        kernel,
+        grid=(hts // group,),
+        out_shape=jax.ShapeDtypeStruct((count, dps * depth), F32),
+        in_specs=[
+            pl.BlockSpec((count, group * cols), lambda j: (0, j)),
+            pl.BlockSpec((dps, group, depth, cols), lambda j: (0, j, 0, 0)),
+        ],
+        out_specs=pl.BlockSpec((count, dps * depth), lambda j: (0, 0)),
+        compiler_params=local_params(),
+        cost_estimate=pl.CostEstimate(
+            flops=2 * count * pieces.size, bytes_accessed=2 * pieces.size, transcendentals=0
+        ),
+    )(values, pieces)
+
+
+def gradient_pieces(left, values, hts):
+    xs, depth, count = left.shape
+    cols = values.shape[1] // hts
+    group = group_of(cols)
+
+    def kernel(left_ref, value_ref, out_ref):
+        for at in range(xs):
+            for one in range(group):
+                out_ref[at, one] = jnp.dot(
+                    left_ref[at], value_ref[:, one * cols : (one + 1) * cols], preferred_element_type=F32
+                ).astype(BF16)
+
+    return pl.pallas_call(
+        kernel,
+        grid=(hts // group,),
+        out_shape=jax.ShapeDtypeStruct((xs, hts, depth, cols), BF16),
+        in_specs=[
+            pl.BlockSpec(left.shape, lambda j: (0, 0, 0)),
+            pl.BlockSpec((count, group * cols), lambda j: (0, j)),
+        ],
+        out_specs=pl.BlockSpec((xs, group, depth, cols), lambda j: (0, j, 0, 0)),
+        compiler_params=local_params(),
+        cost_estimate=pl.CostEstimate(
+            flops=2 * left.size * values.shape[1], bytes_accessed=2 * values.size, transcendentals=0
+        ),
+    )(left, values)
 
 
 def conv_before(ext, taps, bias, same):
@@ -104,24 +645,30 @@
     chunks = own // CHUNK
     head_width = inner // heads
 
+    sizes = (dp_size // 2, lax.axis_size("head"), lax.axis_size("tensor"))
+    core = lax.rem(lax.axis_index("dp"), 2)
     bc_own = lax.dynamic_slice_in_dim(w_bc, place * bc_cols, bc_cols, 1)
-    side = heads_own + bc_cols
-    pack = jnp.concatenate([w_zx.reshape(dp_rows, 2 * cols), w_out, bc_own, w_dt], 1)
-    full = lax.all_gather(pack, ALL, axis=0, tiled=False).reshape(dp_size, size, dp_rows, -1)
-    full = jnp.moveaxis(full, 1, 2).reshape(width, size, -1)
-    w_z = full[:, :, :cols].reshape(width, inner)
-    w_x = full[:, :, cols : 2 * cols].reshape(width, inner)
-    w_o = full[:, :, 2 * cols : 3 * cols].reshape(width, inner)
-    w_b = full[:, :, 3 * cols : 3 * cols + bc_cols].reshape(width, state2)
-    w_d = full[:, :, 3 * cols + bc_cols :].reshape(width, heads)
-    per_head = jnp.concatenate(
-        [dt_bias[None], a_log[None], d_skip[None]], 0
-    )
-    per_channel = jnp.concatenate([conv_x_weight, conv_x_bias[None], norm_gain[None]], 0)
-    per_head = lax.all_gather(per_head, SEQ, axis=1, tiled=True)
-    per_channel = lax.all_gather(per_channel, SEQ, axis=1, tiled=True)
+    side = bc_cols + heads_own
+    side_part = jnp.pad(jnp.concatenate([bc_own, w_dt], 1), ((0, 0), (0, 128 - side)))
     taps = conv_x_weight.shape[0]
+    small_rows = [conv_x_weight, conv_x_bias[None], norm_gain[None]]
+    head_rows = jnp.stack([dt_bias, a_log, d_skip])
+    small = jnp.concatenate(small_rows + [jnp.pad(head_rows, ((0, 0), (0, cols - heads_own)))], 0)
+    small = jnp.pad(small, ((0, 16 - small.shape[0]), (0, 0)))
+    gathered = gather_weights([side_part, w_zx[:, 1], w_zx[:, 0], w_out], small, sizes)
+    side_full, w_x, w_z, w_o, small_full = gathered
+
+    def pieces(v):
+        return v.reshape(dp_size, size, dp_rows, v.shape[-1])
+
+    side_full, w_x, w_z, w_o = pieces(side_full), pieces(w_x), pieces(w_z), pieces(w_o)
+    side_cols = jnp.moveaxis(side_full[..., :side], 1, 2).reshape(width, size, side)
+    w_b = side_cols[:, :, :bc_cols].reshape(width, state2)
+    w_d = side_cols[:, :, bc_cols:].reshape(width, heads)
+    small_full = jnp.moveaxis(small_full.reshape(size, 16, cols), 0, 1)
+    per_channel = small_full.reshape(16, inner)
     x_taps, x_bias, out_gain = per_channel[:taps], per_channel[taps], per_channel[taps + 1]
+    per_head = small_full[taps + 2 : taps + 5, :, :heads_own].reshape(3, heads)
     dt_shift, log_rate, skip = per_head[0], per_head[1], per_head[2]
     rate = -jnp.exp(log_rate)
     skip_wide = jnp.repeat(skip, head_width)
@@ -145,8 +692,8 @@
     inv_ext = lax.rsqrt(jnp.mean(rows_ext * rows_ext, axis=1, keepdims=True) + EPSILON)
     normed = (rows_ext * inv_ext * norm_in_gain).astype(BF16)
     rows_in, inv_rms = rows_ext[HALO:], inv_ext[HALO:]
-    x_ext = dot16("td,dk->tk", normed, w_x)
-    z = dot16("td,dk->tk", normed[HALO:], w_z)
+    x_ext = onto_columns(normed, w_x)
+    z = onto_columns(normed[HALO:], w_z)
     bc_ext = dot16("td,dk->tk", normed, w_b)
     dt_raw = dot16("td,dk->tk", normed[HALO:], w_d)
 
@@ -199,9 +746,8 @@
     gated = y * z_gate
     inv_gate = lax.rsqrt(jnp.mean(gated * gated, axis=1, keepdims=True) + EPSILON)
     gated_out = (gated * inv_gate * out_gain).astype(BF16)
-    block_out = (rows_in + dot16("ti,di->td", gated_out, w_o)).astype(BF16)
-    grad_gate = dot16("td,di->ti", cotangent, w_o)
-    grad_wout = dot16("td,ti->di", cotangent, gated_out)
+    block_out = (rows_in + back_from_columns(gated_out, w_o)).astype(BF16)
+    grad_gate = onto_columns(cotangent, w_o)
     grad_norm_gain = jnp.sum(grad_gate * gated * inv_gate, axis=0)
     scaled_gate = grad_gate * out_gain
     cross = jnp.sum(scaled_gate * gated, axis=1, keepdims=True)
@@ -256,13 +802,12 @@
     )
     low_x = gx.astype(BF16)
     low_bc = gbc.astype(BF16)
-    above = jnp.zeros((HALO, 1), BF16)
     low_z = dz.astype(BF16)
     low_dt = ddt_raw.astype(BF16)
     normed_own = normed[HALO:]
 
-    own_part = dot16("tk,dk->td", low_z, w_z) + dot16("tk,dk->td", low_dt, w_d)
-    ext_part = dot16("tk,dk->td", low_x, w_x) + dot16("tk,dk->td", low_bc, w_b)
+    own_part = back_from_columns(low_z, w_z) + dot16("tk,dk->td", low_dt, w_d)
+    ext_part = back_from_columns(low_x, w_x) + dot16("tk,dk->td", low_bc, w_b)
     last = from_later(ext_part[:HALO], 1, size)
     grad_normed = own_part + ext_part[HALO:]
     grad_normed = grad_normed.at[own - HALO :].add(last)
@@ -274,30 +819,57 @@
     )
     grad_in_gain = jnp.sum(grad_normed * rows_in * inv_rms, axis=0)
 
-    grad_z = dot16("td,tk->dk", normed_own, low_z)
-    grad_d = dot16("td,tk->dk", normed_own, low_dt)
-    grad_x = dot16("td,tk->dk", normed, low_x)
-    grad_b = dot16("td,tk->dk", normed, low_bc)
-
-    def columns(v):
-        return v.astype(BF16).reshape(width, size, -1)
-
-    parts = jnp.concatenate([columns(v) for v in (grad_z, grad_x, grad_wout, grad_b, grad_d)], 2)
-    parts = jnp.moveaxis(parts.reshape(dp_size, dp_rows, size, -1), 2, 1)
-    mine = lax.psum_scatter(
-        parts.reshape(dp_size * size * dp_rows, -1), ALL, scatter_dimension=0, tiled=True
-    ).astype(F32)
-    grad_wzx = mine[:, : 2 * cols].reshape(dp_rows, 2, cols)
-    grad_wo = mine[:, 2 * cols : 3 * cols]
-    grad_wbc = lax.all_gather(mine[:, 3 * cols : 3 * cols + bc_cols], SEQ, axis=1, tiled=True)
-    grad_wdt = mine[:, 3 * cols + bc_cols :]
-
-    channel_sum = jnp.concatenate([grad_taps, grad_bias[None], grad_norm_gain[None]], 0)
-    head_sum = jnp.stack([grad_shift, grad_log, grad_skip], 0)
-    gain_sum, taps_sum, bias_sum, channel_sum, head_sum = lax.psum(
-        (grad_in_gain, grad_bc_taps, grad_bc_bias, channel_sum, head_sum), ALL
-    )
-    channel_own = lax.dynamic_slice_in_dim(channel_sum, place * cols, cols, 1)
+    def to_pair(v):
+        pairs = [(at, at ^ 1) for at in range(dp_size)]
+        other = lax.ppermute(v, "dp", pairs)
+        return jnp.where(core == 0, jnp.stack([v, other]), jnp.stack([other, v])).reshape(
+            2 * v.shape[0], -1
+        )
+
+    def left_of(v):
+        split_rows = v.T.reshape(dp_size // 2, 2, dp_rows, v.shape[0])
+        return lax.dynamic_index_in_dim(split_rows, core, 1, keepdims=False)
+
+    normed_pair = to_pair(normed)
+    left_ext = left_of(normed_pair)
+    low_z_ext = jnp.pad(low_z, ((HALO, 0), (0, 0)))
+    low_side = jnp.concatenate(
+        [
+            low_bc.reshape(-1, size, bc_cols),
+            jnp.pad(low_dt, ((HALO, 0), (0, 0))).reshape(-1, size, heads_own),
+        ],
+        2,
+    )
+    low_side = jnp.pad(low_side, ((0, 0), (0, 0), (0, 128 - side))).reshape(-1, size * 128)
+    parts = [
+        gradient_pieces(left_of(to_pair(cotangent)), to_pair(gated_out), size),
+        gradient_pieces(left_ext, to_pair(low_z_ext), size),
+        gradient_pieces(left_ext, to_pair(low_x), size),
+        gradient_pieces(left_ext, to_pair(low_side), size),
+    ]
+    parts = [v.reshape((dp_size // 2,) + sizes[1:] + v.shape[2:]) for v in parts]
+    head_sum = jnp.stack([grad_shift, grad_log, grad_skip], 0).reshape(-1)
+    row = jnp.concatenate([grad_in_gain, grad_bc_taps.reshape(-1), grad_bc_bias])
+    small_sum = jnp.concatenate(
+        [
+            grad_taps,
+            grad_bias[None],
+            grad_norm_gain[None],
+            jnp.pad(row, (0, inner - row.shape[0]))[None],
+            jnp.pad(head_sum, (0, inner - head_sum.shape[0]))[None],
+        ],
+        0,
+    )
+    grad_wo, grad_wz, grad_wx, grad_side, small_sum = scatter_gradients(parts, small_sum, sizes)
+    grad_wzx = jnp.stack([grad_wz, grad_wx], 1)
+    grad_wbc = lax.all_gather(grad_side[:, :bc_cols], SEQ, axis=1, tiled=True)
+    grad_wdt = grad_side[:, bc_cols:side]
+    channel_own = lax.dynamic_slice_in_dim(small_sum[: taps + 2], place * cols, cols, 1)
+    row = small_sum[taps + 2]
+    gain_sum = row[:width]
+    taps_sum = row[width : width + taps * state2].reshape(taps, state2)
+    bias_sum = row[width + taps * state2 : width + (taps + 1) * state2]
+    head_sum = small_sum[taps + 3, : 3 * heads].reshape(3, heads)
     head_own = lax.dynamic_slice_in_dim(head_sum, place * heads_own, heads_own, 1)
     return (
         block_out,

time: 1200 us -> 1010 us (0.84)
  Pallas kernels: 0 us -> 462 us
  waiting for transfers between devices: 419 us -> 52.2 us
  local copies, waits for them, and re-layouts: 332 us -> 182 us
  blocking collectives: 130 us -> 31 us
  matrix products: 139 us -> 62 us
  other arithmetic: 117 us -> 170 us
  between operations: 16.3 us -> 2.52 us
    pallas_call x0 -> x12, Pallas kernels: none -> 462 us  [the longest x1 184 us: gather_weights(): pl.pallas_call(functools.partial(gather_kernel, sizes, chunks, kinds), ou...]
    unnamed x4 -> x0, waiting for transfers between devices: 238 us -> none
    all_gather x1 -> x0, waiting for transfers between devices: 116 us -> none  [body(): lax.all_gather(pack, ALL, axis=0, tiled=False)]
    concatenate x7 -> x2, local copies, waits for them, and re-layouts: 79.1 us -> 0.92 us  [the longest x1 0.78 us: body(): jnp.concatenate([grad_taps, grad_bias[None], grad_norm_gain[None], jnp.pa...]
    dot_general x27 -> x16, matrix products: 138 us -> 59.6 us  [dot16(): jnp.einsum(pattern, left.astype(BF16), right.astype(BF16), preferred_elem...]
    unnamed x293 -> x285, local copies, waits for them, and re-layouts: 84 us -> 24.2 us
    all_gather x3 -> x1, blocking collectives: 88.9 us -> 31 us  [body(): grad_wbc = lax.all_gather(grad_side[:, :bc_cols], SEQ, axis=1, tiled=True)]
    slice x12, local copies, waits for them, and re-layouts: 55.2 us -> 10.8 us  [the longest x1 2.3 us: body(): w_zx[:, 0]]
  transfers between devices with their start and end apart: 15 -> 18, of which waited for: 7 -> 4; matrix products, arithmetic and copies ran while one was open for 19% -> 32% of each run, Pallas kernels for 0% -> 28%
where the time goes in v2:
time: 1010 us; the launch traced here: 997 us
  Pallas kernels  462 us (46%)
  local copies, waits for them, and re-layouts  182 us (18%)
  other arithmetic  170 us (17%)
  matrix products  62 us (6%)
  waiting for transfers between devices  52.2 us (5%)
  starting transfers between devices  34.7 us (3%)
  blocking collectives  31 us (3%)
    pallas_call x1, Pallas kernels, gather_weights(): pl.pallas_call(functools.partial(gather_kernel, sizes, chunks, kinds), ou...  184 us
    pallas_call x1, Pallas kernels, scatter_gradients(): pl.pallas_call(functools.partial(scatter_kernel, sizes, chunks, kinds), o...  155 us
    dot_general x16, matrix products, dot16(): jnp.einsum(pattern, left.astype(BF16), right.astype(BF16), preferred_elem...  59.6 us
    pallas_call x4, Pallas kernels, gradient_pieces(): pl.pallas_call(kernel, grid=(hts // group,), out_shape=jax.ShapeDtypeStru...  45.5 us
    reshape x4, local copies, waits for them, and re-layouts, split(): return v.reshape(chunks, CHUNK, heads, head_width)  40.6 us
    ppermute x6, waiting for transfers between devices, from_later(): lax.ppermute(values, SEQ, [(i + distance, i) for i in range(size - distan...  40.3 us
    pallas_call x3, Pallas kernels, back_from_columns(): pl.pallas_call(kernel, grid=(hts // group,), out_shape=jax.ShapeDtypeStru...  38.9 us
    pallas_call x3, Pallas kernels, onto_columns(): pl.pallas_call(kernel, grid=(hts // group,), out_shape=jax.ShapeDtypeStru...  38.2 us
  transfers between devices with their start and end apart: 18, of which 4 were waited for; matrix products, arithmetic and copies ran while one was open for 32% of the time, Pallas kernels for 28%

profile of v2, /device:TPU:0, one launch (start us, length us, event | category | flops | bytes accessed | tf_op | source)
XLA Modules:
  0.0 996.6 jit_solution(13532155701367235270)
XLA Ops:
  16.6 184.3 %shard_map.271 = (bf16[4,4,2,384,128]{4,3,2,1,0:T(8,128)(2,1)}, bf16[4,4,2,384,384]{4,3,2,1,0:T(8,128)(2,1)}, bf16[4,4,2,384,384]{4,3,2,1,0:T(8,128)(2,1)}, bf16...) custom-call(bf16[384,128]{1,0:T(8,128)(2,1)} %pad.64.refs_0_, bf16[384,384]{1,0:T(8,128)(2,1)} %get-tuple-element.235.refs_1_, ...), custom_call_target="tpu_custom_call" | custom-call | tf_op jit(solution)/shard_map/pallas_call | solution.py:218
  203.2 12.7 %shard_map.275 = f32[512,3072]{1,0:T(8,128)} custom-call(bf16[512,1536]{1,0:T(8,128)(2,1)} %rows_ref.1, bf16[4,8,384,384]{3,2,1,0:T(8,128)(2,1)} %bitcast.409), custom_call_target="tpu_custom_call" | custom-call | flops 4831838208 | bytes 9437184 | tf_op jit(solution)/shard_map/pallas_call | solution.py:493
  251.4 12.8 %shard_map.272 = f32[528,3072]{1,0:T(8,128)} custom-call(bf16[528,1536]{1,0:T(8,128)(2,1)} %copy-done.17, bf16[4,8,384,384]{3,2,1,0:T(8,128)(2,1)} %bitcast.405), custom_call_target="tpu_custom_call" | custom-call | flops 4982833152 | bytes 9437184 | tf_op jit(solution)/shard_map/pallas_call | solution.py:493
  268.4 16.3 %fusion.4 = (f32[512,3072]{1,0:T(8,128)}, f32[512,3072]{1,0:T(8,128)}) fusion(f32[512]{0:T(512)S(1)} %copy-done.74, f32[528,3072]{1,0:T(8,128)} %shard_map.272, f32[3072]{0:T(1024)S(1)} %copy-done.63, f32[512]{0:T(512)S(1)} %copy-done.77, f32[3072]{0:T(1024)S(1)} %copy-done.65, f32[512]{0:T(512)S(1)} %get-tuple-element.218, f32[3072]{0:T(1024)S(1)} %copy-done.67, ...), kind=kLoop, calls=%fused_computation.37 | loop fusion | flops 23592960 | bytes 37816320 | tf_op jit(solution)/shard_map/jit(silu)/mul | solution.py:702
  284.7 10.0 %reshape.483 = f32[4,128,48,64]{3,2,1,0:T(8,128)} reshape(f32[512,3072]{1,0:T(8,128)} %get-tuple-element.170) | data formatting | bytes 12582912 | tf_op jit(solution)/shard_map/reshape | solution.py:713
  294.7 10.3 %copy.204 = f32[4,128,48,64]{1,3,2,0:T(8,128)} copy(f32[4,128,48,64]{3,2,1,0:T(8,128)} %reshape.483) | data formatting | bytes 12582912 | tf_op jit(solution)/shard_map/reshape | solution.py:713
  325.9 12.6 %shard_map.273 = f32[512,3072]{1,0:T(8,128)} custom-call(bf16[512,1536]{1,0:T(8,128)(2,1)} %slice.378.rows_ref, bf16[4,8,384,384]{3,2,1,0:T(8,128)(2,1)} %bitcast.407), custom_call_target="tpu_custom_call" | custom-call | flops 4831838208 | bytes 9437184 | tf_op jit(solution)/shard_map/pallas_call | solution.py:493
  357.8 11.9 %collective-permute-done.4 = f32[48]{0:T(128)S(1)} collective-permute-done((f32[48]{0:T(128)}, f32[48]{0:T(128)S(1)}, u32[]{:S(2)}, u32[]{:S(2)}) %collective-permute-start.4) | collective-permute-done | bytes 224 | tf_op jit(solution)/shard_map/ppermute | solution.py:596
  443.0 10.8 %reshape.481 = f32[512,3072]{1,0:T(8,128)} reshape(f32[4,128,48,64]{3,2,1,0:T(8,128)} %copy.241) | data formatting | bytes 12582912 | tf_op jit(solution)/shard_map/reshape | solution.py:743
  476.8 12.9 %shard_map.274 = f32[512,1536]{1,0:T(8,128)} custom-call(bf16[512,3072]{1,0:T(8,128)(2,1)} %get-tuple-element.176.value_ref, bf16[4,8,384,384]{3,2,1,0:T(8,128)(2,1)} %bitcast.410), custom_call_target="tpu_custom_call" | custom-call | flops 4831838208 | bytes 9437184 | tf_op jit(solution)/shard_map/pallas_call | solution.py:528
  489.6 12.9 %shard_map.276 = f32[512,1536]{1,0:T(8,128)} custom-call(bf16[512,3072]{1,0:T(8,128)(2,1)} %get-tuple-element.172.value_ref, bf16[4,8,384,384]{3,2,1,0:T(8,128)(2,1)} %bitcast.408), custom_call_target="tpu_custom_call" | custom-call | flops 4831838208 | bytes 9437184 | tf_op jit(solution)/shard_map/pallas_call | solution.py:528
  502.6 10.0 %reshape.484 = f32[4,128,48,64]{3,2,1,0:T(8,128)} reshape(f32[512,3072]{1,0:T(8,128)} %get-tuple-element.159) | data formatting | bytes 12582912 | tf_op jit(solution)/shard_map/reshape | solution.py:713
  512.6 10.3 %copy.215 = f32[4,128,48,64]{1,3,2,0:T(8,128)} copy(f32[4,128,48,64]{3,2,1,0:T(8,128)} %reshape.484) | data formatting | bytes 12582912 | tf_op jit(solution)/shard_map/reshape | solution.py:713
  561.6 17.4 %collective-permute-done.8 = bf16[48,64,128]{2,1,0:T(8,128)(2,1)S(1)} collective-permute-done((bf16[48,64,128]{2,1,0:T(8,128)(2,1)}, bf16[48,64,128]{2,1,0:T(8,128)(2,1)S(1)}, u32[]{:S(2)}, u32[]{:S(2)}) %collective-permute-start.8) | collective-permute-done | bytes 786464 | tf_op jit(solution)/shard_map/ppermute | solution.py:600
  587.0 13.8 %collective-permute-done.10 = bf16[48,64,128]{2,1,0:T(8,128)(2,1)S(1)} collective-permute-done((bf16[48,64,128]{2,1,0:T(8,128)(2,1)S(1)}, bf16[48,64,128]{2,1,0:T(8,128)(2,1)S(1)}, u32[]{:S(2)}, u32[]{:S(2)}) %collective-permute-start.10) | collective-permute-done | bytes 786464 | tf_op jit(solution)/shard_map/ppermute | solution.py:600
  606.9 18.4 %multiply_reduce_fusion.8 = (f32[4,128,48]{1,2,0:T(8,128)}, f32[4,128,48]{1,2,0:T(8,128)}, f32[4,128,48]{1,2,0:T(8,128)}, f32[4,128,48,64]{1,3,2,0:T(8,128)}) fusion(bf16[4,128,48,64]{1,3,2,0:T(8,128)(2,1)S(1)} %copy-done.8, f32[4,128,48,64]{1,3,2,0:T(8,128)} %copy.204, f32[4,128,48]{1,2,0:T(8,128)S(1)} %copy-done.48, f32[4,48,64,128]{3,2,1,0:T(8,128)} %fusion.78, ...), kind=kOutput, calls=%fused_computation.24 | convolution fusion | flops 441901056 | bytes 50954240 | tf_op jit(solution)/shard_map/cms,chps->cmhp/dot_general | solution.py:25
  635.3 10.6 %reshape.482 = f32[512,3072]{1,0:T(8,128)} reshape(f32[4,128,48,64]{3,2,1,0:T(8,128)} %copy.242) | data formatting | bytes 12582912 | tf_op jit(solution)/shard_map/reshape | solution.py:775
  645.9 19.7 %multiply_reduce_fusion.3 = (f32[3072]{0:T(1024)}, f32[3072]{0:T(1024)}, f32[3072]{0:T(1024)}, f32[3072]{0:T(1024)}, f32[3072]{0:T(1024)}, /*index=5*/f32[512,3072]{1,0:T(8,128)}) fusion(f32[528,3072]{1,0:T(8,128)} %shard_map.272, f32[512]{0:T(512)S(1)} %copy-done.73, f32[512]{0:T(512)S(1)} %copy-done.78, f32[512]{0:T(512)S(1)} %copy-done.75, ...), kind=kLoop, calls=%fused_computation.18 | loop fusion | flops 34587648 | bytes 50411520 | tf_op jit(solution)/shard_map/reduce_sum | solution.py:585
  678.7 13.1 %shard_map.277 = f32[528,1536]{1,0:T(8,128)} custom-call(bf16[528,3072]{1,0:T(8,128)(2,1)} %add_convert_fusion.value_ref, bf16[4,8,384,384]{3,2,1,0:T(8,128)(2,1)} %bitcast.406), custom_call_target="tpu_custom_call" | custom-call | flops 4982833152 | bytes 9437184 | tf_op jit(solution)/shard_map/pallas_call | solution.py:528
  732.6 11.8 %shard_map.278 = bf16[2,8,384,384]{3,2,1,0:T(8,128)(2,1)} custom-call(bf16[2,384,1024]{2,1,0:T(8,128)(2,1)} %dynamic-slice_bitcast_fusion.left_ref, bf16[1024,3072]{1,0:T(8,128)(2,1)} %bitcast.340), custom_call_target="tpu_custom_call" | custom-call | flops 4831838208 | bytes 6291456 | tf_op jit(solution)/shard_map/pallas_call | solution.py:556
  751.7 12.6 %shard_map.279 = bf16[2,8,384,384]{3,2,1,0:T(8,128)(2,1)} custom-call(bf16[2,384,1056]{2,1,0:T(8,128)(2,1)} %bitcast.356, bf16[1056,3072]{1,0:T(8,128)(2,1)} %bitcast.339), custom_call_target="tpu_custom_call" | custom-call | flops 4982833152 | bytes 6488064 | tf_op jit(solution)/shard_map/pallas_call | solution.py:556
  783.6 12.5 %shard_map.280 = bf16[2,8,384,384]{3,2,1,0:T(8,128)(2,1)} custom-call(bf16[2,384,1056]{2,1,0:T(8,128)(2,1)} %bitcast.358, bf16[1056,3072]{1,0:T(8,128)(2,1)} %bitcast.338), custom_call_target="tpu_custom_call" | custom-call | flops 4982833152 | bytes 6488064 | tf_op jit(solution)/shard_map/pallas_call | solution.py:556
  796.1 155.0 %shard_map.282 = (f32[384,384]{1,0:T(8,128)}, f32[384,384]{1,0:T(8,128)}, f32[384,384]{1,0:T(8,128)}, f32[384,128]{1,0:T(8,128)}, f32[8,3072]{1,0:T(8,128)}) custom-call(bf16[2,4,2,384,384]{4,3,2,1,0:T(8,128)(2,1)} %bitcast.342, bf16[2,4,2,384,384]{4,3,2,1,0:T(8,128)(2,1)} %bitcast.343, bf16[2,4,2,384,384]{4,3,2,1,0:T(8,128)(2,1)} %bitcast.344, ...), custom_call_target="tpu_custom_call" | custom-call | tf_op jit(solution)/shard_map/pallas_call | solution.py:451
  958.9 31.0 %all_gather.3 = f32[384,256]{0,1:T(8,128)S(1)} all-gather(f32[384,32]{0,1:T(8,128)S(1)} %copy.231), channel_id=1, replica_groups=mesh['dp'=4,'head'=4,'tensor'=2] {'head','tensor'}, dimensions={1}, use_global_device_ids=true | all-gather | bytes 442368 | tf_op jit(solution)/shard_map/all_gather | solution.py:865
  (485 shorter events, 350.2 us)
Async XLA Ops:
  2.2 235.2 %collective-permute-start = (bf16[16,1536]{1,0:T(8,128)(2,1)}, bf16[16,1536]{1,0:T(8,128)(2,1)S(1)}, u32[]{:S(2)}, u32[]{:S(2)}) collective-permute-start(bf16[16,1536]{1,0:T(8,128)(2,1)} %slice.295), channel_id=1, source_target_pairs={{0,1},{1,2},{2,3},{3,4},{4,5},{5,6},{6,7},{8,9},{9,10},{10,11},{11... | collective-permute-start | bytes 147464 | tf_op jit(solution)/shard_map/ppermute | solution.py:596
  7.1 363.9 %collective-permute-start.12 = (bf16[512,1536]{1,0:T(8,128)(2,1)}, bf16[512,1536]{1,0:T(8,128)(2,1)}, u32[]{:S(2)}, u32[]{:S(2)}) collective-permute-start(bf16[512,1536]{1,0:T(8,128)(2,1)} %rows_ref.1), channel_id=1, source_target_pairs={{0,8},{8,0},{16,24},{24,16},{1,9},{9,1},{17,25},{25,17},{2,10},{10... | collective-permute-start | bytes 4718600 | tf_op jit(solution)/shard_map/ppermute | solution.py:824
  8.6 259.7 %copy-start.72 = (f32[512]{0:T(512)}, f32[512]{0:T(512)S(1)}, u32[]{:S(2)}) copy-start(f32[512]{0:T(512)S(1)} %get-tuple-element.218) | copy-start | bytes 6148
  245.9 108.7 %collective-permute-start.2 = (f32[48]{0:T(128)}, f32[48]{0:T(128)}, u32[]{:S(2)}, u32[]{:S(2)}) collective-permute-start(f32[48]{0:T(128)} %multiply_multiply_fusion.9), channel_id=1, source_target_pairs={{0,1},{1,2},{2,3},{3,4},{4,5},{5,6},{6,7},{8,9},{9,10},{10,11},{11... | collective-permute-start | bytes 584 | tf_op jit(solution)/shard_map/ppermute | solution.py:596
  249.4 107.0 %collective-permute-start.7 = (f32[48]{0:T(128)}, f32[48]{0:T(128)}, u32[]{:S(2)}, u32[]{:S(2)}) collective-permute-start(f32[48]{0:T(128)} %multiply_multiply_fusion.9), channel_id=1, source_target_pairs={{1,0},{2,1},{3,2},{4,3},{5,4},{6,5},{7,6},{9,8},{10,9},{11,10},{12... | collective-permute-start | bytes 584 | tf_op jit(solution)/shard_map/ppermute | solution.py:600
  250.9 140.4 %collective-permute-start.14 = (bf16[528,1536]{1,0:T(8,128)(2,1)S(1)}, bf16[528,1536]{1,0:T(8,128)(2,1)}, u32[]{:S(2)}, u32[]{:S(2)}) collective-permute-start(bf16[528,1536]{1,0:T(8,128)(2,1)S(1)} %multiply_convert_fusion.7.rows_ref), channel_id=1, source_target_pairs={{0,8},{8,0},{16,24},{24,16},{1,9},{9,1},{17,25},{25,17},{2,10},{10... | collective-permute-start | bytes 4866056 | tf_op jit(solution)/shard_map/ppermute | solution.py:824
  268.4 70.0 %copy-start.37 = (bf16[512,128]{1,0:T(8,128)(2,1)}, bf16[512,128]{1,0:T(8,128)(2,1)S(1)}, u32[]{:S(2)}) copy-start(bf16[512,128]{1,0:T(8,128)(2,1)S(1)} %get-tuple-element.198) | copy-start | bytes 393220
  319.9 28.6 %collective-permute-start.1 = (bf16[48,64,128]{2,1,0:T(8,128)(2,1)S(1)}, bf16[48,64,128]{2,1,0:T(8,128)(2,1)}, u32[]{:S(2)}, u32[]{:S(2)}) collective-permute-start(bf16[48,64,128]{2,1,0:T(8,128)(2,1)S(1)} %fusion.15), channel_id=1, source_target_pairs={{0,1},{1,2},{2,3},{3,4},{4,5},{5,6},{6,7},{8,9},{9,10},{10,11},{11... | collective-permute-start | bytes 2359304 | tf_op jit(solution)/shard_map/ppermute | solution.py:596
  346.9 28.9 %copy-start.95 = (f32[512]{0:T(512)}, f32[512]{0:T(512)S(1)}, u32[]{:S(2)}) copy-start(f32[512]{0:T(512)S(1)} %slice.344) | copy-start | bytes 6148
  348.5 34.8 %collective-permute-start.3 = (bf16[48,64,128]{2,1,0:T(8,128)(2,1)}, bf16[48,64,128]{2,1,0:T(8,128)(2,1)S(1)}, u32[]{:S(2)}, u32[]{:S(2)}) collective-permute-start(bf16[48,64,128]{2,1,0:T(8,128)(2,1)} %collective-permute-done.1), channel_id=1, source_target_pairs={{0,1},{1,2},{2,3},{3,4},{4,5},{5,6},{6,7},{8,9},{9,10},{10,11},{11... | collective-permute-start | bytes 2359304 | tf_op jit(solution)/shard_map/ppermute | solution.py:596
  354.6 15.1 %collective-permute-start.4 = (f32[48]{0:T(128)}, f32[48]{0:T(128)S(1)}, u32[]{:S(2)}, u32[]{:S(2)}) collective-permute-start(f32[48]{0:T(128)} %collective-permute-done.2), channel_id=1, source_target_pairs={{0,1},{1,2},{2,3},{3,4},{4,5},{5,6},{6,7},{8,9},{9,10},{10,11},{11... | collective-permute-start | bytes 584 | tf_op jit(solution)/shard_map/ppermute | solution.py:596
  356.5 13.9 %collective-permute-start.9 = (f32[48]{0:T(128)}, f32[48]{0:T(128)S(1)}, u32[]{:S(2)}, u32[]{:S(2)}) collective-permute-start(f32[48]{0:T(128)} %collective-permute-done.7), channel_id=1, source_target_pairs={{1,0},{2,1},{3,2},{4,3},{5,4},{6,5},{7,6},{9,8},{10,9},{11,10},{12... | collective-permute-start | bytes 584 | tf_op jit(solution)/shard_map/ppermute | solution.py:600
  385.9 26.2 %collective-permute-start.5 = (bf16[48,64,128]{2,1,0:T(8,128)(2,1)}, bf16[48,64,128]{2,1,0:T(8,128)(2,1)}, u32[]{:S(2)}, u32[]{:S(2)}) collective-permute-start(bf16[48,64,128]{2,1,0:T(8,128)(2,1)} %fusion.16), channel_id=1, source_target_pairs={{0,2},{1,3},{2,4},{3,5},{4,6},{5,7},{8,10},{9,11},{10,12},{11,13},... | collective-permute-start | bytes 2359304 | tf_op jit(solution)/shard_map/ppermute | solution.py:596
  489.6 234.7 %collective-permute-start.13 = (bf16[512,3072]{1,0:T(8,128)(2,1)}, bf16[512,3072]{1,0:T(8,128)(2,1)}, u32[]{:S(2)}, u32[]{:S(2)}) collective-permute-start(bf16[512,3072]{1,0:T(8,128)(2,1)} %get-tuple-element.176.value_ref), channel_id=1, source_target_pairs={{0,8},{8,0},{16,24},{24,16},{1,9},{9,1},{17,25},{25,17},{2,10},{10... | collective-permute-start | bytes 9437192 | tf_op jit(solution)/shard_map/ppermute | solution.py:824
  531.1 28.2 %copy-start.9 = (bf16[4,128,48,64]{1,3,2,0:T(8,128)(2,1)}, bf16[4,128,48,64]{1,3,2,0:T(8,128)(2,1)S(1)}, u32[]{:S(2)}) copy-start(bf16[4,128,48,64]{1,3,2,0:T(8,128)(2,1)S(1)} %get-tuple-element.182) | copy-start | bytes 9437188
  535.6 22.1 %collective-permute-start.6 = (bf16[48,64,128]{2,1,0:T(8,128)(2,1)}, bf16[48,64,128]{2,1,0:T(8,128)(2,1)}, u32[]{:S(2)}, u32[]{:S(2)}) collective-permute-start(bf16[48,64,128]{2,1,0:T(8,128)(2,1)} %fusion.13), channel_id=1, source_target_pairs={{1,0},{2,1},{3,2},{4,3},{5,4},{6,5},{7,6},{9,8},{10,9},{11,10},{12... | collective-permute-start | bytes 2359304 | tf_op jit(solution)/shard_map/ppermute | solution.py:600
  540.4 204.0 %collective-permute-start.15 = (bf16[528,3072]{1,0:T(8,128)(2,1)}, bf16[528,3072]{1,0:T(8,128)(2,1)}, u32[]{:S(2)}, u32[]{:S(2)}) collective-permute-start(bf16[528,3072]{1,0:T(8,128)(2,1)} %get-tuple-element.186), channel_id=1, source_target_pairs={{0,8},{8,0},{16,24},{24,16},{1,9},{9,1},{17,25},{25,17},{2,10},{10... | collective-permute-start | bytes 9732104 | tf_op jit(solution)/shard_map/ppermute | solution.py:824
  557.8 21.2 %collective-permute-start.8 = (bf16[48,64,128]{2,1,0:T(8,128)(2,1)}, bf16[48,64,128]{2,1,0:T(8,128)(2,1)S(1)}, u32[]{:S(2)}, u32[]{:S(2)}) collective-permute-start(bf16[48,64,128]{2,1,0:T(8,128)(2,1)} %collective-permute-done.6), channel_id=1, source_target_pairs={{1,0},{2,1},{3,2},{4,3},{5,4},{6,5},{7,6},{9,8},{10,9},{11,10},{12... | collective-permute-start | bytes 2359304 | tf_op jit(solution)/shard_map/ppermute | solution.py:600
  580.6 20.2 %collective-permute-start.10 = (bf16[48,64,128]{2,1,0:T(8,128)(2,1)S(1)}, bf16[48,64,128]{2,1,0:T(8,128)(2,1)S(1)}, u32[]{:S(2)}, u32[]{:S(2)}) collective-permute-start(bf16[48,64,128]{2,1,0:T(8,128)(2,1)S(1)} %fusion.17), channel_id=1, source_target_pairs={{2,0},{3,1},{4,2},{5,3},{6,4},{7,5},{10,8},{11,9},{12,10},{13,11},... | collective-permute-start | bytes 2359304 | tf_op jit(solution)/shard_map/ppermute | solution.py:600
  691.8 84.5 %collective-permute-start.16 = (bf16[528,3072]{1,0:T(8,128)(2,1)}, bf16[528,3072]{1,0:T(8,128)(2,1)}, u32[]{:S(2)}, u32[]{:S(2)}) collective-permute-start(bf16[528,3072]{1,0:T(8,128)(2,1)} %add_convert_fusion.value_ref), channel_id=1, source_target_pairs={{0,8},{8,0},{16,24},{24,16},{1,9},{9,1},{17,25},{25,17},{2,10},{10... | collective-permute-start | bytes 9732104 | tf_op jit(solution)/shard_map/ppermute | solution.py:824
  706.7 8.7 collective-permute-start.11
  709.8 54.5 %collective-permute-start.17 = (bf16[528,1024]{1,0:T(8,128)(2,1)}, bf16[528,1024]{1,0:T(8,128)(2,1)}, u32[]{:S(2)}, u32[]{:S(2)}) collective-permute-start(bf16[528,1024]{1,0:T(8,128)(2,1)} %copy.227), channel_id=1, source_target_pairs={{0,8},{8,0},{16,24},{24,16},{1,9},{9,1},{17,25},{25,17},{2,10},{10... | collective-permute-start | bytes 3244040 | tf_op jit(solution)/shard_map/ppermute | solution.py:824
  955.4 40.2 %copy-start.53 = (f32[384,384]{1,0:T(8,128)S(1)}, f32[384,384]{1,0:T(8,128)}, u32[]{:S(2)}) copy-start(f32[384,384]{1,0:T(8,128)} %get-tuple-element.267) | copy-start | bytes 1769476
  955.4 41.0 %copy-start.1 = (bf16[384,256]{1,0:T(8,128)(2,1)S(1)}, bf16[384,256]{1,0:T(8,128)(2,1)}, u32[]{:S(2)}) copy-start(bf16[384,256]{1,0:T(8,128)(2,1)} %param.22) | copy-start | bytes 589828
  (133 other events, 1153.5 us)

commit v3 on v2

--- a/solution.py
+++ b/solution.py
@@ -200,17 +200,19 @@
                 one.wait_send()
 
 
-def row_chunks(rows, kinds, pieces):
+def row_chunks(rows, first, kinds, pieces):
     step = rows // pieces
     return [
-        (kind, piece * step, step, piece % 2 == 0) for kind in range(kinds) for piece in range(pieces)
+        (kind, piece * step, step, piece % 2 == 1)
+        for kind in range(first, kinds)
+        for piece in range(pieces)
     ]
 
 
 def gather_weights(parts, small, sizes):
     xs, hs, ts = sizes
     kinds = len(parts)
-    chunks = row_chunks(parts[0].shape[0], kinds, 4)
+    chunks = [(0, 0, parts[0].shape[0], True)] + row_chunks(parts[1].shape[0], 1, kinds, 4)
     slots = hs - 1 + max(xs, ts) + max(xs, xs * ts) + xs
     full = [jax.ShapeDtypeStruct((2 * xs, hs, ts) + part.shape, part.dtype) for part in parts]
     full.append(jax.ShapeDtypeStruct((hs, ts) + small.shape, small.dtype))
@@ -230,6 +232,7 @@
         compiler_params=pltpu.CompilerParams(
             collective_id=0, has_side_effects=True, vmem_limit_bytes=VMEM_BYTES
         ),
+        cost_estimate=busy(60),
     )(*parts, small)
 
 
@@ -239,7 +242,7 @@
     outs, small_out = refs[kinds + 1 : 2 * kinds + 1], refs[2 * kinds + 1]
     rest = refs[2 * kinds + 2 :]
     bufs, rest = rest[: 4 * len(chunks)], rest[4 * len(chunks) :]
-    small_acc, small_in, send, recv, small_send, small_recv, own_sem = rest
+    small_acc, small_in, send, recv, small_send, small_recv, own_sem, side_send, side_recv = rest
     x, core, head, tensor = coordinates()
     dp = 2 * x + core
     total = len(chunks)
@@ -347,7 +350,29 @@
             value = held[where].astype(F32)
             for step in range(third.shape[0]):
                 value = value + third[step].astype(F32)
-            outs[kind][start : start + length, :] = value
+            if kind == 0:
+                outs[kind][head, tensor] = value
+            else:
+                outs[kind][start : start + length, :] = value
+
+    def side_copy(view, slot, device):
+        return pltpu.make_async_remote_copy(
+            src_ref=view,
+            dst_ref=view,
+            send_sem=side_send.at[slot],
+            recv_sem=side_recv.at[slot],
+            device_id=device,
+            device_id_type=MESH,
+        )
+
+    side_tensor = [
+        side_copy(outs[0].at[head, tensor], step - 1, {"tensor": lax.rem(tensor + step, ts)})
+        for step in range(1, ts)
+    ]
+    side_head = [
+        side_copy(outs[0].at[head], ts + step - 2, {"head": lax.rem(head + step, hs)})
+        for step in range(1, hs)
+    ]
 
     small_slots = [1, xs - 1, ts - 1, hs - 1]
     small_base = [0, 1, xs, xs + ts - 1]
@@ -413,6 +438,14 @@
                 if number < 2:
                     for one in stage(index, number + 1):
                         one.start()
+        if tick == 4:
+            for one in side_tensor:
+                one.start()
+        if tick == 6:
+            for one in side_tensor:
+                one.wait_recv()
+            for one in side_head:
+                one.start()
         if tick < 4:
             for one in small_stage(tick):
                 one.wait_recv()
@@ -420,6 +453,10 @@
             if tick < 3:
                 for one in small_stage(tick + 1):
                     one.start()
+    for one in side_head:
+        one.wait_recv()
+    for one in side_tensor + side_head:
+        one.wait_send()
     for number in range(4):
         for one in small_stage(number):
             one.wait_send()
@@ -432,7 +469,7 @@
 def scatter_gradients(parts, small, sizes):
     xs, hs, ts = sizes
     kinds = len(parts)
-    chunks = row_chunks(parts[0].shape[3], kinds, 4)
+    chunks = [(0, 0, parts[0].shape[3], True)] + row_chunks(parts[1].shape[3], 1, kinds, 4)
     scratch = []
     for kind, _, length, x_first in chunks:
         cols = parts[kind].shape[4]
@@ -450,7 +487,8 @@
     whole = pl.BlockSpec(memory_space=pltpu.VMEM)
     return pl.pallas_call(
         functools.partial(scatter_kernel, sizes, chunks, kinds),
-        out_shape=[jax.ShapeDtypeStruct(part.shape[3:], F32) for part in parts]
+        out_shape=[jax.ShapeDtypeStruct((hs, ts) + parts[0].shape[3:], F32)]
+        + [jax.ShapeDtypeStruct(part.shape[3:], F32) for part in parts[1:]]
         + [jax.ShapeDtypeStruct(small.shape, F32)],
         in_specs=[anywhere] * kinds + [whole],
         out_specs=[whole] * (kinds + 1),
@@ -463,10 +501,13 @@
             pltpu.SemaphoreType.DMA((small_slots,)),
             pltpu.SemaphoreType.DMA((small_slots,)),
             pltpu.SemaphoreType.DMA((len(chunks),)),
+            pltpu.SemaphoreType.DMA((hs + ts,)),
+            pltpu.SemaphoreType.DMA((hs + ts,)),
         ],
         compiler_params=pltpu.CompilerParams(
             collective_id=1, has_side_effects=True, vmem_limit_bytes=VMEM_BYTES
         ),
+        cost_estimate=busy(60),
     )(*parts, small)
 
 
@@ -474,99 +515,465 @@
     return 1 if cols % 128 == 0 else 128 // cols if 128 % cols == 0 else 2
 
 
+def busy(microseconds):
+    return pl.CostEstimate(flops=microseconds * 900_000_000, bytes_accessed=0, transcendentals=0)
+
+
 def local_params():
     return pltpu.CompilerParams(vmem_limit_bytes=VMEM_BYTES)
 
 
-def onto_columns(rows, pieces):
-    dps, hts, depth, cols = pieces.shape
+def gradient_pieces(lefts, values, hts):
+    kinds = len(lefts)
+    left, value = lefts[0], values[0]
+    xs, depth, count = left.shape
+    cols = value.shape[1] // hts
     group = group_of(cols)
-    count = rows.shape[0]
-
-    def kernel(rows_ref, piece_ref, out_ref):
-        for one in range(group):
-            weights = piece_ref[:, one].reshape(dps * depth, cols)
-            out_ref[:, one * cols : (one + 1) * cols] = jnp.dot(
-                rows_ref[...], weights, preferred_element_type=F32
-            )
+
+    def kernel(*refs):
+        out_ref = refs[-1]
+        for kind in range(kinds):
+            left_ref, value_ref = refs[kind], refs[kinds + kind]
+            for at in range(xs):
+                for one in range(group):
+                    out_ref[at, one, kind] = jnp.dot(
+                        left_ref[at],
+                        value_ref[:, one * cols : (one + 1) * cols],
+                        preferred_element_type=F32,
+                    ).astype(BF16)
 
     return pl.pallas_call(
         kernel,
         grid=(hts // group,),
-        out_shape=jax.ShapeDtypeStruct((count, hts * cols), F32),
-        in_specs=[
-            pl.BlockSpec(rows.shape, lambda j: (0, 0)),
-            pl.BlockSpec((dps, group, depth, cols), lambda j: (0, j, 0, 0)),
-        ],
-        out_specs=pl.BlockSpec((count, group * cols), lambda j: (0, j)),
+        out_shape=jax.ShapeDtypeStruct((xs, hts, kinds, depth, cols), BF16),
+        in_specs=[pl.BlockSpec(left.shape, lambda j: (0, 0, 0))] * kinds
+        + [pl.BlockSpec((count, group * cols), lambda j: (0, j))] * kinds,
+        out_specs=pl.BlockSpec((xs, group, kinds, depth, cols), lambda j: (0, j, 0, 0, 0)),
         compiler_params=local_params(),
-        cost_estimate=pl.CostEstimate(
-            flops=2 * count * pieces.size, bytes_accessed=2 * pieces.size, transcendentals=0
-        ),
-    )(rows, pieces)
-
-
-def back_from_columns(values, pieces):
-    dps, hts, depth, cols = pieces.shape
-    group = group_of(cols)
-    count = values.shape[0]
-
-    def kernel(value_ref, piece_ref, out_ref):
+        cost_estimate=busy(12 * kinds),
+    )(*lefts, *values)
+
+
+def silu_of(v):
+    return v * jax.nn.sigmoid(v)
+
+
+def dot_nt(left, right):
+    return lax.dot_general(left, right, (((1,), (1,)), ((), ())), preferred_element_type=F32)
+
+
+def dot_tn(left, right):
+    return lax.dot_general(left, right, (((0,), (0,)), ((), ())), preferred_element_type=F32)
+
+
+def dot_nn(left, right):
+    return jnp.dot(left, right, preferred_element_type=F32)
+
+
+def thirds(v):
+    high = rounded(v)
+    rest = v - high.astype(F32)
+    middle = rounded(rest)
+    return jnp.concatenate([high, middle, rounded(rest - middle.astype(F32))], 1)
+
+
+def conv_pre(ext_ref, taps_ref, same_ref, own, width):
+    total = taps_ref[width : width + 1] + taps_ref[width - 1 : width] * ext_ref[HALO:]
+    for back in range(1, width):
+        total = total + (
+            taps_ref[width - 1 - back : width - back]
+            * ext_ref[HALO - back : HALO - back + own]
+            * same_ref[:, back - 1 : back]
+        )
+    return total
+
+
+def lane_masks():
+    lane = lax.broadcasted_iota(jnp.int32, (1, 128), 1)
+    first = (lane < 64).astype(F32)
+    return first, 1.0 - first
+
+
+def two_apart(pair, masks):
+    return jnp.concatenate([pair * masks[0].astype(BF16), pair * masks[1].astype(BF16)], 0)
+
+
+def decay_pair(cum_ref, cumt_ref, bias, rows, pair):
+    parts = []
+    for head in (2 * pair, 2 * pair + 1):
+        spread = cum_ref[0, rows, head : head + 1] - cumt_ref[0, head : head + 1, rows] + bias
+        parts.append(jnp.exp(spread))
+    return parts
+
+
+class Scan:
+    def __init__(self, own, sizes, rows, cols, heads_own, taps):
+        self.own, self.ext, self.taps = own, own + HALO, taps
+        self.dps, self.hts = 2 * sizes[0], sizes[1] * sizes[2]
+        self.rows, self.cols = rows, cols
+        self.group = group_of(cols)
+        self.wide = self.group * cols
+        self.heads = self.group * heads_own
+        self.groups = self.hts // self.group
+        self.chunks = own // CHUNK
+        self.width = self.dps * rows
+        self.inner = self.hts * cols
+        self.pairs = self.wide // 128
+
+    def call(self, kernel, ins, outs, scratch=()):
+        arrays = [array for array, _ in ins]
+        return pl.pallas_call(
+            kernel,
+            grid=(self.groups,),
+            out_shape=[shape for shape, _ in outs],
+            in_specs=[spec for _, spec in ins],
+            out_specs=[spec for _, spec in outs],
+            scratch_shapes=list(scratch),
+            compiler_params=local_params(),
+            cost_estimate=busy(22),
+        )(*arrays)
+
+    def full(self, array):
+        return (array, pl.BlockSpec(array.shape, lambda j: (0,) * array.ndim))
+
+    def pieces(self, array, kind=None):
+        if kind is None:
+            block = (self.dps, self.group, self.rows, self.cols)
+            return (array, pl.BlockSpec(block, lambda j: (0, j, 0, 0)))
+        block = (self.dps, self.group, None, self.rows, self.cols)
+        return (array, pl.BlockSpec(block, lambda j: (0, j, kind, 0, 0)))
+
+    def lanes(self, array):
+        lead = array.shape[:-1]
+        return (array, pl.BlockSpec(lead + (self.wide,), lambda j: (0,) * len(lead) + (j,)))
+
+    def states(self, array):
+        lead = array.shape[:-2]
+        block = lead + (self.wide, array.shape[-1])
+        return (array, pl.BlockSpec(block, lambda j: (0,) * len(lead) + (j, 0)))
+
+    def grouped(self, array):
+        block = (1,) + array.shape[1:]
+        return (array, pl.BlockSpec(block, lambda j: (j,) + (0,) * (array.ndim - 1)))
+
+    def project(self, rows_ref, piece_ref, out_ref):
+        for one in range(self.group):
+            weights = piece_ref[:, one].reshape(self.width, self.cols)
+            out_ref[:, one * self.cols : (one + 1) * self.cols] = dot_nn(rows_ref, weights)
+
+    def project_back(self, value_ref, piece_ref, out_ref):
         @pl.when(pl.program_id(0) == 0)
         def _():
             out_ref[...] = jnp.zeros_like(out_ref)
 
-        for one in range(group):
-            weights = piece_ref[:, one].reshape(dps * depth, cols)
-            out_ref[...] += lax.dot_general(
-                value_ref[:, one * cols : (one + 1) * cols],
-                weights,
-                (((1,), (1,)), ((), ())),
-                preferred_element_type=F32,
+        for one in range(self.group):
+            weights = piece_ref[:, one].reshape(self.width, self.cols)
+            out_ref[...] += dot_nt(value_ref[:, one * self.cols : (one + 1) * self.cols], weights)
+
+    def chunk_rows(self, c):
+        return slice(c * CHUNK, (c + 1) * CHUNK)
+
+    def lane_sums(self, v):
+        total = v[:, :128]
+        for pair in range(1, self.pairs):
+            total = total + v[:, pair * 128 : (pair + 1) * 128]
+        return total
+
+    def head_sums(self, v, ones_ref):
+        high = v.astype(BF16)
+        low = (v - high.astype(F32)).astype(BF16)
+        return dot_nn(high, ones_ref[...]) + dot_nn(low, ones_ref[...])
+
+    def s1(self, normed, w_x, conv_rows, same, dt3, tail3, widen, cum_g, cumt_g, coupling, bias, bc, keep_cols):
+        own, state = self.own, bc.shape[1] // 2
+
+        def kernel(
+            normed_ref, w_ref, conv_ref, same_ref, dt_ref, tail_ref, widen_ref, cum_ref, cumt_ref,
+            coupling_ref, bias_ref, bc_ref, keep_ref, ext_ref, x_ref, within_ref, added_ref, local_ref, xd_ref, xt_ref,
+        ):
+            self.project(normed_ref[...], w_ref, ext_ref)
+            x = silu_of(conv_pre(ext_ref, conv_ref, same_ref, own, self.taps))
+            x_ref[...] = x
+            xd = x * dot_nn(dt_ref[...], widen_ref[...])
+            xd_ref[...] = xd.astype(BF16)
+            xt_ref[...] = (xd * dot_nn(tail_ref[...], widen_ref[...])).astype(BF16)
+            masks = lane_masks()
+            held = None
+            for c in range(self.chunks):
+                rows = self.chunk_rows(c)
+                for pair in range(self.pairs):
+                    lanes = slice(pair * 128, (pair + 1) * 128)
+                    first, second = decay_pair(cum_ref, cumt_ref, bias_ref[c], rows, pair)
+                    mix = coupling_ref[c]
+                    kernel16 = jnp.concatenate([(first * mix).astype(BF16), (second * mix).astype(BF16)], 1)
+                    within_ref[rows, lanes] = dot_nn(kernel16, two_apart(xd_ref[rows, lanes], masks))
+                added = dot_tn(xt_ref[rows], bc_ref[rows, :state])
+                added_ref[c] = added
+                held = added if held is None else added + keep_ref[:, c : c + 1] * held
+            local_ref[...] = held.astype(BF16)
+
+        f = jax.ShapeDtypeStruct
+        return self.call(
+            kernel,
+            [
+                self.full(normed), self.pieces(w_x), self.lanes(conv_rows), self.full(same), self.full(dt3),
+                self.full(tail3), self.lanes(widen), self.grouped(cum_g), self.grouped(cumt_g),
+                self.full(coupling), self.full(bias), self.full(bc), self.states(keep_cols),
+            ],
+            [
+                self.lanes(f((self.ext, self.inner), F32)), self.lanes(f((own, self.inner), F32)),
+                self.lanes(f((own, self.inner), F32)), self.states(f((self.chunks, self.inner, state), F32)),
+                self.states(f((self.inner, state), BF16)),
+            ],
+            [pltpu.VMEM((own, self.wide), BF16), pltpu.VMEM((own, self.wide), BF16)],
+        )
+
+    def s2(self, normed_own, w_zo, within, x, skip_rows, entry3, widen, bc, entering, added, keep_cols):
+        own, state = self.own, bc.shape[1] // 2
+
+        def kernel(
+            normed_ref, w_ref, within_ref, x_ref, skip_ref, entry_ref, widen_ref, bc_ref, entering_ref,
+            added_ref, keep_ref, z_ref, y_ref, states_ref, squares_ref,
+        ):
+            self.project(normed_ref[...], w_ref, z_ref)
+            entry = dot_nn(entry_ref[...], widen_ref[...])
+            held = entering_ref[...]
+            for c in range(self.chunks):
+                rows = self.chunk_rows(c)
+                held16 = held.astype(BF16)
+                states_ref[c] = held16
+                carried = dot_nt(bc_ref[rows, state:], held16)
+                y_ref[rows] = within_ref[rows] + carried * entry[rows] + skip_ref[...] * x_ref[rows]
+                if c + 1 < self.chunks:
+                    held = added_ref[c] + keep_ref[:, c : c + 1] * held
+            gated = y_ref[...] * silu_of(z_ref[...])
+            squares = self.lane_sums(gated * gated)
+
+            @pl.when(pl.program_id(0) == 0)
+            def _():
+                squares_ref[...] = squares
+
+            @pl.when(pl.program_id(0) > 0)
+            def _():
+                squares_ref[...] += squares
+
+        f = jax.ShapeDtypeStruct
+        return self.call(
+            kernel,
+            [
+                self.full(normed_own), self.pieces(w_zo, 0), self.lanes(within), self.lanes(x), self.lanes(skip_rows),
+                self.full(entry3), self.lanes(widen), self.full(bc), self.states(entering), self.states(added),
+                self.states(keep_cols),
+            ],
+            [
+                self.lanes(f((own, self.inner), F32)), self.lanes(f((own, self.inner), F32)),
+                self.states(f((self.chunks, self.inner, state), BF16)), self.full(f((own, 128), F32)),
+            ],
+        )
+
+    def inv_gate(self, squares_ref):
+        return lax.rsqrt(jnp.sum(squares_ref[...], axis=1, keepdims=True) / self.inner + EPSILON)
+
+    def s3(self, y, z, squares, gain_row, w_zo, cotangent, residual):
+        own = self.own
+
+        def kernel(
+            y_ref, z_ref, squares_ref, gain_ref, w_ref, cot_ref, residual_ref,
+            gated_ref, grad_ref, cross_ref, gain_grad_ref, out_ref, sum_ref,
+        ):
+            inv = self.inv_gate(squares_ref)
+            gated = y_ref[...] * silu_of(z_ref[...])
+            normal = gated * inv
+            gated_ref[...] = (normal * gain_ref[...]).astype(BF16)
+            self.project_back(gated_ref, w_ref, sum_ref)
+            self.project(cot_ref[...], w_ref, grad_ref)
+            grad = grad_ref[...]
+            gain_grad_ref[...] = jnp.broadcast_to(
+                jnp.sum(grad * normal, axis=0, keepdims=True), gain_grad_ref.shape
             )
-
-    return pl.pallas_call(
-        kernel,
-        grid=(hts // group,),
-        out_shape=jax.ShapeDtypeStruct((count, dps * depth), F32),
-        in_specs=[
-            pl.BlockSpec((count, group * cols), lambda j: (0, j)),
-            pl.BlockSpec((dps, group, depth, cols), lambda j: (0, j, 0, 0)),
-        ],
-        out_specs=pl.BlockSpec((count, dps * depth), lambda j: (0, 0)),
-        compiler_params=local_params(),
-        cost_estimate=pl.CostEstimate(
-            flops=2 * count * pieces.size, bytes_accessed=2 * pieces.size, transcendentals=0
-        ),
-    )(values, pieces)
-
-
-def gradient_pieces(left, values, hts):
-    xs, depth, count = left.shape
-    cols = values.shape[1] // hts
-    group = group_of(cols)
-
-    def kernel(left_ref, value_ref, out_ref):
-        for at in range(xs):
-            for one in range(group):
-                out_ref[at, one] = jnp.dot(
-                    left_ref[at], value_ref[:, one * cols : (one + 1) * cols], preferred_element_type=F32
-                ).astype(BF16)
-
-    return pl.pallas_call(
-        kernel,
-        grid=(hts // group,),
-        out_shape=jax.ShapeDtypeStruct((xs, hts, depth, cols), BF16),
-        in_specs=[
-            pl.BlockSpec(left.shape, lambda j: (0, 0, 0)),
-            pl.BlockSpec((count, group * cols), lambda j: (0, j)),
-        ],
-        out_specs=pl.BlockSpec((xs, group, depth, cols), lambda j: (0, j, 0, 0)),
-        compiler_params=local_params(),
-        cost_estimate=pl.CostEstimate(
-            flops=2 * left.size * values.shape[1], bytes_accessed=2 * values.size, transcendentals=0
-        ),
-    )(left, values)
+            cross = self.lane_sums(grad * gain_ref[...] * gated)
+
+            @pl.when(pl.program_id(0) == 0)
+            def _():
+                cross_ref[...] = cross
+
+            @pl.when(pl.program_id(0) > 0)
+            def _():
+                cross_ref[...] += cross
+
+            @pl.when(pl.program_id(0) == self.groups - 1)
+            def _():
+                out_ref[...] = (residual_ref[...].astype(F32) + sum_ref[...]).astype(BF16)
+
+        f = jax.ShapeDtypeStruct
+        return self.call(
+            kernel,
+            [
+                self.lanes(y), self.lanes(z), self.full(squares), self.lanes(gain_row), self.pieces(w_zo, 1),
+                self.full(cotangent), self.full(residual),
+            ],
+            [
+                self.lanes(f((own, self.inner), BF16)), self.lanes(f((own, self.inner), F32)),
+                self.full(f((own, 128), F32)), self.lanes(f((8, self.inner), F32)),
+                self.full(f((own, self.width), BF16)),
+            ],
+            [pltpu.VMEM((own, self.width), F32)],
+        )
+
+    def s4(self, y, z, squares, cross, gain_row, grad_gate, w_zo, entry3, widen, bc, keep_cols):
+        own, state = self.own, bc.shape[1] // 2
+
+        def kernel(
+            y_ref, z_ref, squares_ref, cross_ref, gain_ref, grad_ref, w_ref, entry_ref, widen_ref, bc_ref,
+            keep_ref, low_ref, dy_ref, back_ref, local_ref, through_ref, dye_ref,
+        ):
+            inv = self.inv_gate(squares_ref)
+            cross_mean = jnp.sum(cross_ref[...], axis=1, keepdims=True) / self.inner
+            z = z_ref[...]
+            gate = jax.nn.sigmoid(z)
+            z_gate = z * gate
+            y = y_ref[...]
+            grad_gated = inv * (grad_ref[...] * gain_ref[...]) - (y * z_gate) * (inv * inv * inv * cross_mean)
+            dy = grad_gated * z_gate
+            dy_ref[...] = dy
+            low_ref[...] = (grad_gated * y * (gate * (1.0 + z * (1.0 - gate)))).astype(BF16)
+            self.project_back(low_ref, w_ref, through_ref)
+            dye_ref[...] = (dy * dot_nn(entry_ref[...], widen_ref[...])).astype(BF16)
+            held = None
+            for c in range(self.chunks - 1, -1, -1):
+                rows = self.chunk_rows(c)
+                added = dot_tn(dye_ref[rows], bc_ref[rows, state:])
+                back_ref[c] = added
+                held = added if held is None else added + keep_ref[:, c : c + 1] * held
+            local_ref[...] = held.astype(BF16)
+
+        f = jax.ShapeDtypeStruct
+        return self.call(
+            kernel,
+            [
+                self.lanes(y), self.lanes(z), self.full(squares), self.full(cross), self.lanes(gain_row),
+                self.lanes(grad_gate), self.pieces(w_zo, 0), self.full(entry3), self.lanes(widen), self.full(bc),
+                self.states(keep_cols),
+            ],
+            [
+                self.lanes(f((own, self.inner), BF16)), self.lanes(f((own, self.inner), F32)),
+                self.states(f((self.chunks, self.inner, state), F32)), self.states(f((self.inner, state), BF16)),
+                self.full(f((own, self.width), F32)),
+            ],
+            [pltpu.VMEM((own, self.wide), BF16)],
+        )
+
+    def s5(
+        self, dy, x_ext, within, conv_rows, skip_rows, same, dt3, tail3, entry3, widen, ones, cum_g, cumt_g, coupling,
+        bias, bc, states, leaving, back_added, keep_cols, w_x,
+    ):
+        own, state = self.own, bc.shape[1] // 2
+        taps = self.taps
+
+        def kernel(
+            dy_ref, ext_ref, within_ref, conv_ref, skip_ref, same_ref, dt_ref, tail_ref, entry_ref, widen_ref,
+            ones_ref, cum_ref, cumt_ref, coupling_ref, bias_ref, bc_ref, states_ref, leaving_ref, back_ref, keep_ref,
+            w_ref, low_ref, rows_ref, head_ref, dots_ref, dbc_ref, dmix_ref, through_ref,
+            xd_ref, xt_ref, dy16_ref, dye_ref, dxd_ref, shift_ref,
+        ):
+            first_step = pl.program_id(0) == 0
+
+            @pl.when(first_step)
+            def _():
+                dbc_ref[...] = jnp.zeros_like(dbc_ref)
+                dmix_ref[...] = jnp.zeros_like(dmix_ref)
+
+            pre = conv_pre(ext_ref, conv_ref, same_ref, own, taps)
+            gate = jax.nn.sigmoid(pre)
+            x = pre * gate
+            dt = dot_nn(dt_ref[...], widen_ref[...])
+            tail = dot_nn(tail_ref[...], widen_ref[...])
+            xd = x * dt
+            xd_ref[...] = xd.astype(BF16)
+            xt_ref[...] = (xd * tail).astype(BF16)
+            dy = dy_ref[...]
+            dy16_ref[...] = dy.astype(BF16)
+            entry = dot_nn(entry_ref[...], widen_ref[...])
+            dye_ref[...] = (dy * entry).astype(BF16)
+            masks = lane_masks()
+            held = leaving_ref[...]
+            for c in range(self.chunks - 1, -1, -1):
+                rows = self.chunk_rows(c)
+                held16 = held.astype(BF16)
+                into16 = states_ref[c]
+                product = held * into16.astype(F32)
+                dots_ref[0, c] = jnp.sum(product.reshape(self.heads, 64, state), axis=1)
+                spread_back = dot_nt(bc_ref[rows, :state], held16)
+                dmix = dmix_ref[c]
+                for pair in range(self.pairs):
+                    lanes = slice(pair * 128, (pair + 1) * 128)
+                    first, second = decay_pair(cum_ref, cumt_ref, bias_ref[c], rows, pair)
+                    mix = coupling_ref[c]
+                    kernel16 = jnp.concatenate([(first * mix).astype(BF16), (second * mix).astype(BF16)], 1)
+                    dy_pair = dy16_ref[rows, lanes]
+                    both = dot_tn(kernel16, dy_pair)
+                    dxd_ref[rows, lanes] = both[:CHUNK] * masks[0] + both[CHUNK:] * masks[1]
+                    dkernel = dot_nt(dy_pair, two_apart(xd_ref[rows, lanes], masks))
+                    dmix = dmix + dkernel[:, :CHUNK] * first + dkernel[:, CHUNK:] * second
+                dmix_ref[c] = dmix
+                dxd_within = dxd_ref[rows]
+                carried = dot_nt(bc_ref[rows, state:], into16)
+                falls = (
+                    dy16_ref[rows].astype(F32) * within_ref[rows]
+                    + dye_ref[rows].astype(F32) * carried
+                    - xd_ref[rows].astype(F32) * dxd_within
+                )
+                dxd = dxd_within + tail[rows] * spread_back
+                dxd_ref[rows] = dxd
+                head_ref[0, 0, rows] = self.head_sums(falls, ones_ref)
+                head_ref[0, 1, rows] = self.head_sums(xt_ref[rows].astype(F32) * spread_back, ones_ref)
+                head_ref[0, 2, rows] = self.head_sums(x[rows] * dxd, ones_ref)
+                dbc_ref[rows, :state] += dot_nn(xt_ref[rows], held16)
+                dbc_ref[rows, state:] += dot_nn(dye_ref[rows], into16)
+                if c > 0:
+                    held = back_ref[c] + keep_ref[:, c : c + 1] * held
+            dx = dxd_ref[...] * dt + skip_ref[...] * dy
+            grad = dx * (gate * (1.0 + pre * (1.0 - gate)))
+            shift_ref[:HALO] = jnp.zeros((HALO, self.wide), F32)
+            shift_ref[HALO + own :] = jnp.zeros((HALO, self.wide), F32)
+            rows_ref[taps : taps + 1] = jnp.sum(grad, axis=0, keepdims=True)
+            rows_ref[taps + 1 : taps + 2] = jnp.sum(dy * x, axis=0, keepdims=True)
+            total = None
+            for back in range(taps):
+                masked = grad if back == 0 else grad * same_ref[:, back - 1 : back]
+                shift_ref[HALO : HALO + own] = masked
+                tap = conv_ref[taps - 1 - back : taps - back]
+                piece = tap * shift_ref[back : back + own + HALO]
+                total = piece if total is None else total + piece
+                rows_ref[taps - 1 - back : taps - back] = jnp.sum(
+                    masked * ext_ref[HALO - back : HALO - back + own], axis=0, keepdims=True
+                )
+            low_ref[...] = total.astype(BF16)
+            self.project_back(low_ref, w_ref, through_ref)
+
+        f = jax.ShapeDtypeStruct
+        scratch16 = pltpu.VMEM((own, self.wide), BF16)
+        return self.call(
+            kernel,
+            [
+                self.lanes(dy), self.lanes(x_ext), self.lanes(within), self.lanes(conv_rows), self.lanes(skip_rows),
+                self.full(same), self.full(dt3), self.full(tail3), self.full(entry3), self.lanes(widen),
+                self.full(ones), self.grouped(cum_g), self.grouped(cumt_g), self.full(coupling), self.full(bias),
+                self.full(bc), self.states(states), self.states(leaving), self.states(back_added),
+                self.states(keep_cols), self.pieces(w_x),
+            ],
+            [
+                self.lanes(f((self.ext, self.inner), BF16)), self.lanes(f((8, self.inner), F32)),
+                self.grouped(f((self.groups, 3, own, 128), F32)),
+                self.grouped(f((self.groups, self.chunks, self.heads, state), F32)),
+                self.full(f((own, 2 * state), F32)), self.full(f((self.chunks, CHUNK, CHUNK), F32)),
+                self.full(f((self.ext, self.width), F32)),
+            ],
+            [
+                scratch16, scratch16, scratch16, scratch16, pltpu.VMEM((own, self.wide), F32),
+                pltpu.VMEM((own + 2 * HALO, self.wide), F32),
+            ],
+        )
 
 
 def conv_before(ext, taps, bias, same):
@@ -601,12 +1008,13 @@
 
 
 def reach_over(shift, local, keep, size, need):
-    total = shift(local.astype(BF16), 1, size).astype(F32)
+    total = shift(local, 1, size).astype(F32)
+    repeat = local.shape[0] // keep.shape[0]
     factor = shift(keep, 1, size)
     covered = 1
     while covered < min(need, size - 1):
         got = shift(total.astype(BF16), covered, size).astype(F32)
-        total = total + factor[:, None, None] * got
+        total = total + jnp.repeat(factor, repeat)[:, None] * got
         if covered * 2 < min(need, size - 1):
             factor = factor * shift(factor, covered, size)
         covered *= 2
@@ -649,22 +1057,21 @@
     core = lax.rem(lax.axis_index("dp"), 2)
     bc_own = lax.dynamic_slice_in_dim(w_bc, place * bc_cols, bc_cols, 1)
     side = bc_cols + heads_own
-    side_part = jnp.pad(jnp.concatenate([bc_own, w_dt], 1), ((0, 0), (0, 128 - side)))
+    side_rows = -(-side // 16) * 16
+    side_part = jnp.pad(jnp.concatenate([bc_own, w_dt], 1).T, ((0, side_rows - side), (0, 0)))
     taps = conv_x_weight.shape[0]
     small_rows = [conv_x_weight, conv_x_bias[None], norm_gain[None]]
     head_rows = jnp.stack([dt_bias, a_log, d_skip])
     small = jnp.concatenate(small_rows + [jnp.pad(head_rows, ((0, 0), (0, cols - heads_own)))], 0)
     small = jnp.pad(small, ((0, 16 - small.shape[0]), (0, 0)))
-    gathered = gather_weights([side_part, w_zx[:, 1], w_zx[:, 0], w_out], small, sizes)
-    side_full, w_x, w_z, w_o, small_full = gathered
-
-    def pieces(v):
-        return v.reshape(dp_size, size, dp_rows, v.shape[-1])
-
-    side_full, w_x, w_z, w_o = pieces(side_full), pieces(w_x), pieces(w_z), pieces(w_o)
-    side_cols = jnp.moveaxis(side_full[..., :side], 1, 2).reshape(width, size, side)
-    w_b = side_cols[:, :, :bc_cols].reshape(width, state2)
-    w_d = side_cols[:, :, bc_cols:].reshape(width, heads)
+    w_zo = lax.all_gather(jnp.stack([w_zx[:, 0], w_out]), ALL, axis=0, tiled=False)
+    w_zo = w_zo.reshape(dp_size, size, 2, dp_rows, cols)
+    side_full, w_x, small_full = gather_weights([side_part, w_zx[:, 1]], small, sizes)
+    w_x = w_x.reshape(dp_size, size, dp_rows, cols)
+    side_full = side_full.reshape(dp_size, size, side_rows, dp_rows)
+    side_full = jnp.moveaxis(side_full[:, :, :side], 0, 2).reshape(size, side, width)
+    w_b = side_full[:, :bc_cols].reshape(state2, width)
+    w_d = side_full[:, bc_cols:].reshape(heads, width)
     small_full = jnp.moveaxis(small_full.reshape(size, 16, cols), 0, 1)
     per_channel = small_full.reshape(16, inner)
     x_taps, x_bias, out_gain = per_channel[:taps], per_channel[taps], per_channel[taps + 1]
@@ -691,123 +1098,102 @@
     rows_ext = jnp.concatenate([from_earlier(residual[-HALO:], 1, size), residual], 0).astype(F32)
     inv_ext = lax.rsqrt(jnp.mean(rows_ext * rows_ext, axis=1, keepdims=True) + EPSILON)
     normed = (rows_ext * inv_ext * norm_in_gain).astype(BF16)
+    normed_own = normed[HALO:]
     rows_in, inv_rms = rows_ext[HALO:], inv_ext[HALO:]
-    x_ext = onto_columns(normed, w_x)
-    z = onto_columns(normed[HALO:], w_z)
-    bc_ext = dot16("td,dk->tk", normed, w_b)
-    dt_raw = dot16("td,dk->tk", normed[HALO:], w_d)
-
-    x_pre = conv_before(x_ext, x_taps, x_bias, same)
+    bc_ext = dot16("td,kd->tk", normed, w_b)
+    dt_raw = dot16("td,kd->tk", normed_own, w_d)
     bc_pre = conv_before(bc_ext, conv_bc_weight, conv_bc_bias, same)
-    x = jax.nn.silu(x_pre)
-    bc = jax.nn.silu(bc_pre).astype(BF16)
+    bc = rounded(jax.nn.silu(bc_pre))
     dt = jax.nn.softplus(dt_raw + dt_shift)
 
-    cum = jnp.einsum(
-        "lm,cmh->clh", lower, (dt * rate).reshape(chunks, CHUNK, heads), precision=HIGHEST
-    )
+    scan = Scan(own, sizes, dp_rows, cols, heads_own, taps)
+    dt_chunk = dt.reshape(chunks, CHUNK, heads)
+    cum = jnp.einsum("lm,cmh->clh", lower, dt_chunk * rate, precision=HIGHEST)
+    in_end = (seg_chunk == end_chunk[:, None]).astype(F32)[..., None]
+    in_start = (seg_chunk == end_before[:, None]).astype(F32)[..., None]
+    tail = (jnp.exp(cum[:, -1:] - cum) * in_end).reshape(own, heads)
+    entry = (jnp.exp(cum) * in_start).reshape(own, heads)
+    keep = jnp.exp(cum[:, -1]) * (end_before == end_chunk).astype(F32)[:, None]
+    keep_local = jnp.prod(keep, axis=0)
+    keep_cols = jnp.repeat(keep.T, head_width, axis=0)
     b_chunk = bc[:, :state].reshape(chunks, CHUNK, state)
     c_chunk = bc[:, state:].reshape(chunks, CHUNK, state)
-
-    def split(v):
-        return v.reshape(chunks, CHUNK, heads, head_width)
-
-    x4 = split(x)
-    dt_chunk = dt.reshape(chunks, CHUNK, heads)
-    xd = x4 * dt_chunk[..., None]
-    xd16 = rounded(xd)
     coupling = dot16("cls,cms->clm", c_chunk, b_chunk)
-    cum_t = jnp.moveaxis(cum, 2, 1)
-    decay = jnp.exp(cum_t[:, :, :, None] - cum_t[:, :, None, :] + mask_bias[:, None])
-    kernel = rounded(decay * coupling[:, None])
-    y_within = dot16("chlm,cmhp->clhp", kernel, xd16)
-    in_end = (seg_chunk == end_chunk[:, None]).astype(F32)[..., None]
-    in_start = (seg_chunk == end_before[:, None]).astype(F32)[..., None]
-    tail = jnp.exp(cum[:, -1:] - cum) * in_end
-    entry = jnp.exp(cum) * in_start
-    keep = jnp.exp(cum[:, -1]) * (end_before == end_chunk).astype(F32)[:, None]
-    xt16 = rounded(xd * tail[..., None])
-    added = dot16("cmhp,cms->chps", xt16, b_chunk)
-
-    local, keep_local = added[0], keep[0]
-    for c in range(1, chunks):
-        local = added[c] + keep[c][:, None, None] * local
-        keep_local = keep_local * keep[c]
+    cum_g = jnp.moveaxis(cum.reshape(own, scan.groups, scan.heads), 1, 0)
+    cumt_g = jnp.moveaxis(cum_g, 1, 2)
+    dt3, tail3, entry3 = thirds(dt), thirds(tail), thirds(entry)
+    head_of = lax.broadcasted_iota(jnp.int32, (heads, inner), 1) // head_width
+    widen = (head_of == lax.broadcasted_iota(jnp.int32, (heads, inner), 0)).astype(BF16)
+    widen = jnp.concatenate([widen] * 3, 0)
+    ones = (
+        lax.broadcasted_iota(jnp.int32, (scan.wide, 128), 0) // head_width
+        == lax.broadcasted_iota(jnp.int32, (scan.wide, 128), 1)
+    ).astype(BF16)
+    same_cols = jnp.pad(jnp.concatenate(same, 1), ((0, 0), (0, 8 - len(same))))
+    conv_rows = jnp.concatenate([x_taps, x_bias[None]], 0)
+    conv_rows = jnp.pad(conv_rows, ((0, 8 - conv_rows.shape[0]), (0, 0)))
+    skip_rows, gain_row = skip_wide[None], out_gain[None]
     need = -(-(DOC_MOST - 1) // own)
-    entering = [reach_over(from_earlier, local, keep_local, size, need)]
-    for c in range(chunks - 1):
-        entering.append(added[c] + keep[c][:, None, None] * entering[c])
-    entering = jnp.stack(entering, 0)
-    entering16 = entering.astype(BF16)
-    y_entry = dot16("cls,chps->clhp", c_chunk, entering16)
-    y = (y_within + y_entry * entry[..., None]).reshape(own, inner) + skip_wide * x
-
-    z_gate = jax.nn.silu(z)
-    gated = y * z_gate
-    inv_gate = lax.rsqrt(jnp.mean(gated * gated, axis=1, keepdims=True) + EPSILON)
-    gated_out = (gated * inv_gate * out_gain).astype(BF16)
-    block_out = (rows_in + back_from_columns(gated_out, w_o)).astype(BF16)
-    grad_gate = onto_columns(cotangent, w_o)
-    grad_norm_gain = jnp.sum(grad_gate * gated * inv_gate, axis=0)
-    scaled_gate = grad_gate * out_gain
-    cross = jnp.sum(scaled_gate * gated, axis=1, keepdims=True)
-    grad_gated = inv_gate * scaled_gate - gated * (inv_gate * inv_gate * inv_gate) * (cross / inner)
-
-    dy = grad_gated * z_gate
-    dz = grad_gated * y * silu_grad(z)
-    grad_skip = jnp.sum((dy * x).reshape(own, heads, head_width), axis=(0, 2))
-
-    dy4 = split(dy)
-    dy16 = rounded(dy4)
-    dye16 = rounded(dy4 * entry[..., None])
-    back_added = dot16("clhp,cls->chps", dye16, c_chunk)
-    back_local = back_added[-1]
-    for c in range(chunks - 2, -1, -1):
-        back_local = back_added[c] + keep[c][:, None, None] * back_local
-    leaving = [reach_over(from_later, back_local, keep_local, size, need)]
-    for c in range(chunks - 1, 0, -1):
-        leaving.append(back_added[c] + keep[c][:, None, None] * leaving[-1])
-    leaving = jnp.stack(leaving[::-1], 0)
-    leaving16 = leaving.astype(BF16)
-    dxd_within = dot16("chlm,clhp->cmhp", kernel, dy16)
-    dxt = dot16("cms,chps->cmhp", b_chunk, leaving16)
-    dxd = dxd_within + tail[..., None] * dxt
-    dx = (dxd * dt_chunk[..., None]).reshape(own, inner) + skip_wide * dy
-    dkernel = dot16("clhp,cmhp->chlm", dy16, xd16)
-    dcoupling = jnp.sum(dkernel * decay, axis=1)
-    dc = dot16("clm,cms->cls", dcoupling, b_chunk) + dot16("clhp,chps->cls", dye16, entering16)
-    db = dot16("clm,cls->cms", dcoupling, c_chunk) + dot16("cmhp,chps->cms", xt16, leaving16)
-    falls = jnp.sum(
-        dy16.astype(F32) * y_within
-        + dye16.astype(F32) * y_entry
-        - xd16.astype(F32) * dxd_within,
-        axis=3,
-    )
-    rises = jnp.sum(xt16.astype(F32) * dxt, axis=3)
+
+    x_ext, x, within, added, local = scan.s1(
+        normed, w_x, conv_rows, same_cols, dt3, tail3, widen, cum_g, cumt_g, coupling, mask_bias, bc, keep_cols
+    )
+    entering = reach_over(from_earlier, local, keep_local, size, need)
+    z, y, states, squares = scan.s2(
+        normed_own, w_zo, within, x, skip_rows, entry3, widen, bc, entering, added, keep_cols
+    )
+    gated_out, grad_gate, cross, gain_rows, block_out = scan.s3(
+        y, z, squares, gain_row, w_zo, cotangent, residual
+    )
+    grad_norm_gain = gain_rows[0]
+    low_z, dy, back_added, back_local, own_part = scan.s4(
+        y, z, squares, cross, gain_row, grad_gate, w_zo, entry3, widen, bc, keep_cols
+    )
+    def as_left(v):
+        return v.T.reshape(dp_size, dp_rows, v.shape[0])
+
+    early = gradient_pieces(
+        [as_left(normed_own), as_left(cotangent)], [low_z, gated_out], size
+    )
+    early = lax.psum_scatter(
+        early.reshape((dp_size * size,) + early.shape[2:]), ALL, scatter_dimension=0, tiled=False
+    ).astype(F32)
+    leaving = reach_over(from_later, back_local, keep_local, size, need)
+    low_x, conv_sums, head_sums, state_dots, dbc, dmix, through = scan.s5(
+        dy, x_ext, within, conv_rows, skip_rows, same_cols, dt3, tail3, entry3, widen, ones, cum_g, cumt_g,
+        coupling, mask_bias, bc, states, leaving, back_added, keep_cols, w_x
+    )
+    grad_taps, grad_bias = conv_sums[:taps], conv_sums[taps]
+    grad_skip = jnp.sum(conv_sums[taps + 1].reshape(heads, head_width), axis=1)
+    dbc = dbc + jnp.concatenate(
+        [
+            dot16("clm,cls->cms", dmix, c_chunk).reshape(own, state),
+            dot16("clm,cms->cls", dmix, b_chunk).reshape(own, state),
+        ],
+        1,
+    )
+    head_sums = jnp.moveaxis(head_sums[..., : scan.heads], 0, 2).reshape(3, chunks, CHUNK, heads)
+    falls, rises, direct = head_sums[0], head_sums[1], head_sums[2]
+    state_dots = jnp.moveaxis(jnp.sum(state_dots, axis=3), 0, 1).reshape(chunks, heads)
     strict = lower - jnp.eye(CHUNK, dtype=F32)
     da = (
         jnp.einsum("lm,clh->cmh", lower, falls, precision=HIGHEST)
         + jnp.einsum("lm,cmh->clh", strict, rises, precision=HIGHEST)
-        + (keep * jnp.sum(leaving * entering, axis=(2, 3)))[:, None]
-    )
-    ddt = jnp.sum(x4 * dxd, axis=3) + rate * da
+        + (keep * state_dots)[:, None]
+    )
+    ddt = direct + rate * da
     grad_log = rate * jnp.sum(dt_chunk * da, axis=(0, 1))
     ddt_raw = ddt.reshape(own, heads) * jax.nn.sigmoid(dt_raw + dt_shift)
     grad_shift = jnp.sum(ddt_raw, axis=0)
 
-    gx, grad_taps, grad_bias = conv_back(dx * silu_grad(x_pre), x_ext, x_taps, same)
-    dbc = jnp.concatenate([db, dc], 2).reshape(own, state2)
     gbc, grad_bc_taps, grad_bc_bias = conv_back(
         dbc * silu_grad(bc_pre), bc_ext, conv_bc_weight, same
     )
-    low_x = gx.astype(BF16)
     low_bc = gbc.astype(BF16)
-    low_z = dz.astype(BF16)
     low_dt = ddt_raw.astype(BF16)
-    normed_own = normed[HALO:]
-
-    own_part = back_from_columns(low_z, w_z) + dot16("tk,dk->td", low_dt, w_d)
-    ext_part = back_from_columns(low_x, w_x) + dot16("tk,dk->td", low_bc, w_b)
+
+    own_part = own_part + dot16("tk,kd->td", low_dt, w_d)
+    ext_part = through + dot16("tk,kd->td", low_bc, w_b)
     last = from_later(ext_part[:HALO], 1, size)
     grad_normed = own_part + ext_part[HALO:]
     grad_normed = grad_normed.at[own - HALO :].add(last)
@@ -832,7 +1218,6 @@
 
     normed_pair = to_pair(normed)
     left_ext = left_of(normed_pair)
-    low_z_ext = jnp.pad(low_z, ((HALO, 0), (0, 0)))
     low_side = jnp.concatenate(
         [
             low_bc.reshape(-1, size, bc_cols),
@@ -840,14 +1225,14 @@
         ],
         2,
     )
-    low_side = jnp.pad(low_side, ((0, 0), (0, 0), (0, 128 - side))).reshape(-1, size * 128)
+    low_side = jnp.pad(low_side, ((0, 0), (0, 0), (0, side_rows - side))).reshape(-1, size * side_rows)
+    side_pieces = dot16("tk,xdt->xkd", to_pair(low_side), left_ext).astype(BF16)
+    x_pieces = gradient_pieces([left_ext], [to_pair(low_x)], size)
+    grid = (dp_size // 2,) + sizes[1:]
     parts = [
-        gradient_pieces(left_of(to_pair(cotangent)), to_pair(gated_out), size),
-        gradient_pieces(left_ext, to_pair(low_z_ext), size),
-        gradient_pieces(left_ext, to_pair(low_x), size),
-        gradient_pieces(left_ext, to_pair(low_side), size),
+        side_pieces.reshape(grid + (side_rows, dp_rows)),
+        x_pieces.reshape(grid + (dp_rows, cols)),
     ]
-    parts = [v.reshape((dp_size // 2,) + sizes[1:] + v.shape[2:]) for v in parts]
     head_sum = jnp.stack([grad_shift, grad_log, grad_skip], 0).reshape(-1)
     row = jnp.concatenate([grad_in_gain, grad_bc_taps.reshape(-1), grad_bc_bias])
     small_sum = jnp.concatenate(
@@ -860,10 +1245,12 @@
         ],
         0,
     )
-    grad_wo, grad_wz, grad_wx, grad_side, small_sum = scatter_gradients(parts, small_sum, sizes)
-    grad_wzx = jnp.stack([grad_wz, grad_wx], 1)
-    grad_wbc = lax.all_gather(grad_side[:, :bc_cols], SEQ, axis=1, tiled=True)
-    grad_wdt = grad_side[:, bc_cols:side]
+    grad_side, grad_wx, small_sum = scatter_gradients(parts, small_sum, sizes)
+    grad_wzx = jnp.stack([early[0], grad_wx], 1)
+    grad_wo = early[1]
+    grad_side = grad_side.reshape(size, side_rows, dp_rows)
+    grad_wbc = grad_side[:, :bc_cols].reshape(state2, dp_rows).T
+    grad_wdt = lax.dynamic_index_in_dim(grad_side, place, 0, keepdims=False)[bc_cols:side].T
     channel_own = lax.dynamic_slice_in_dim(small_sum[: taps + 2], place * cols, cols, 1)
     row = small_sum[taps + 2]
     gain_sum = row[:width]

time: 1010 us -> 654 us (0.65)
  other arithmetic: 170 us -> 57.7 us
  Pallas kernels: 462 us -> 367 us
  local copies, waits for them, and re-layouts: 182 us -> 90.7 us
  matrix products: 62 us -> 11.7 us
  blocking collectives: 31 us -> 0 us
  between operations: 2.52 us -> 15.6 us
    pallas_call x1, Pallas kernels: 184 us -> 97.2 us  [gather_weights(): pl.pallas_call(functools.partial(gather_kernel, sizes, chunks, kinds), ou...]
    reshape x11 -> x8, local copies, waits for them, and re-layouts: 86 us -> 5.66 us  [the longest x2 2.01 us: body(): cum_g = jnp.moveaxis(cum.reshape(own, scan.groups, scan.heads), 1, 0)]
    pallas_call x6 -> x5, Pallas kernels: 77.1 us -> 143 us  [call(): pl.pallas_call(kernel, grid=(self.groups,), out_shape=[shape for shape, _...]
    pallas_call x1, Pallas kernels: 155 us -> 95.8 us  [scatter_gradients(): pl.pallas_call(functools.partial(scatter_kernel, sizes, chunks, kinds), o...]
    dot_general x16 -> x8, matrix products: 59.6 us -> 10.8 us  [dot16(): jnp.einsum(pattern, left.astype(BF16), right.astype(BF16), preferred_elem...]
    reduce_sum x6 -> x2, other arithmetic: 43 us -> 0.23 us  [the longest x1 0.12 us: body(): jnp.sum(state_dots, axis=3)]
    all_gather x1 -> x0, blocking collectives: 31 us -> none  [body(): grad_wbc = lax.all_gather(grad_side[:, :bc_cols], SEQ, axis=1, tiled=True)]
    select_n x6 -> x3, other arithmetic: 33.4 us -> 11.6 us  [to_pair(): jnp.where(core == 0, jnp.stack([v, other]), jnp.stack([other, v]))]
  transfers between devices with their start and end apart: 18 -> 17, of which waited for: 4 -> 6; matrix products, arithmetic and copies ran while one was open for 32% -> 23% of each run, Pallas kernels for 28% -> 44%
where the time goes in v3:
time: 654 us; the launch traced here: 642 us
  Pallas kernels  367 us (56%)
  local copies, waits for them, and re-layouts  90.7 us (14%)
  waiting for transfers between devices  59.5 us (9%)
  other arithmetic  57.7 us (9%)
  starting transfers between devices  40 us (6%)
  between operations  15.6 us (2%)
  matrix products  11.7 us (2%)
    pallas_call x5, Pallas kernels, call(): pl.pallas_call(kernel, grid=(self.groups,), out_shape=[shape for shape, _...  143 us
    pallas_call x1, Pallas kernels, gather_weights(): pl.pallas_call(functools.partial(gather_kernel, sizes, chunks, kinds), ou...  97.2 us
    pallas_call x1, Pallas kernels, scatter_gradients(): pl.pallas_call(functools.partial(scatter_kernel, sizes, chunks, kinds), o...  95.8 us
    ppermute x6, starting transfers between devices, from_earlier(): lax.ppermute(values, SEQ, [(i, i + distance) for i in range(size - distan...  30.8 us
    pallas_call x2, Pallas kernels, gradient_pieces(): pl.pallas_call(kernel, grid=(hts // group,), out_shape=jax.ShapeDtypeStru...  30.7 us
    ppermute x6, waiting for transfers between devices, from_earlier(): lax.ppermute(values, SEQ, [(i, i + distance) for i in range(size - distan...  29.8 us
    ppermute x6, waiting for transfers between devices, from_later(): lax.ppermute(values, SEQ, [(i + distance, i) for i in range(size - distan...  29.7 us
  transfers between devices with their start and end apart: 17, of which 6 were waited for; matrix products, arithmetic and copies ran while one was open for 23% of the time, Pallas kernels for 44%

profile of v3, /device:TPU:0, one launch (start us, length us, event | category | flops | bytes accessed | tf_op | source)
XLA Modules:
  0.0 641.9 jit_solution(2010564246905365730)
XLA Ops:
  11.4 4.9 collective-permute-start
  19.2 97.2 %shard_map.271 = (bf16[4,4,2,48,384]{4,3,2,1,0:T(8,128)(2,1)}, bf16[4,4,2,384,384]{4,3,2,1,0:T(8,128)(2,1)}, f32[4,2,16,384]{3,2,1,0:T(8,128)}) custom-call(bf16[48,384]{1,0:T(8,128)(2,1)} %pad.55.refs_0_, bf16[384,384]{1,0:T(8,128)(2,1)} %bitcast.242, f32[16,384]{1,0:T(8,128)} %select_maximum_fusion.1.refs_2_), custom_call_target="tpu_custom_call" | custom-call | flops 54000001024 | tf_op jit(solution)/shard_map/pallas_call | solution.py:220
  152.4 23.3 %shard_map.272 = (f32[528,3072]{1,0:T(8,128)}, f32[512,3072]{1,0:T(8,128)}, f32[512,3072]{1,0:T(8,128)}, f32[4,3072,128]{2,1,0:T(8,128)}, bf16[3072,128]{1,0:T(8,128)(2,1)}) custom-call(bf16[528,1536]{1,0:T(8,128)(2,1)} %copy-done.5, bf16[4,8,384,384]{3,2,1,0:T(8,128)(2,1)} %bitcast.286, f32[8,3072]{1,0:T(8,128)} %select_maximum_fusion.conv_ref, ...), custom_call_target="tpu_custom_call" | custom-call | flops 19800000512 | tf_op jit(solution)/shard_map/pallas_call | solution.py:625
  175.7 4.0 collective-permute-start.1
  179.7 17.5 %collective-permute-done.1 = bf16[3072,128]{1,0:T(8,128)(2,1)S(1)} collective-permute-done((bf16[3072,128]{1,0:T(8,128)(2,1)}, bf16[3072,128]{1,0:T(8,128)(2,1)S(1)}, u32[]{:S(2)}, u32[]{:S(2)}) %collective-permute-start.1) | collective-permute-done | bytes 786464 | tf_op jit(solution)/shard_map/ppermute | solution.py:1003
  197.3 6.3 collective-permute-start.3
  207.8 4.5 collective-permute-start.2
  213.4 5.9 collective-permute-done.2
  221.9 8.0 %collective-permute-start.5 = (bf16[3072,128]{1,0:T(8,128)(2,1)}, bf16[3072,128]{1,0:T(8,128)(2,1)}, u32[]{:S(2)}, u32[]{:S(2)}) collective-permute-start(bf16[3072,128]{1,0:T(8,128)(2,1)} %fusion.1), channel_id=1, source_target_pairs={{0,2},{1,3},{2,4},{3,5},{4,6},{5,7},{8,10},{9,11},{10,12},{11,13},... | collective-permute-start | bytes 2359304 | tf_op jit(solution)/shard_map/ppermute | solution.py:1003
  238.6 6.4 collective-permute-done.5
  248.6 21.8 %shard_map.273 = (f32[512,3072]{1,0:T(8,128)}, f32[512,3072]{1,0:T(8,128)}, bf16[4,3072,128]{2,1,0:T(8,128)(2,1)}, f32[512,128]{1,0:T(8,128)}) custom-call(bf16[512,1536]{1,0:T(8,128)(2,1)} %get-tuple-element.197.normed_ref, bf16[4,8,2,384,384]{4,3,2,1,0:T(8,128)(2,1)} %bitcast.283, f32[512,3072]{1,0:T(8,128)} %get-tuple-element.62.within_ref, ...), custom_call_target="tpu_custom_call" | custom-call | flops 19800000512 | tf_op jit(solution)/shard_map/pallas_call | solution.py:625
  270.4 22.2 %shard_map.274 = (bf16[512,3072]{1,0:T(8,128)(2,1)}, f32[512,3072]{1,0:T(8,128)}, f32[512,128]{1,0:T(8,128)}, f32[8,3072]{1,0:T(8,128)}, bf16[512,1536]{1,0:T(8,128)(2,1)}) custom-call(f32[512,3072]{1,0:T(8,128)} %get-tuple-element.66.y_ref, f32[512,3072]{1,0:T(8,128)} %get-tuple-element.67.z_ref, f32[512,128]{1,0:T(8,128)} %get-tuple-element.68.squares_ref, ...), custom_call_target="tpu_custom_call" | custom-call | flops 19800000512 | tf_op jit(solution)/shard_map/pallas_call | solution.py:625
  292.6 23.3 %shard_map.275 = (bf16[512,3072]{1,0:T(8,128)(2,1)}, f32[512,3072]{1,0:T(8,128)}, f32[4,3072,128]{2,1,0:T(8,128)}, bf16[3072,128]{1,0:T(8,128)(2,1)}, f32[512,1536]{1,0:T(8,128)}) custom-call(f32[512,3072]{1,0:T(8,128)} %get-tuple-element.66.y_ref, f32[512,3072]{1,0:T(8,128)} %get-tuple-element.67.z_ref, f32[512,128]{1,0:T(8,128)} %get-tuple-element.68.squares_ref, ...), custom_call_target="tpu_custom_call" | custom-call | flops 19800000512 | tf_op jit(solution)/shard_map/pallas_call | solution.py:625
  315.9 18.2 %shard_map.279 = bf16[4,8,2,384,384]{4,3,2,1,0:T(8,128)(2,1)} custom-call(bf16[4,384,512]{2,1,0:T(8,128)(2,1)} %bitcast.217, bf16[4,384,512]{2,1,0:T(8,128)(2,1)} %bitcast.216, bf16[512,3072]{1,0:T(8,128)(2,1)} %get-tuple-element.87.refs_2_, bf16[512,3072]{1,0:T(8,128)(2,1)} %get-tuple-element.88.refs_3_), custom_call_target="tpu_custom_call" | custom-call | flops 21600000000 | tf_op jit(solution)/shard_map/pallas_call | solution.py:545
  337.9 15.7 %collective-permute-done.6 = bf16[3072,128]{1,0:T(8,128)(2,1)S(1)} collective-permute-done((bf16[3072,128]{1,0:T(8,128)(2,1)}, bf16[3072,128]{1,0:T(8,128)(2,1)S(1)}, u32[]{:S(2)}, u32[]{:S(2)}) %collective-permute-start.6) | collective-permute-done | bytes 786464 | tf_op jit(solution)/shard_map/ppermute | solution.py:1007
  360.9 12.3 %collective-permute-done.9 = f32[48]{0:T(128)S(1)} collective-permute-done((f32[48]{0:T(128)S(1)}, f32[48]{0:T(128)S(1)}, u32[]{:S(2)}, u32[]{:S(2)}) %collective-permute-start.9) | collective-permute-done | bytes 224 | tf_op jit(solution)/shard_map/ppermute | solution.py:1007
  377.7 3.8 maximum_select_fusion.1
  381.6 5.7 reshape.433
  387.2 6.7 %constant_dynamic-slice_fusion.2 = bf16[2,1,384,1056]{2,1,0,3:T(2,128)(2,1)} fusion(bf16[2,2,384,1056]{2,1,0,3:T(2,128)(2,1)} %reshape.433, s32[]{:T(128)S(6)} %select_n.108), kind=kLoop, calls=%fused_computation.163 | loop fusion | bytes 3244036 | tf_op jit(solution)/shard_map/jit(dynamic_index_in_dim)/dynamic_slice | solution.py:1217
  393.9 8.6 %copy.239 = bf16[2,1,384,1056]{3,2,0,1:T(8,128)(2,1)} copy(bf16[2,1,384,1056]{2,1,0,3:T(2,128)(2,1)} %constant_dynamic-slice_fusion.2) | data formatting | bytes 3244032 | tf_op jit(solution)/shard_map/jit(dynamic_index_in_dim)/squeeze | solution.py:1217
  407.2 52.5 %shard_map.276 = (bf16[528,3072]{1,0:T(8,128)(2,1)}, f32[8,3072]{1,0:T(8,128)}, f32[8,3,512,128]{3,2,1,0:T(8,128)}, f32[8,4,6,128]{3,2,1,0:T(8,128)}, f32[512,25...) custom-call(f32[512,3072]{1,0:T(8,128)} %get-tuple-element.73.dy_ref, ...), custom_call_target="tpu_custom_call" | custom-call | flops 19800000512 | tf_op jit(solution)/shard_map/pallas_call | solution.py:625
  503.3 7.5 %maximum_select_fusion = bf16[2,528,3072]{2,1,0:T(8,128)(2,1)} fusion(bf16[1,528,3072]{2,1,0:T(8,128)(2,1)} %bitcast.64, bf16[1,528,3072]{2,1,0:T(8,128)(2,1)S(1)} %bitcast.206, pred[]{:T(512)S(6)} %eq.82), kind=kLoop, calls=%fused_computation | loop fusion | flops 9732096 | bytes 12976129 | tf_op jit(solution)/shard_map/jit(_where)/select_n | solution.py:1211
  510.8 12.6 %shard_map.277 = bf16[2,8,1,384,384]{4,3,2,1,0:T(8,128)(2,1)} custom-call(bf16[2,384,1056]{2,1,0:T(8,128)(2,1)} %bitcast.211, bf16[1056,3072]{1,0:T(8,128)(2,1)} %bitcast.203), custom_call_target="tpu_custom_call" | custom-call | flops 10800000000 | tf_op jit(solution)/shard_map/pallas_call | solution.py:545
  523.4 95.8 %shard_map.278 = (f32[4,2,48,384]{3,2,1,0:T(8,128)}, f32[384,384]{1,0:T(8,128)}, f32[8,3072]{1,0:T(8,128)}) custom-call(bf16[2,4,2,48,384]{4,3,2,1,0:T(8,128)(2,1)} %bitcast.289, bf16[2,4,2,384,384]{4,3,2,1,0:T(8,128)(2,1)} %bitcast.288, f32[8,3072]{1,0:T(8,128)} %pad_maximum_fusion.5.refs_2_), custom_call_target="tpu_custom_call" | custom-call | flops 54000001024 | tf_op jit(solution)/shard_map/pallas_call | solution.py:488
  (361 shorter events, 141.7 us)
Async XLA Ops:
  7.3 241.3 %all-gather.3.cloned.1.call-start = ((), (), s32[]{:S(2)}) async-start(), calls=%async_computation.2 | async-start | bytes 19464192 | tf_op jit(solution)/shard_map/all_gather | solution.py:1067
  10.7 620.0 %reduce-scatter.2.cloned.1.call-start = ((), (), s32[]{:S(2)}) async-start(), calls=%async_computation.1 | async-start | bytes 19464192 | tf_op jit(solution)/shard_map/reduce_scatter | solution.py:1158
  11.4 126.2 %collective-permute-start = (bf16[16,1536]{1,0:T(8,128)(2,1)}, bf16[16,1536]{1,0:T(8,128)(2,1)S(1)}, u32[]{:S(2)}, u32[]{:S(2)}) collective-permute-start(bf16[16,1536]{1,0:T(8,128)(2,1)} %slice.245), channel_id=1, source_target_pairs={{0,1},{1,2},{2,3},{3,4},{4,5},{5,6},{6,7},{8,9},{9,10},{10,11},{11... | collective-permute-start | bytes 147464 | tf_op jit(solution)/shard_map/ppermute | solution.py:1003
  19.2 100.9 %copy-start.69 = (f32[4,256]{1,0:T(4,128)S(1)}, f32[4,256]{1,0:T(4,128)}, u32[]{:S(2)}) copy-start(f32[4,256]{1,0:T(4,128)} %param.26) | copy-start | bytes 12292
  146.8 61.0 %copy-start.73 = (f32[48]{0:T(128)}, f32[48]{0:T(128)S(1)}, u32[]{:S(2)}) copy-start(f32[48]{0:T(128)S(1)} %get-tuple-element.208) | copy-start | bytes 580
  152.4 51.2 %copy-start.49 = (f32[1,8,6]{2,1,0:T(8,128)S(1)}, f32[1,8,6]{2,1,0:T(8,128)}, u32[]{:S(2)}) copy-start(f32[1,8,6]{2,1,0:T(8,128)} %get-tuple-element.218) | copy-start | bytes 580
  152.4 52.0 %copy-start.45 = (f32[1,1,8,384]{3,2,1,0:T(8,128)S(1)}, f32[1,1,8,384]{3,2,1,0:T(8,128)}, u32[]{:S(2)}) copy-start(f32[1,1,8,384]{3,2,1,0:T(8,128)} %get-tuple-element.216) | copy-start | bytes 36868
  175.7 21.6 %collective-permute-start.1 = (bf16[3072,128]{1,0:T(8,128)(2,1)}, bf16[3072,128]{1,0:T(8,128)(2,1)S(1)}, u32[]{:S(2)}, u32[]{:S(2)}) collective-permute-start(bf16[3072,128]{1,0:T(8,128)(2,1)} %get-tuple-element.64), channel_id=1, source_target_pairs={{0,1},{1,2},{2,3},{3,4},{4,5},{5,6},{6,7},{8,9},{9,10},{10,11},{11... | collective-permute-start | bytes 2359304 | tf_op jit(solution)/shard_map/ppermute | solution.py:1003
  197.3 22.2 %collective-permute-start.3 = (bf16[3072,128]{1,0:T(8,128)(2,1)S(1)}, bf16[3072,128]{1,0:T(8,128)(2,1)}, u32[]{:S(2)}, u32[]{:S(2)}) collective-permute-start(bf16[3072,128]{1,0:T(8,128)(2,1)S(1)} %collective-permute-done.1), channel_id=1, source_target_pairs={{0,1},{1,2},{2,3},{3,4},{4,5},{5,6},{6,7},{8,9},{9,10},{10,11},{11... | collective-permute-start | bytes 2359304 | tf_op jit(solution)/shard_map/ppermute | solution.py:1003
  207.8 11.5 %collective-permute-start.2 = (f32[48]{0:T(128)S(1)}, f32[48]{0:T(128)S(1)}, u32[]{:S(2)}, u32[]{:S(2)}) collective-permute-start(f32[48]{0:T(128)S(1)} %get-tuple-element.208), channel_id=1, source_target_pairs={{0,1},{1,2},{2,3},{3,4},{4,5},{5,6},{6,7},{8,9},{9,10},{10,11},{11... | collective-permute-start | bytes 584 | tf_op jit(solution)/shard_map/ppermute | solution.py:1003
  221.9 23.1 %collective-permute-start.5 = (bf16[3072,128]{1,0:T(8,128)(2,1)}, bf16[3072,128]{1,0:T(8,128)(2,1)}, u32[]{:S(2)}, u32[]{:S(2)}) collective-permute-start(bf16[3072,128]{1,0:T(8,128)(2,1)} %fusion.1), channel_id=1, source_target_pairs={{0,2},{1,3},{2,4},{3,5},{4,6},{5,7},{8,10},{9,11},{10,12},{11,13},... | collective-permute-start | bytes 2359304 | tf_op jit(solution)/shard_map/ppermute | solution.py:1003
  231.9 6.6 %collective-permute-start.4 = (f32[48]{0:T(128)S(1)}, f32[48]{0:T(128)S(1)}, u32[]{:S(2)}, u32[]{:S(2)}) collective-permute-start(f32[48]{0:T(128)S(1)} %collective-permute-done.2), channel_id=1, source_target_pairs={{0,1},{1,2},{2,3},{3,4},{4,5},{5,6},{6,7},{8,9},{9,10},{10,11},{11... | collective-permute-start | bytes 584 | tf_op jit(solution)/shard_map/ppermute | solution.py:1003
  334.1 19.5 %collective-permute-start.6 = (bf16[3072,128]{1,0:T(8,128)(2,1)}, bf16[3072,128]{1,0:T(8,128)(2,1)S(1)}, u32[]{:S(2)}, u32[]{:S(2)}) collective-permute-start(bf16[3072,128]{1,0:T(8,128)(2,1)} %get-tuple-element.76), channel_id=1, source_target_pairs={{1,0},{2,1},{3,2},{4,3},{5,4},{6,5},{7,6},{9,8},{10,9},{11,10},{12... | collective-permute-start | bytes 2359304 | tf_op jit(solution)/shard_map/ppermute | solution.py:1007
  336.5 22.2 %collective-permute-start.7 = (f32[48]{0:T(128)S(1)}, f32[48]{0:T(128)S(1)}, u32[]{:S(2)}, u32[]{:S(2)}) collective-permute-start(f32[48]{0:T(128)S(1)} %copy-done.74), channel_id=1, source_target_pairs={{1,0},{2,1},{3,2},{4,3},{5,4},{6,5},{7,6},{9,8},{10,9},{11,10},{12... | collective-permute-start | bytes 584 | tf_op jit(solution)/shard_map/ppermute | solution.py:1007
  337.8 39.9 %collective-permute-start.12 = (bf16[528,1536]{1,0:T(8,128)(2,1)}, bf16[528,1536]{1,0:T(8,128)(2,1)}, u32[]{:S(2)}, u32[]{:S(2)}) collective-permute-start(bf16[528,1536]{1,0:T(8,128)(2,1)} %copy-done.5), channel_id=1, source_target_pairs={{0,8},{8,0},{16,24},{24,16},{1,9},{9,1},{17,25},{25,17},{2,10},{10... | collective-permute-start | bytes 4866056 | tf_op jit(solution)/shard_map/ppermute | solution.py:1210
  353.5 19.8 %collective-permute-start.8 = (bf16[3072,128]{1,0:T(8,128)(2,1)S(1)}, bf16[3072,128]{1,0:T(8,128)(2,1)}, u32[]{:S(2)}, u32[]{:S(2)}) collective-permute-start(bf16[3072,128]{1,0:T(8,128)(2,1)S(1)} %collective-permute-done.6), channel_id=1, source_target_pairs={{1,0},{2,1},{3,2},{4,3},{5,4},{6,5},{7,6},{9,8},{10,9},{11,10},{12... | collective-permute-start | bytes 2359304 | tf_op jit(solution)/shard_map/ppermute | solution.py:1007
  358.7 14.5 %collective-permute-start.9 = (f32[48]{0:T(128)S(1)}, f32[48]{0:T(128)S(1)}, u32[]{:S(2)}, u32[]{:S(2)}) collective-permute-start(f32[48]{0:T(128)S(1)} %collective-permute-done.7), channel_id=1, source_target_pairs={{1,0},{2,1},{3,2},{4,3},{5,4},{6,5},{7,6},{9,8},{10,9},{11,10},{12... | collective-permute-start | bytes 584 | tf_op jit(solution)/shard_map/ppermute | solution.py:1007
  376.0 27.5 %collective-permute-start.10 = (bf16[3072,128]{1,0:T(8,128)(2,1)}, bf16[3072,128]{1,0:T(8,128)(2,1)}, u32[]{:S(2)}, u32[]{:S(2)}) collective-permute-start(bf16[3072,128]{1,0:T(8,128)(2,1)} %fusion.2), channel_id=1, source_target_pairs={{2,0},{3,1},{4,2},{5,3},{6,4},{7,5},{10,8},{11,9},{12,10},{13,11},... | collective-permute-start | bytes 2359304 | tf_op jit(solution)/shard_map/ppermute | solution.py:1007
  407.2 52.5 %copy-start.22 = (bf16[512,128]{1,0:T(8,128)(2,1)S(1)}, bf16[512,128]{1,0:T(8,128)(2,1)}, u32[]{:S(2)}) copy-start(bf16[512,128]{1,0:T(8,128)(2,1)} %copy-done.21) | copy-start | bytes 393220
  407.2 53.7 %copy-start.20 = (bf16[512,128]{1,0:T(8,128)(2,1)S(1)}, bf16[512,128]{1,0:T(8,128)(2,1)}, u32[]{:S(2)}) copy-start(bf16[512,128]{1,0:T(8,128)(2,1)} %copy-done.19) | copy-start | bytes 393220
  407.2 54.9 %copy-start.14 = (f32[512,256]{1,0:T(8,128)S(1)}, f32[512,256]{1,0:T(8,128)}, u32[]{:S(2)}) copy-start(f32[512,256]{1,0:T(8,128)} %get-tuple-element.192) | copy-start | bytes 1572868
  483.4 9.5 %collective-permute-start.11 = (f32[16,1536]{1,0:T(8,128)}, f32[16,1536]{1,0:T(8,128)}, u32[]{:S(2)}, u32[]{:S(2)}) collective-permute-start(f32[16,1536]{1,0:T(8,128)} %slice.334), channel_id=1, source_target_pairs={{1,0},{2,1},{3,2},{4,3},{5,4},{6,5},{7,6},{9,8},{10,9},{11,10},{12... | collective-permute-start | bytes 294920 | tf_op jit(solution)/shard_map/ppermute | solution.py:1007
  487.7 15.6 %collective-permute-start.14 = (bf16[528,3072]{1,0:T(8,128)(2,1)}, bf16[528,3072]{1,0:T(8,128)(2,1)}, u32[]{:S(2)}, u32[]{:S(2)}) collective-permute-start(bf16[528,3072]{1,0:T(8,128)(2,1)} %get-tuple-element.83), channel_id=1, source_target_pairs={{0,8},{8,0},{16,24},{24,16},{1,9},{9,1},{17,25},{25,17},{2,10},{10... | collective-permute-start | bytes 9732104 | tf_op jit(solution)/shard_map/ppermute | solution.py:1210
  490.7 7.9 %collective-permute-start.13 = (bf16[528,384]{0,1:T(8,128)(2,1)S(1)}, bf16[528,384]{0,1:T(8,128)(2,1)S(1)}, u32[]{:S(2)}, u32[]{:S(2)}) collective-permute-start(bf16[528,384]{0,1:T(8,128)(2,1)S(1)} %bitcast.209), channel_id=1, source_target_pairs={{0,8},{8,0},{16,24},{24,16},{1,9},{9,1},{17,25},{25,17},{2,10},{10... | collective-permute-start | bytes 1216520 | tf_op jit(solution)/shard_map/ppermute | solution.py:1210
  (72 other events, 468.1 us)
Sparse Core Ops, SparseCore 0:
  11.6 164.4 all-gather.2
  334.2 212.0 reduce-scatter.1

commit v4 on v3

v4 whole, which is shorter than its diff:
```python
import functools

import jax
import jax.numpy as jnp
from jax import lax
from jax.experimental import pallas as pl
from jax.experimental.pallas import tpu as pltpu
from jax.sharding import PartitionSpec as P

EPSILON = 1e-05
CHUNK = 128
HALO = 16
AHEAD = 2
LAGS = (0, 1, 3, 5)
CHUNK_ROWS = 48
MASKED = -1e30
HIGHEST = lax.Precision.HIGHEST
SEQ = ("head", "tensor")
ALL = ("dp", "head", "tensor")
BF16 = jnp.bfloat16
F32 = jnp.float32
MESH = pl.DeviceIdType.MESH
VMEM_BYTES = 56 << 20


def coordinates():
    dp = lax.axis_index("dp")
    return lax.div(dp, 2), lax.rem(dp, 2), lax.axis_index("head"), lax.axis_index("tensor")


def enter_kernel(x, core, head, tensor, xs, hs, ts, sibling):
    barrier = pltpu.get_barrier_semaphore()
    count = 0
    for step in range(1, hs):
        pl.semaphore_signal(barrier, 1, device_id={"head": lax.rem(head + step, hs)}, device_id_type=MESH)
        count += 1
    for step in range(1, ts):
        pl.semaphore_signal(barrier, 1, device_id={"tensor": lax.rem(tensor + step, ts)}, device_id_type=MESH)
        count += 1
    for step in range(1, xs):
        other = 2 * lax.rem(x + step, xs) + core
        pl.semaphore_signal(barrier, 1, device_id={"dp": other}, device_id_type=MESH)
        count += 1
    if sibling:
        pl.semaphore_signal(barrier, 1, device_id={"dp": 2 * x + 1 - core}, device_id_type=MESH)
        count += 1
    pl.semaphore_wait(barrier, count)


def gatherer(sizes, chunks, parts, fulls, sems):
    xs, hs, ts = sizes
    send, recv, own_sem = sems
    x, core, head, tensor = coordinates()
    dp = 2 * x + core
    total = len(chunks)
    ahead = 4

    def own():
        return [
            pltpu.make_async_copy(part, full.at[dp, head, tensor], own_sem.at[kind])
            for kind, (part, full) in enumerate(zip(parts, fulls))
        ]

    def copy(src, dst, index, slot, device):
        return pltpu.make_async_remote_copy(
            src_ref=src,
            dst_ref=dst,
            send_sem=send.at[index, slot],
            recv_sem=recv.at[index, slot],
            device_id=device,
            device_id_type=MESH,
        )

    def along_head(index):
        kind, start, length, _ = chunks[index]
        rows = pl.ds(start, length)
        return [
            copy(
                parts[kind].at[rows],
                fulls[kind].at[dp, head, tensor, rows],
                index,
                step - 1,
                {"head": lax.rem(head + step, hs)},
            )
            for step in range(1, hs)
        ]

    def over(index, axis, second):
        kind, start, length, _ = chunks[index]
        rows = pl.ds(start, length)
        base = hs - 1 if second else hs - 1 + max(xs, ts)
        copies = []
        if axis == "tensor":
            homes = [dp] if second else [2 * home + core for home in range(xs)]
            for step in range(1, ts):
                for home in homes:
                    view = fulls[kind].at[home, :, tensor, rows]
                    device = {"tensor": lax.rem(tensor + step, ts)}
                    copies.append(copy(view, view, index, base + len(copies), device))
        else:
            for step in range(1, xs):
                view = fulls[kind].at[dp, :, tensor, rows] if second else fulls[kind].at[dp, :, :, rows]
                device = {"dp": 2 * lax.rem(x + step, xs) + core}
                copies.append(copy(view, view, index, base + len(copies), device))
        return copies

    def to_sibling(index):
        kind, start, length, _ = chunks[index]
        rows = pl.ds(start, length)
        base = hs - 1 + max(xs, ts) + max(xs, xs * ts)
        return [
            copy(
                fulls[kind].at[2 * home + core, :, :, rows],
                fulls[kind].at[2 * home + core, :, :, rows],
                index,
                base + home,
                {"dp": 2 * x + 1 - core},
            )
            for home in range(xs)
        ]

    def stage(index, number):
        tensor_first = chunks[index][3]
        if number == 0:
            return along_head(index)
        if number == 1:
            return over(index, "tensor" if tensor_first else "x", True)
        if number == 2:
            return over(index, "x" if tensor_first else "tensor", False)
        return to_sibling(index)

    def start(first):
        if first:
            for one in own():
                one.start()
        else:
            for index in range(min(ahead, total)):
                for one in stage(index, 0):
                    one.start()
            for one in own():
                one.wait()

    def tick(at):
        for number in range(4):
            index = at - 2 * number
            if 0 <= index < total:
                for one in stage(index, number):
                    one.wait_recv()
                if number < 3:
                    for one in stage(index, number + 1):
                        one.start()
                if number == 0 and index + ahead < total:
                    for one in stage(index + ahead, 0):
                        one.start()

    def end():
        for index in range(total):
            for number in range(4):
                for one in stage(index, number):
                    one.wait_send()

    return start, tick, end, total + 6


def gatherer_scratch(sizes, chunks, kinds):
    xs, hs, ts = sizes
    slots = hs - 1 + max(xs, ts) + max(xs, xs * ts) + xs
    return [
        pltpu.SemaphoreType.DMA((len(chunks), slots)),
        pltpu.SemaphoreType.DMA((len(chunks), slots)),
        pltpu.SemaphoreType.DMA((kinds,)),
    ]


def gather_kernel(sizes, chunks, kinds, *refs):
    xs, hs, ts = sizes
    parts, small = refs[:kinds], refs[kinds]
    fulls, small_full = refs[kinds + 1 : 2 * kinds + 1], refs[2 * kinds + 1]
    sems, rest = refs[2 * kinds + 2 : 2 * kinds + 5], refs[2 * kinds + 5 :]
    small_send, small_recv, small_own = rest
    x, core, head, tensor = coordinates()
    begin, step_on, end, ticks = gatherer(sizes, chunks, parts, fulls, sems)
    begin(True)
    own_small = pltpu.make_async_copy(small, small_full.at[head, tensor], small_own.at[0])
    own_small.start()
    enter_kernel(x, core, head, tensor, xs, hs, ts, True)
    small_tensor = [
        pltpu.make_async_remote_copy(
            src_ref=small,
            dst_ref=small_full.at[head, tensor],
            send_sem=small_send.at[step - 1],
            recv_sem=small_recv.at[step - 1],
            device_id={"tensor": lax.rem(tensor + step, ts)},
            device_id_type=MESH,
        )
        for step in range(1, ts)
    ]
    small_head = [
        pltpu.make_async_remote_copy(
            src_ref=small_full.at[head],
            dst_ref=small_full.at[head],
            send_sem=small_send.at[ts + step - 2],
            recv_sem=small_recv.at[ts + step - 2],
            device_id={"head": lax.rem(head + step, hs)},
            device_id_type=MESH,
        )
        for step in range(1, hs)
    ]
    for one in small_tensor:
        one.start()
    begin(False)
    own_small.wait()
    for one in small_tensor:
        one.wait_recv()
    for one in small_head:
        one.start()
    for tick in range(ticks):
        step_on(tick)
    for one in small_head:
        one.wait_recv()
    for one in small_tensor + small_head:
        one.wait_send()
    end()


def row_chunks(rows, first, kinds, pieces):
    step = rows // pieces
    return [
        (kind, piece * step, step, piece % 2 == 1)
        for kind in range(first, kinds)
        for piece in range(pieces)
    ]


def gather_weights(parts, small, sizes):
    xs, hs, ts = sizes
    kinds = len(parts)
    count = parts[1].shape[0]
    chunks = [(0, 0, parts[0].shape[0], True)] + row_chunks(count, 1, kinds, count // CHUNK_ROWS)
    full = [jax.ShapeDtypeStruct((2 * xs, hs, ts) + part.shape, part.dtype) for part in parts]
    full.append(jax.ShapeDtypeStruct((hs, ts) + small.shape, small.dtype))
    anywhere = pl.BlockSpec(memory_space=pl.ANY)
    return pl.pallas_call(
        functools.partial(gather_kernel, sizes, chunks, kinds),
        out_shape=full,
        in_specs=[anywhere] * (kinds + 1),
        out_specs=[anywhere] * (kinds + 1),
        scratch_shapes=gatherer_scratch(sizes, chunks, kinds)
        + [
            pltpu.SemaphoreType.DMA((hs + ts,)),
            pltpu.SemaphoreType.DMA((hs + ts,)),
            pltpu.SemaphoreType.DMA((1,)),
        ],
        compiler_params=pltpu.CompilerParams(
            collective_id=0, has_side_effects=True, vmem_limit_bytes=VMEM_BYTES
        ),
        cost_estimate=busy(60),
    )(*parts, small)


def reducer(sizes, chunks, parts, bufs, sems, put):
    xs, hs, ts = sizes
    send, recv, own_sem = sems
    x, core, head, tensor = coordinates()
    total = len(chunks)

    def loads(index):
        kind, start, length, _ = chunks[index]
        rows = pl.ds(start, length)
        return [
            pltpu.make_async_copy(
                parts[kind].at[2 * home + core, :, :, rows],
                bufs[5 * index].at[home],
                own_sem.at[index, home],
            )
            for home in range(xs)
        ]

    def stage(index, number):
        kind, start, length, x_first = chunks[index]
        rows = pl.ds(start, length)
        held = bufs[5 * index]
        into = bufs[5 * index + 1 + number]
        slots = (0, xs, xs + max(xs, ts) - 1, xs + 2 * (max(xs, ts) - 1))
        by_x = [
            (lax.rem(x + step, xs), {"dp": 2 * lax.rem(x + step, xs) + core}) for step in range(1, xs)
        ]
        by_tensor = [
            (lax.rem(tensor + step, ts), {"tensor": lax.rem(tensor + step, ts)}) for step in range(1, ts)
        ]
        if number == 0:
            moves = [
                (parts[kind].at[2 * home + 1 - core, :, :, rows], into.at[home], {"dp": 2 * x + 1 - core})
                for home in range(xs)
            ]
        elif number == 1 and x_first:
            moves = [(held.at[to], into.at[at], device) for at, (to, device) in enumerate(by_x)]
        elif number == 1:
            moves = [(held.at[:, :, to], into.at[at], device) for at, (to, device) in enumerate(by_tensor)]
        elif number == 2 and x_first:
            moves = [(held.at[x, :, to], into.at[at], device) for at, (to, device) in enumerate(by_tensor)]
        elif number == 2:
            moves = [(held.at[to, :, tensor], into.at[at], device) for at, (to, device) in enumerate(by_x)]
        else:
            moves = []
            for step in range(1, hs):
                to = lax.rem(head + step, hs)
                moves.append((held.at[x, to, tensor], into.at[step - 1], {"head": to}))
        return [
            pltpu.make_async_remote_copy(
                src_ref=src,
                dst_ref=dst,
                send_sem=send.at[index, slots[number] + at],
                recv_sem=recv.at[index, slots[number] + at],
                device_id=device,
                device_id_type=MESH,
            )
            for at, (src, dst, device) in enumerate(moves)
        ]

    def add(index, number):
        kind, start, length, x_first = chunks[index]
        held = bufs[5 * index]
        into = bufs[5 * index + 1 + number]
        if number == 0:

            @pl.loop(0, xs * hs)
            def _(both):
                one, two = lax.div(both, hs), lax.rem(both, hs)
                value = held[one, two].astype(F32) + into[one, two].astype(F32)
                held[one, two] = value.astype(BF16)

        elif number == 1 and x_first:

            @pl.loop(0, hs)
            def _(one):
                value = held[x, one].astype(F32)
                for step in range(xs - 1):
                    value = value + into[step, one].astype(F32)
                held[x, one] = value.astype(BF16)

        elif number == 1:

            @pl.loop(0, xs * hs)
            def _(both):
                one, two = lax.div(both, hs), lax.rem(both, hs)
                value = held[one, two, tensor].astype(F32)
                for step in range(ts - 1):
                    value = value + into[step, one, two].astype(F32)
                held[one, two, tensor] = value.astype(BF16)

        elif number == 2:

            @pl.loop(0, hs)
            def _(one):
                value = held[x, one, tensor].astype(F32)
                for step in range(into.shape[0]):
                    value = value + into[step, one].astype(F32)
                held[x, one, tensor] = value.astype(BF16)

        else:
            value = held[x, head, tensor].astype(F32)
            for step in range(hs - 1):
                value = value + into[step].astype(F32)
            put(kind, start, length, value)

    def start(first):
        for index in range(total):
            if first:
                for one in loads(index):
                    one.start()
            elif index < AHEAD:
                for one in stage(index, 0):
                    one.start()

    def tick(at):
        for number, lag in enumerate(LAGS):
            index = at - lag
            if 0 <= index < total:
                for one in stage(index, number):
                    one.wait_recv()
                if number == 0:
                    if index + AHEAD < total:
                        for one in stage(index + AHEAD, 0):
                            one.start()
                    for one in loads(index):
                        one.wait()
                add(index, number)
                if number < 3:
                    for one in stage(index, number + 1):
                        one.start()

    def end():
        for index in range(total):
            for number in range(4):
                for one in stage(index, number):
                    one.wait_send()

    return start, tick, end, total + LAGS[3]


def reducer_scratch(sizes, chunks, parts):
    xs, hs, ts = sizes
    scratch = []
    for kind, _, length, x_first in chunks:
        block = (length, parts[kind].shape[4])
        kept = (hs, ts) if x_first else (xs, hs)
        near, far = (xs, ts) if x_first else (ts, xs)
        scratch += [
            pltpu.VMEM((xs, hs, ts) + block, BF16),
            pltpu.VMEM((xs, hs, ts) + block, BF16),
            pltpu.VMEM((near - 1,) + kept + block, BF16),
            pltpu.VMEM((far - 1, hs) + block, BF16),
            pltpu.VMEM((hs - 1,) + block, BF16),
        ]
    slots = xs + 2 * (max(xs, ts) - 1) + hs - 1
    return scratch + [
        pltpu.SemaphoreType.DMA((len(chunks), slots)),
        pltpu.SemaphoreType.DMA((len(chunks), slots)),
        pltpu.SemaphoreType.DMA((len(chunks), xs)),
    ]


def scatter_kernel(sizes, chunks, kinds, *refs):
    xs, hs, ts = sizes
    parts, small = refs[:kinds], refs[kinds]
    outs, small_out = refs[kinds + 1 : 2 * kinds + 1], refs[2 * kinds + 1]
    rest = refs[2 * kinds + 2 :]
    count = 5 * len(chunks)
    bufs, sems, rest = rest[:count], rest[count : count + 3], rest[count + 3 :]
    small_acc, small_in, small_send, small_recv, side_send, side_recv = rest
    x, core, head, tensor = coordinates()

    def put(kind, start, length, value):
        if kind == 0:
            outs[kind][head, tensor] = value.astype(BF16)
        else:
            outs[kind][start : start + length, :] = value

    begin, step_on, end, ticks = reducer(sizes, chunks, parts, bufs, sems, put)

    def side_copy(view, slot, device):
        return pltpu.make_async_remote_copy(
            src_ref=view,
            dst_ref=view,
            send_sem=side_send.at[slot],
            recv_sem=side_recv.at[slot],
            device_id=device,
            device_id_type=MESH,
        )

    side_tensor = [
        side_copy(outs[0].at[head, tensor], step - 1, {"tensor": lax.rem(tensor + step, ts)})
        for step in range(1, ts)
    ]
    side_head = [
        side_copy(outs[0].at[head], ts + step - 2, {"head": lax.rem(head + step, hs)})
        for step in range(1, hs)
    ]
    small_slots = [1, xs - 1, ts - 1, hs - 1]
    small_base = [0, 1, xs, xs + ts - 1]

    def small_stage(number):
        copies = []
        for step in range(1, small_slots[number] + 1):
            slot = small_base[number] + step - 1
            device = (
                {"dp": 2 * x + 1 - core},
                {"dp": 2 * lax.rem(x + step, xs) + core},
                {"tensor": lax.rem(tensor + step, ts)},
                {"head": lax.rem(head + step, hs)},
            )[number]
            copies.append(
                pltpu.make_async_remote_copy(
                    src_ref=small if number == 0 else small_acc.at[number - 1],
                    dst_ref=small_in.at[slot],
                    send_sem=small_send.at[slot],
                    recv_sem=small_recv.at[slot],
                    device_id=device,
                    device_id_type=MESH,
                )
            )
        return copies

    def small_add(number):
        mine = small[...] if number == 0 else small_acc[number - 1]
        size = small_slots[number] + 1
        place = (core, x, tensor, head)[number]
        value = None
        for at in range(size):
            step = lax.rem(place - at + size, size)
            slot = small_base[number] + jnp.maximum(step - 1, 0)
            here = jnp.where(step == 0, mine, small_in[slot])
            value = here if value is None else value + here
        if number < 3:
            small_acc[number] = value
        else:
            small_out[...] = value

    begin(True)
    enter_kernel(x, core, head, tensor, xs, hs, ts, True)
    for one in small_stage(0):
        one.start()
    begin(False)
    for tick in range(max(ticks, 9)):
        step_on(tick)
        if tick == 5:
            for one in side_tensor:
                one.start()
        if tick == 7:
            for one in side_tensor:
                one.wait_recv()
            for one in side_head:
                one.start()
        if tick in (0, 2, 4, 6):
            number = tick // 2
            for one in small_stage(number):
                one.wait_recv()
            small_add(number)
            if number < 3:
                for one in small_stage(number + 1):
                    one.start()
    for one in side_head:
        one.wait_recv()
    for one in side_tensor + side_head:
        one.wait_send()
    for number in range(4):
        for one in small_stage(number):
            one.wait_send()
    end()


def scatter_gradients(parts, small, sizes):
    xs, hs, ts = sizes
    kinds = len(parts)
    count = parts[1].shape[3]
    chunks = [(0, 0, parts[0].shape[3], True)] + row_chunks(count, 1, kinds, count // CHUNK_ROWS)
    small_slots = xs + ts + hs - 2
    anywhere = pl.BlockSpec(memory_space=pl.ANY)
    whole = pl.BlockSpec(memory_space=pltpu.VMEM)
    return pl.pallas_call(
        functools.partial(scatter_kernel, sizes, chunks, kinds),
        out_shape=[jax.ShapeDtypeStruct((hs, ts) + parts[0].shape[3:], BF16)]
        + [jax.ShapeDtypeStruct(part.shape[3:], F32) for part in parts[1:]]
        + [jax.ShapeDtypeStruct(small.shape, F32)],
        in_specs=[anywhere] * kinds + [whole],
        out_specs=[whole] * (kinds + 1),
        scratch_shapes=reducer_scratch(sizes, chunks, parts)
        + [
            pltpu.VMEM((3,) + small.shape, F32),
            pltpu.VMEM((small_slots,) + small.shape, F32),
            pltpu.SemaphoreType.DMA((small_slots,)),
            pltpu.SemaphoreType.DMA((small_slots,)),
            pltpu.SemaphoreType.DMA((hs + ts,)),
            pltpu.SemaphoreType.DMA((hs + ts,)),
        ],
        compiler_params=pltpu.CompilerParams(
            collective_id=1, has_side_effects=True, vmem_limit_bytes=VMEM_BYTES
        ),
        cost_estimate=busy(60),
    )(*parts, small)


def exchange_kernel(sizes, forward, chunks, *refs):
    xs, hs, ts = sizes
    size = hs * ts
    hosts = bool(chunks)
    local, keep = refs[:2]
    parts, out = refs[2 : 2 + hosts], refs[2 + hosts]
    outs, rest = refs[3 + hosts : 3 + 2 * hosts], refs[3 + 2 * hosts :]
    got, keeps, sums, sems, keep_sems, back_sems = rest[:6]
    x, core, head, tensor = coordinates()
    me = head * ts + tensor

    def put(kind, start, length, value):
        outs[kind][start : start + length, :] = value

    ticks = 0
    if hosts:
        begin, step_on, end, ticks = reducer(sizes, chunks, parts, rest[6:-3], rest[-3:], put)
        begin(True)
    barrier = pltpu.get_barrier_semaphore()
    peers = []
    for step in range(1, size):
        to = lax.rem(me + step, size)
        peers.append((to, {"head": lax.div(to, ts), "tensor": lax.rem(to, ts)}))
    others = [device for _, device in peers]
    if hosts:
        others += [{"dp": 2 * lax.rem(x + step, xs) + core} for step in range(1, xs)]
        others.append({"dp": 2 * x + 1 - core})
    for device in others:
        pl.semaphore_signal(barrier, 1, device_id=device, device_id_type=MESH)
    pl.semaphore_wait(barrier, len(others))

    def copies(src, dst, pair):
        return [
            pltpu.make_async_remote_copy(
                src_ref=src.at[to],
                dst_ref=dst.at[me],
                send_sem=pair.at[0, at],
                recv_sem=pair.at[1, at],
                device_id=device,
                device_id_type=MESH,
            )
            for at, (to, device) in enumerate(peers)
        ]

    factors = copies(keep, keeps, keep_sems)
    states = copies(local, got, sems)
    for one in factors + states:
        one.start()
    if hosts:
        begin(False)
    got[me] = local[me]
    keeps[me] = keep[me]
    for tick in range(min(3, ticks)):
        step_on(tick)
    for one in factors + states:
        one.wait_recv()
    third = lax.broadcasted_iota(jnp.int32, (keep.shape[1], local.shape[2]), 0) < 3
    third = third.astype(BF16)
    held = jnp.zeros(local.shape[1:], F32)
    order = range(size) if forward else range(size - 1, -1, -1)
    for at in order:
        sums[at] = held.astype(BF16)
        held = got[at].astype(F32) + dot_tn(keeps[at], third) * held
    back = copies(sums, out, back_sems)
    for one in back:
        one.start()
    out[me] = sums[me]
    for tick in range(3, ticks):
        step_on(tick)
    for one in back:
        one.wait_recv()
    for one in factors + states + back:
        one.wait_send()
    if hosts:
        end()


def exchange_states(local, keep, sizes, forward, parts=()):
    _, hs, ts = sizes
    size = hs * ts
    inner, state = local.shape
    blocks = (size, inner // size, state)
    whole = pl.BlockSpec(memory_space=pltpu.VMEM)
    anywhere = pl.BlockSpec(memory_space=pl.ANY)
    pair = pltpu.SemaphoreType.DMA((2, size))
    chunks, scratch = [], []
    if parts:
        count = parts[0].shape[3]
        chunks = row_chunks(count, 0, 1, count // CHUNK_ROWS)
        scratch = reducer_scratch(sizes, chunks, parts)
    out = pl.pallas_call(
        functools.partial(exchange_kernel, sizes, forward, chunks),
        out_shape=[jax.ShapeDtypeStruct(blocks, BF16)]
        + [jax.ShapeDtypeStruct(part.shape[3:], F32) for part in parts],
        in_specs=[whole, whole] + [anywhere] * len(parts),
        out_specs=[whole] * (1 + len(parts)),
        scratch_shapes=[
            pltpu.VMEM(blocks, BF16),
            pltpu.VMEM(keep.shape, BF16),
            pltpu.VMEM(blocks, BF16),
            pair,
            pair,
            pair,
        ]
        + scratch,
        compiler_params=pltpu.CompilerParams(
            collective_id=2 if forward else 3, has_side_effects=True, vmem_limit_bytes=VMEM_BYTES
        ),
        cost_estimate=busy(60),
    )(local.reshape(blocks), keep, *parts)
    return (out[0].reshape(inner, state),) + tuple(out[1:])


def group_of(cols):
    return 1 if cols % 128 == 0 else 128 // cols if 128 % cols == 0 else 2


def busy(microseconds):
    return pl.CostEstimate(flops=microseconds * 900_000_000, bytes_accessed=0, transcendentals=0)


def local_params():
    return pltpu.CompilerParams(vmem_limit_bytes=VMEM_BYTES)


def silu_of(v):
    return v * jax.nn.sigmoid(v)


def dot_nt(left, right):
    return lax.dot_general(left, right, (((1,), (1,)), ((), ())), preferred_element_type=F32)


def dot_tn(left, right):
    return lax.dot_general(left, right, (((0,), (0,)), ((), ())), preferred_element_type=F32)


def dot_nn(left, right):
    return jnp.dot(left, right, preferred_element_type=F32)


def dot_exact(left, right):
    return jnp.dot(left, right, preferred_element_type=F32, precision=HIGHEST)


def thirds(v):
    high = v.astype(BF16)
    rest = v - high.astype(F32)
    middle = rest.astype(BF16)
    return high, middle, (rest - middle.astype(F32)).astype(BF16)


def places(shape):
    return lax.broadcasted_iota(jnp.int32, shape, 0), lax.broadcasted_iota(jnp.int32, shape, 1)


def one_hot(hit):
    return hit.astype(F32).astype(BF16)


def conv_pre(ext_ref, taps_ref, same_ref, own, width):
    total = taps_ref[width : width + 1] + taps_ref[width - 1 : width] * ext_ref[HALO:]
    for back in range(1, width):
        total = total + (
            taps_ref[width - 1 - back : width - back]
            * ext_ref[HALO - back : HALO - back + own]
            * same_ref[:, back - 1 : back]
        )
    return total


def lane_masks():
    lane = lax.broadcasted_iota(jnp.int32, (1, 128), 1)
    first = (lane < 64).astype(F32)
    return first, 1.0 - first


def two_apart(pair, masks):
    return jnp.concatenate([pair * masks[0].astype(BF16), pair * masks[1].astype(BF16)], 0)


def decay_pair(cum_ref, cumt_ref, bias, rows, pair):
    parts = []
    for head in (2 * pair, 2 * pair + 1):
        spread = cum_ref[0, rows, head : head + 1] - cumt_ref[0, head : head + 1, rows] + bias
        parts.append(jnp.exp(spread))
    return parts


class Scan:
    def __init__(self, own, sizes, rows, cols, heads_own, taps):
        self.own, self.ext, self.taps = own, own + HALO, taps
        self.dps, self.hts = 2 * sizes[0], sizes[1] * sizes[2]
        self.rows, self.cols = rows, cols
        self.group = group_of(cols)
        self.wide = self.group * cols
        self.heads = self.group * heads_own
        self.groups = self.hts // self.group
        self.chunks = own // CHUNK
        self.width = self.dps * rows
        self.inner = self.hts * cols
        self.pairs = self.wide // 128

    def call(self, kernel, ins, outs, scratch=()):
        arrays = [array for array, _ in ins]
        return pl.pallas_call(
            kernel,
            grid=(self.groups,),
            out_shape=[shape for shape, _ in outs],
            in_specs=[spec for _, spec in ins],
            out_specs=[spec for _, spec in outs],
            scratch_shapes=list(scratch),
            compiler_params=local_params(),
            cost_estimate=busy(22),
        )(*arrays)

    def full(self, array):
        return (array, pl.BlockSpec(array.shape, lambda j: (0,) * array.ndim))

    def pieces(self, array):
        block = (self.dps, self.group, self.rows, self.cols)
        return (array, pl.BlockSpec(block, lambda j: (0, j, 0, 0)))

    def lanes(self, array):
        lead = array.shape[:-1]
        return (array, pl.BlockSpec(lead + (self.wide,), lambda j: (0,) * len(lead) + (j,)))

    def states(self, array):
        lead = array.shape[:-2]
        block = lead + (self.wide, array.shape[-1])
        return (array, pl.BlockSpec(block, lambda j: (0,) * len(lead) + (j, 0)))

    def grouped(self, array):
        block = (1,) + array.shape[1:]
        return (array, pl.BlockSpec(block, lambda j: (j,) + (0,) * (array.ndim - 1)))

    def project(self, rows_ref, piece_ref, out_ref):
        for one in range(self.group):
            weights = piece_ref[:, one].reshape(self.width, self.cols)
            out_ref[:, one * self.cols : (one + 1) * self.cols] = dot_nn(rows_ref, weights)

    def project_back(self, value_ref, piece_ref, out_ref):
        @pl.when(pl.program_id(0) == 0)
        def _():
            out_ref[...] = jnp.zeros_like(out_ref)

        for one in range(self.group):
            weights = piece_ref[:, one].reshape(self.width, self.cols)
            out_ref[...] += dot_nt(value_ref[:, one * self.cols : (one + 1) * self.cols], weights)

    def chunk_rows(self, c):
        return slice(c * CHUNK, (c + 1) * CHUNK)

    def lane_sums(self, v):
        total = v[:, :128]
        for pair in range(1, self.pairs):
            total = total + v[:, pair * 128 : (pair + 1) * 128]
        return total

    def widen(self):
        count = self.heads * self.groups
        row, lane = places((3 * count, self.wide))
        row = row - jnp.where(row >= 2 * count, 2 * count, jnp.where(row >= count, count, 0))
        return one_hot(row == pl.program_id(0) * self.heads + lax.div(lane, 64))

    def heads_of(self):
        row, lane = places((self.wide, 128))
        return one_hot(lane == pl.program_id(0) * self.heads + lax.div(row, 64))

    def keep_columns(self, keep_ref, widen):
        return dot_tn(widen, keep_ref[...])

    def halves(self, v):
        high = v.astype(BF16)
        return high, (v - high.astype(F32)).astype(BF16)

    def head_sums(self, v, heads_of):
        high, low = self.halves(v)
        return dot_nn(high, heads_of) + dot_nn(low, heads_of)

    def gradient(self, left_ref, value_ref, out_ref):
        for at in range(self.dps):
            for one in range(self.group):
                value = value_ref[:, one * self.cols : (one + 1) * self.cols]
                out_ref[at, one] = dot_nn(left_ref[at], value).astype(BF16)

    def piece_shape(self):
        return jax.ShapeDtypeStruct((self.dps, self.hts, self.rows, self.cols), BF16)

    def s1(self, normed, w_x, conv_rows, same, dt3, tail3, cum_g, cumt_g, coupling, bias, bc, keep3):
        own, state = self.own, bc.shape[1] // 2

        def kernel(
            normed_ref, w_ref, conv_ref, same_ref, dt_ref, tail_ref, cum_ref, cumt_ref,
            coupling_ref, bias_ref, bc_ref, keep_ref, ext_ref, x_ref, within_ref, added_ref, local_ref, xd_ref, xt_ref,
        ):
            self.project(normed_ref[...], w_ref, ext_ref)
            widen = self.widen()
            keep = self.keep_columns(keep_ref, widen)
            x = silu_of(conv_pre(ext_ref, conv_ref, same_ref, own, self.taps))
            x_ref[...] = x
            xd = x * dot_nn(dt_ref[...], widen)
            xd_ref[...] = xd.astype(BF16)
            xt_ref[...] = (xd * dot_nn(tail_ref[...], widen)).astype(BF16)
            masks = lane_masks()
            held = None
            for c in range(self.chunks):
                rows = self.chunk_rows(c)
                for pair in range(self.pairs):
                    lanes = slice(pair * 128, (pair + 1) * 128)
                    first, second = decay_pair(cum_ref, cumt_ref, bias_ref[c], rows, pair)
                    mix = coupling_ref[c]
                    kernel16 = jnp.concatenate([(first * mix).astype(BF16), (second * mix).astype(BF16)], 1)
                    within_ref[rows, lanes] = dot_nn(kernel16, two_apart(xd_ref[rows, lanes], masks))
                added = dot_tn(xt_ref[rows], bc_ref[rows, :state])
                added_ref[c] = added
                held = added if held is None else added + keep[:, c : c + 1] * held
            local_ref[...] = held.astype(BF16)

        f = jax.ShapeDtypeStruct
        return self.call(
            kernel,
            [
                self.full(normed), self.pieces(w_x), self.lanes(conv_rows), self.full(same), self.full(dt3),
                self.full(tail3), self.grouped(cum_g), self.grouped(cumt_g),
                self.full(coupling), self.full(bias), self.full(bc), self.full(keep3),
            ],
            [
                self.lanes(f((self.ext, self.inner), F32)), self.lanes(f((own, self.inner), F32)),
                self.lanes(f((own, self.inner), F32)), self.states(f((self.chunks, self.inner, state), F32)),
                self.states(f((self.inner, state), BF16)),
            ],
            [pltpu.VMEM((own, self.wide), BF16), pltpu.VMEM((own, self.wide), BF16)],
        )

    def s2(self, normed_own, w_z, within, x, skip_rows, entry3, bc, entering, added, keep3):
        own, state = self.own, bc.shape[1] // 2

        def kernel(
            normed_ref, w_ref, within_ref, x_ref, skip_ref, entry_ref, bc_ref, entering_ref,
            added_ref, keep_ref, z_ref, y_ref, states_ref, squares_ref,
        ):
            self.project(normed_ref[...], w_ref, z_ref)
            widen = self.widen()
            keep = self.keep_columns(keep_ref, widen)
            entry = dot_nn(entry_ref[...], widen)
            held = entering_ref[...].astype(F32)
            for c in range(self.chunks):
                rows = self.chunk_rows(c)
                held16 = held.astype(BF16)
                states_ref[c] = held16
                carried = dot_nt(bc_ref[rows, state:], held16)
                y_ref[rows] = within_ref[rows] + carried * entry[rows] + skip_ref[...] * x_ref[rows]
                if c + 1 < self.chunks:
                    held = added_ref[c] + keep[:, c : c + 1] * held
            gated = y_ref[...] * silu_of(z_ref[...])
            squares = self.lane_sums(gated * gated)

            @pl.when(pl.program_id(0) == 0)
            def _():
                squares_ref[...] = squares

            @pl.when(pl.program_id(0) > 0)
            def _():
                squares_ref[...] += squares

        f = jax.ShapeDtypeStruct
        return self.call(
            kernel,
            [
                self.full(normed_own), self.pieces(w_z), self.lanes(within), self.lanes(x), self.lanes(skip_rows),
                self.full(entry3), self.full(bc), self.states(entering), self.states(added),
                self.full(keep3),
            ],
            [
                self.lanes(f((own, self.inner), F32)), self.lanes(f((own, self.inner), F32)),
                self.states(f((self.chunks, self.inner, state), BF16)), self.full(f((own, 128), F32)),
            ],
        )

    def inv_gate(self, squares_ref):
        return lax.rsqrt(jnp.sum(squares_ref[...], axis=1, keepdims=True) / self.inner + EPSILON)

    def s3(self, y, z, squares, gain_row, w_o, cotangent, residual, cot_left):
        own = self.own

        def kernel(
            y_ref, z_ref, squares_ref, gain_ref, w_ref, cot_ref, residual_ref, left_ref,
            grad_ref, cross_ref, gain_grad_ref, out_ref, pieces_ref, gated_ref, sum_ref,
        ):
            inv = self.inv_gate(squares_ref)
            gated = y_ref[...] * silu_of(z_ref[...])
            normal = gated * inv
            gated_ref[...] = (normal * gain_ref[...]).astype(BF16)
            self.project_back(gated_ref, w_ref, sum_ref)
            self.gradient(left_ref, gated_ref, pieces_ref)
            self.project(cot_ref[...], w_ref, grad_ref)
            grad = grad_ref[...]
            gain_grad_ref[...] = jnp.broadcast_to(
                jnp.sum(grad * normal, axis=0, keepdims=True), gain_grad_ref.shape
            )
            cross = self.lane_sums(grad * gain_ref[...] * gated)

            @pl.when(pl.program_id(0) == 0)
            def _():
                cross_ref[...] = cross

            @pl.when(pl.program_id(0) > 0)
            def _():
                cross_ref[...] += cross

            @pl.when(pl.program_id(0) == self.groups - 1)
            def _():
                out_ref[...] = (residual_ref[...].astype(F32) + sum_ref[...]).astype(BF16)

        f = jax.ShapeDtypeStruct
        return self.call(
            kernel,
            [
                self.lanes(y), self.lanes(z), self.full(squares), self.lanes(gain_row), self.pieces(w_o),
                self.full(cotangent), self.full(residual), self.full(cot_left),
            ],
            [
                self.lanes(f((own, self.inner), F32)), self.full(f((own, 128), F32)),
                self.lanes(f((8, self.inner), F32)), self.full(f((own, self.width), BF16)),
                self.pieces(self.piece_shape()),
            ],
            [pltpu.VMEM((own, self.wide), BF16), pltpu.VMEM((own, self.width), F32)],
        )

    def s4(self, y, z, squares, cross, gain_row, grad_gate, w_z, entry3, bc, keep3, left):
        own, state = self.own, bc.shape[1] // 2

        def kernel(
            y_ref, z_ref, squares_ref, cross_ref, gain_ref, grad_ref, w_ref, entry_ref, bc_ref,
            keep_ref, left_ref, dy_ref, back_ref, local_ref, through_ref, pieces_ref, low_ref, dye_ref,
        ):
            inv = self.inv_gate(squares_ref)
            cross_mean = jnp.sum(cross_ref[...], axis=1, keepdims=True) / self.inner
            z = z_ref[...]
            gate = jax.nn.sigmoid(z)
            z_gate = z * gate
            y = y_ref[...]
            grad_gated = inv * (grad_ref[...] * gain_ref[...]) - (y * z_gate) * (inv * inv * inv * cross_mean)
            dy = grad_gated * z_gate
            dy_ref[...] = dy
            low_ref[...] = (grad_gated * y * (gate * (1.0 + z * (1.0 - gate)))).astype(BF16)
            self.project_back(low_ref, w_ref, through_ref)
            self.gradient(left_ref, low_ref, pieces_ref)
            widen = self.widen()
            keep = self.keep_columns(keep_ref, widen)
            dye_ref[...] = (dy * dot_nn(entry_ref[...], widen)).astype(BF16)
            held = None
            for c in range(self.chunks - 1, -1, -1):
                rows = self.chunk_rows(c)
                added = dot_tn(dye_ref[rows], bc_ref[rows, state:])
                back_ref[c] = added
                held = added if held is None else added + keep[:, c : c + 1] * held
            local_ref[...] = held.astype(BF16)

        f = jax.ShapeDtypeStruct
        return self.call(
            kernel,
            [
                self.lanes(y), self.lanes(z), self.full(squares), self.full(cross), self.lanes(gain_row),
                self.lanes(grad_gate), self.pieces(w_z), self.full(entry3), self.full(bc),
                self.full(keep3), self.full(left),
            ],
            [
                self.lanes(f((own, self.inner), F32)),
                self.states(f((self.chunks, self.inner, state), F32)), self.states(f((self.inner, state), BF16)),
                self.full(f((own, self.width), F32)), self.pieces(self.piece_shape()),
            ],
            [pltpu.VMEM((own, self.wide), BF16), pltpu.VMEM((own, self.wide), BF16)],
        )

    def s5(
        self, dy, x_ext, within, conv_rows, skip_rows, same, dt3, tail3, entry3, cum_g, cumt_g, coupling,
        bias, bc, states, leaving, back_added, keep3, w_x, left,
    ):
        own, state = self.own, bc.shape[1] // 2
        taps = self.taps

        def kernel(
            dy_ref, ext_ref, within_ref, conv_ref, skip_ref, same_ref, dt_ref, tail_ref, entry_ref,
            cum_ref, cumt_ref, coupling_ref, bias_ref, bc_ref, states_ref, leaving_ref, back_ref, keep_ref,
            w_ref, left_ref, rows_ref, head_ref, dots_ref, dbc_ref, dmix_ref, through_ref, pieces_ref,
            low_ref, xd_ref, xt_ref, dy16_ref, dye_ref, dxd_ref, shift_ref,
        ):
            first_step = pl.program_id(0) == 0

            @pl.when(first_step)
            def _():
                dbc_ref[...] = jnp.zeros_like(dbc_ref)
                dmix_ref[...] = jnp.zeros_like(dmix_ref)
                head_ref[...] = jnp.zeros_like(head_ref)
                dots_ref[...] = jnp.zeros_like(dots_ref)

            widen, heads_of = self.widen(), self.heads_of()
            keep = self.keep_columns(keep_ref, widen)
            pre = conv_pre(ext_ref, conv_ref, same_ref, own, taps)
            gate = jax.nn.sigmoid(pre)
            x = pre * gate
            dt = dot_nn(dt_ref[...], widen)
            tail = dot_nn(tail_ref[...], widen)
            xd = x * dt
            xd_ref[...] = xd.astype(BF16)
            xt_ref[...] = (xd * tail).astype(BF16)
            dy = dy_ref[...]
            dy16_ref[...] = dy.astype(BF16)
            entry = dot_nn(entry_ref[...], widen)
            dye_ref[...] = (dy * entry).astype(BF16)
            masks = lane_masks()
            held = leaving_ref[...].astype(F32)
            for c in range(self.chunks - 1, -1, -1):
                rows = self.chunk_rows(c)
                held16 = held.astype(BF16)
                into16 = states_ref[c]
                product = held * into16.astype(F32)
                high, low = self.halves(product)
                dots_ref[c] += dot_tn(high, heads_of) + dot_tn(low, heads_of)
                spread_back = dot_nt(bc_ref[rows, :state], held16)
                dmix = dmix_ref[c]
                for pair in range(self.pairs):
                    lanes = slice(pair * 128, (pair + 1) * 128)
                    first, second = decay_pair(cum_ref, cumt_ref, bias_ref[c], rows, pair)
                    mix = coupling_ref[c]
                    kernel16 = jnp.concatenate([(first * mix).astype(BF16), (second * mix).astype(BF16)], 1)
                    dy_pair = dy16_ref[rows, lanes]
                    both = dot_tn(kernel16, dy_pair)
                    dxd_ref[rows, lanes] = both[:CHUNK] * masks[0] + both[CHUNK:] * masks[1]
                    dkernel = dot_nt(dy_pair, two_apart(xd_ref[rows, lanes], masks))
                    dmix = dmix + dkernel[:, :CHUNK] * first + dkernel[:, CHUNK:] * second
                dmix_ref[c] = dmix
                dxd_within = dxd_ref[rows]
                carried = dot_nt(bc_ref[rows, state:], into16)
                falls = (
                    dy16_ref[rows].astype(F32) * within_ref[rows]
                    + dye_ref[rows].astype(F32) * carried
                    - xd_ref[rows].astype(F32) * dxd_within
                )
                dxd = dxd_within + tail[rows] * spread_back
                dxd_ref[rows] = dxd
                head_ref[0, rows] += self.head_sums(falls, heads_of)
                head_ref[1, rows] += self.head_sums(xt_ref[rows].astype(F32) * spread_back, heads_of)
                head_ref[2, rows] += self.head_sums(x[rows] * dxd, heads_of)
                dbc_ref[rows, :state] += dot_nn(xt_ref[rows], held16)
                dbc_ref[rows, state:] += dot_nn(dye_ref[rows], into16)
                if c > 0:
                    held = back_ref[c] + keep[:, c : c + 1] * held
            dx = dxd_ref[...] * dt + skip_ref[...] * dy
            grad = dx * (gate * (1.0 + pre * (1.0 - gate)))
            shift_ref[:HALO] = jnp.zeros((HALO, self.wide), F32)
            shift_ref[HALO + own :] = jnp.zeros((HALO, self.wide), F32)
            rows_ref[taps : taps + 1] = jnp.sum(grad, axis=0, keepdims=True)
            rows_ref[taps + 1 : taps + 2] = jnp.sum(dy * x, axis=0, keepdims=True)
            total = None
            for back in range(taps):
                masked = grad if back == 0 else grad * same_ref[:, back - 1 : back]
                shift_ref[HALO : HALO + own] = masked
                tap = conv_ref[taps - 1 - back : taps - back]
                piece = tap * shift_ref[back : back + own + HALO]
                total = piece if total is None else total + piece
                rows_ref[taps - 1 - back : taps - back] = jnp.sum(
                    masked * ext_ref[HALO - back : HALO - back + own], axis=0, keepdims=True
                )
            low_ref[...] = total.astype(BF16)
            self.project_back(low_ref, w_ref, through_ref)
            self.gradient(left_ref, low_ref, pieces_ref)

        f = jax.ShapeDtypeStruct
        scratch16 = pltpu.VMEM((own, self.wide), BF16)
        return self.call(
            kernel,
            [
                self.lanes(dy), self.lanes(x_ext), self.lanes(within), self.lanes(conv_rows), self.lanes(skip_rows),
                self.full(same), self.full(dt3), self.full(tail3), self.full(entry3),
                self.grouped(cum_g), self.grouped(cumt_g), self.full(coupling), self.full(bias),
                self.full(bc), self.states(states), self.states(leaving), self.states(back_added),
                self.full(keep3), self.pieces(w_x), self.full(left),
            ],
            [
                self.lanes(f((8, self.inner), F32)), self.full(f((3, own, 128), F32)),
                self.full(f((self.chunks, state, 128), F32)),
                self.full(f((own, 2 * state), F32)), self.full(f((self.chunks, CHUNK, CHUNK), F32)),
                self.full(f((self.ext, self.width), F32)), self.pieces(self.piece_shape()),
            ],
            [
                pltpu.VMEM((self.ext, self.wide), BF16), scratch16, scratch16, scratch16, scratch16, pltpu.VMEM((own, self.wide), F32),
                pltpu.VMEM((own + 2 * HALO, self.wide), F32),
            ],
        )

    def alone(self, kernel, ins, outs, scratch, microseconds):
        whole = pl.BlockSpec(memory_space=pltpu.VMEM)
        return pl.pallas_call(
            kernel,
            out_shape=outs,
            in_specs=[whole] * len(ins),
            out_specs=[whole] * len(outs),
            scratch_shapes=scratch,
            compiler_params=local_params(),
            cost_estimate=busy(microseconds),
        )(*ins)

    def prepare(self, normed, cotangent, side, seg_col, seg_row, bc_rows, head_rows, bc_cols, heads_own):
        own, taps, chunks = self.own, self.taps, self.chunks
        heads = heads_own * self.hts
        state2 = bc_cols * self.hts
        state = state2 // 2
        wide = self.hts * side.shape[2]

        def kernel(
            normed_ref, cot_ref, side_ref, seg_ref, segr_ref, bcw_ref, headw_ref,
            ext_left_ref, own_left_ref, cot_left_ref, w_ref, bce_ref, bc_ref, same_ref, dt_ref, sig_ref, cum_ref, cumt_ref, dt3_ref, tail3_ref, entry3_ref,
            keep_ref, keep3_ref, send_ref, mix_ref, bias_ref, raw_ref,
        ):
            row, lane = places((heads, self.hts * 16))
            pick = one_hot(lane == lax.div(row, heads_own) * 16 + lax.rem(row, heads_own))
            w_ref[...] = jnp.zeros_like(w_ref)
            for at in range(self.dps):
                cols = slice(at * self.rows, (at + 1) * self.rows)
                ext_left_ref[at] = normed_ref[:, cols].T
                own_left_ref[at] = normed_ref[HALO:, cols].T
                cot_left_ref[at] = cot_ref[:, cols].T
            for at in range(self.dps):
                cols = slice(at * self.rows, (at + 1) * self.rows)
                for one in range(self.hts):
                    w_ref[one * bc_cols : (one + 1) * bc_cols, cols] = side_ref[at, one, :bc_cols]
                padded = jnp.concatenate(
                    [side_ref[at, one, bc_cols : bc_cols + 16] for one in range(self.hts)], 0
                )
                w_ref[state2 : state2 + heads, cols] = dot_nn(pick, padded).astype(BF16)
            bce_ref[...] = dot_nt(normed_ref[...], w_ref[:state2])
            raw_ref[...] = dot_nt(normed_ref[HALO:], w_ref[state2 : state2 + 128])
            mine = seg_ref[HALO:]
            same_ref[...] = jnp.zeros_like(same_ref)
            for back in range(1, taps):
                hit = seg_ref[HALO - back : HALO - back + own] == mine
                same_ref[:, back - 1 : back] = hit.astype(F32)
            bc_ref[...] = silu_of(conv_pre(bce_ref, bcw_ref, same_ref, own, taps)).astype(BF16)
            shifted = raw_ref[:, :heads] + headw_ref[0:1]
            dt = jnp.maximum(shifted, 0.0) + jnp.log1p(jnp.exp(-jnp.abs(shifted)))
            dt_ref[...] = dt
            sig_ref[...] = jax.nn.sigmoid(shifted)
            rate = -jnp.exp(headw_ref[1:2])
            row, lane = places((CHUNK, CHUNK))
            lower = row >= lane
            triangle = lower.astype(F32)

            def put_thirds(ref, rows, v):
                for at, part in enumerate(thirds(v)):
                    ref[rows, at * heads : (at + 1) * heads] = part

            put_thirds(dt3_ref, slice(0, own), dt)
            keep_all = None
            for c in range(chunks):
                rows = self.chunk_rows(c)
                seg = mine[rows]
                before = seg_ref[HALO + c * CHUNK - 1 : HALO + c * CHUNK]
                end = seg_ref[HALO + (c + 1) * CHUNK - 1 : HALO + (c + 1) * CHUNK]
                cum = dot_exact(triangle, dt_ref[rows] * rate)
                last = cum[CHUNK - 1 : CHUNK]
                put_thirds(tail3_ref, rows, jnp.exp(last - cum) * (seg == end).astype(F32))
                put_thirds(entry3_ref, rows, jnp.exp(cum) * (seg == before).astype(F32))
                keep = jnp.exp(last) * (before == end).astype(F32)
                keep_ref[c : c + 1] = keep
                keep_all = keep if keep_all is None else keep_all * keep
                flipped = cum.T
                for j in range(self.groups):
                    cum_ref[j, rows] = cum[:, j * self.heads : (j + 1) * self.heads]
                    cumt_ref[j, :, rows] = flipped[j * self.heads : (j + 1) * self.heads]
                mix_ref[c] = dot_nt(bc_ref[rows, state:], bc_ref[rows, :state])
                bias_ref[c] = jnp.where((seg == segr_ref[0:1, rows]) & lower, 0.0, MASKED)
            keep_ref[chunks:] = jnp.zeros((8 - chunks, heads), F32)
            for at, part in enumerate(thirds(keep_ref[...].T)):
                keep3_ref[at * heads : (at + 1) * heads] = part
            first, second, third = thirds(keep_all)
            row, _ = places((16, heads))
            stacked = jnp.where(
                row == 0,
                first.astype(F32),
                jnp.where(row == 1, second.astype(F32), jnp.where(row == 2, third.astype(F32), 0.0)),
            ).astype(BF16)
            row, lane = places((heads, self.cols))
            for one in range(self.hts):
                spread = one_hot(row == one * heads_own + lax.div(lane, 64))
                send_ref[one] = dot_nn(stacked, spread).astype(BF16)

        f = jax.ShapeDtypeStruct
        return self.alone(
            kernel,
            [normed, cotangent, side, seg_col, seg_row, bc_rows, head_rows],
            [
                f((self.dps, self.rows, self.ext), BF16), f((self.dps, self.rows, own), BF16),
                f((self.dps, self.rows, own), BF16),
                f((wide, self.width), BF16), f((self.ext, state2), F32), f((own, state2), BF16), f((own, 8), F32),
                f((own, heads), F32), f((own, heads), F32), f((self.groups, own, self.heads), F32),
                f((self.groups, self.heads, own), F32), f((own, 3 * heads), BF16), f((own, 3 * heads), BF16),
                f((own, 3 * heads), BF16), f((8, heads), F32), f((3 * heads, 8), BF16),
                f((self.hts, 16, self.cols), BF16), f((chunks, CHUNK, CHUNK), F32), f((chunks, CHUNK, CHUNK), F32),
            ],
            [pltpu.VMEM((own, 128), F32)],
            10,
        )

    def finish(
        self, dbc, dmix, bc, bc_ext, bc_rows, same, head_sums, dots, keep, dt, sig, head_rows, w_side, through,
        own_part, normed,
    ):
        own, taps, chunks = self.own, self.taps, self.chunks
        heads = dt.shape[1]
        state2 = bc.shape[1]
        state = state2 // 2
        wide = w_side.shape[0]

        def kernel(
            dbc_ref, dmix_ref, bc_ref, bce_ref, bcw_ref, same_ref, sums_ref, dots_ref, keep_ref, dt_ref, sig_ref,
            headw_ref, w_ref, through_ref, own_ref, normed_ref,
            part_ref, halo_ref, taps_ref, heads_ref, pieces_ref, low_ref, shift_ref, full_ref,
        ):
            rate = -jnp.exp(headw_ref[1:2])
            row, lane = places((CHUNK, CHUNK))
            upper = (row <= lane).astype(F32)
            strict = (row > lane).astype(F32)
            low_ref[...] = jnp.zeros_like(low_ref)
            grad_shift = jnp.zeros((1, heads), F32)
            grad_log = jnp.zeros((1, heads), F32)
            for c in range(chunks):
                rows = self.chunk_rows(c)
                dmix16 = dmix_ref[c].astype(BF16)
                full_ref[rows, :state] = dbc_ref[rows, :state] + dot_tn(dmix16, bc_ref[rows, state:])
                full_ref[rows, state:] = dbc_ref[rows, state:] + dot_nn(dmix16, bc_ref[rows, :state])
                crossing = jnp.sum(dots_ref[c], axis=0, keepdims=True)[:, :heads]
                da = (
                    dot_exact(upper, sums_ref[0, rows, :heads])
                    + dot_exact(strict, sums_ref[1, rows, :heads])
                    + keep_ref[c : c + 1] * crossing
                )
                grad_log = grad_log + jnp.sum(dt_ref[rows] * da, axis=0, keepdims=True)
                ddt_raw = (sums_ref[2, rows, :heads] + rate * da) * sig_ref[rows]
                grad_shift = grad_shift + jnp.sum(ddt_raw, axis=0, keepdims=True)
                low_ref[HALO + c * CHUNK : HALO + (c + 1) * CHUNK, state2 : state2 + heads] = ddt_raw.astype(BF16)
            heads_ref[...] = jnp.zeros_like(heads_ref)
            heads_ref[0:1] = grad_shift
            heads_ref[1:2] = rate * grad_log
            pre = conv_pre(bce_ref, bcw_ref, same_ref, own, taps)
            gate = jax.nn.sigmoid(pre)
            grad = full_ref[...] * (gate * (1.0 + pre * (1.0 - gate)))
            shift_ref[:HALO] = jnp.zeros((HALO, state2), F32)
            shift_ref[HALO + own :] = jnp.zeros((HALO, state2), F32)
            taps_ref[...] = jnp.zeros_like(taps_ref)
            taps_ref[taps : taps + 1] = jnp.sum(grad, axis=0, keepdims=True)
            total = None
            for back in range(taps):
                masked = grad if back == 0 else grad * same_ref[:, back - 1 : back]
                shift_ref[HALO : HALO + own] = masked
                piece = bcw_ref[taps - 1 - back : taps - back] * shift_ref[back : back + own + HALO]
                total = piece if total is None else total + piece
                taps_ref[taps - 1 - back : taps - back] = jnp.sum(
                    masked * bce_ref[HALO - back : HALO - back + own], axis=0, keepdims=True
                )
            low_ref[:, :state2] = total.astype(BF16)
            part = through_ref[...] + dot_nn(low_ref[...], w_ref[...])
            part_ref[...] = part[HALO:] + own_ref[...]
            halo_ref[...] = part[:HALO]
            for at in range(self.dps):
                cols = slice(at * self.rows, (at + 1) * self.rows)
                pieces_ref[at] = dot_tn(low_ref[...], normed_ref[:, cols]).astype(BF16)

        f = jax.ShapeDtypeStruct
        return self.alone(
            kernel,
            [
                dbc, dmix, bc, bc_ext, bc_rows, same, head_sums, dots, keep, dt, sig, head_rows, w_side, through,
                own_part, normed,
            ],
            [
                f((own, self.width), F32), f((HALO, self.width), F32), f((8, state2), F32), f((8, heads), F32),
                f((self.dps, wide, self.rows), BF16),
            ],
            [
                pltpu.VMEM((self.ext, wide), BF16), pltpu.VMEM((own + 2 * HALO, state2), F32),
                pltpu.VMEM((own, state2), F32),
            ],
            12,
        )


def from_earlier(values, distance, size):
    return lax.ppermute(values, SEQ, [(i, i + distance) for i in range(size - distance)])


def from_later(values, distance, size):
    return lax.ppermute(values, SEQ, [(i + distance, i) for i in range(size - distance)])


def body(
    residual,
    segment_ids,
    norm_in_gain,
    w_zx,
    w_bc,
    w_dt,
    conv_x_weight,
    conv_x_bias,
    conv_bc_weight,
    conv_bc_bias,
    dt_bias,
    a_log,
    d_skip,
    norm_gain,
    w_out,
    cotangent,
):
    own, width = residual.shape
    dp_size = lax.axis_size("dp")
    size = lax.axis_size(SEQ)
    place = lax.axis_index(SEQ)
    dp_rows, _, cols = w_zx.shape
    heads_own = w_dt.shape[1]
    inner = cols * size
    heads = heads_own * size
    state2 = w_bc.shape[1]
    bc_cols = state2 // size
    head_width = inner // heads

    sizes = (dp_size // 2, lax.axis_size("head"), lax.axis_size("tensor"))
    taps = conv_x_weight.shape[0]
    bc_own = lax.dynamic_slice_in_dim(w_bc, place * bc_cols, bc_cols, 1)
    side_part = jnp.concatenate([bc_own, w_dt], 1).T
    side_part = jnp.pad(side_part, ((0, bc_cols + 16 - side_part.shape[0]), (0, 0)))
    small_rows = [conv_x_weight, conv_x_bias[None], norm_gain[None]]
    head_rows = jnp.stack([dt_bias, a_log, d_skip])
    small = jnp.concatenate(small_rows + [jnp.pad(head_rows, ((0, 0), (0, cols - heads_own)))], 0)
    small = jnp.pad(small, ((0, 16 - small.shape[0]), (0, 0)))

    def gathered(part):
        full = lax.all_gather(part, ALL, axis=0, tiled=False)
        return full.reshape(dp_size, size, dp_rows, cols)

    rows_ext = jnp.concatenate([from_earlier(residual[-HALO:], 1, size), residual], 0).astype(F32)
    inv_ext = lax.rsqrt(jnp.mean(rows_ext * rows_ext, axis=1, keepdims=True) + EPSILON)
    normed = (rows_ext * inv_ext * norm_in_gain).astype(BF16)
    normed_own = normed[HALO:]
    rows_in, inv_rms = rows_ext[HALO:], inv_ext[HALO:]

    seg_all = jnp.pad(segment_ids[0], (HALO, 0), constant_values=-1).astype(F32)
    seg_ext = lax.dynamic_slice_in_dim(seg_all, place * own, own + HALO)
    seg_row = jnp.broadcast_to(seg_ext[None, HALO:], (8, own))
    bc_rows = jnp.concatenate([conv_bc_weight, conv_bc_bias[None]], 0)
    bc_rows = jnp.pad(bc_rows, ((0, 8 - bc_rows.shape[0]), (0, 0)))

    w_z = gathered(w_zx[:, 0])
    side_full, w_x, small_full = gather_weights([side_part, w_zx[:, 1]], small, sizes)
    w_out_later, small_full = lax.optimization_barrier((w_out, small_full))
    w_o = gathered(w_out_later)
    w_x = w_x.reshape(dp_size, size, dp_rows, cols)
    side_full = side_full.reshape(dp_size, size, bc_cols + 16, dp_rows)
    small_full = jnp.moveaxis(small_full.reshape(size, 16, cols), 0, 1)
    per_channel = small_full.reshape(16, inner)
    per_head = small_full[taps + 2 : taps + 5, :, :heads_own].reshape(3, heads)
    conv_rows = per_channel[:8]
    gain_row = per_channel[taps + 1 : taps + 2]
    head_rows = jnp.pad(per_head[:2], ((0, 6), (0, 0)))
    skip_rows = jnp.repeat(per_head[2], head_width)[None]

    scan = Scan(own, sizes, dp_rows, cols, heads_own, taps)
    (
        ext_left, own_left, cot_left, w_side, bc_ext, bc, same, dt, sig, cum_g, cumt_g, dt3, tail3, entry3, keep, keep3, keep_send, coupling, bias,
    ) = scan.prepare(normed, cotangent, side_full, seg_ext[:, None], seg_row, bc_rows, head_rows, bc_cols, heads_own)
    x_ext, x, within, added, local = scan.s1(
        normed, w_x, conv_rows, same, dt3, tail3, cum_g, cumt_g, coupling, bias, bc, keep3
    )
    (entering,) = exchange_states(local, keep_send, sizes, True)
    z, y, states, squares = scan.s2(
        normed_own, w_z, within, x, skip_rows, entry3, bc, entering, added, keep3
    )
    grad_gate, cross, gain_rows, block_out, out_pieces = scan.s3(
        y, z, squares, gain_row, w_o, cotangent, residual, cot_left
    )
    dy, back_added, back_local, own_part, z_pieces = scan.s4(
        y, z, squares, cross, gain_row, grad_gate, w_z, entry3, bc, keep3, own_left
    )

    def scattered(pieces):
        pieces = pieces.reshape(dp_size * size, dp_rows, cols)
        return lax.psum_scatter(pieces, ALL, scatter_dimension=0, tiled=False).astype(F32)

    grid = (dp_size,) + sizes[1:]
    grad_wo = scattered(out_pieces)
    leaving, grad_wz = exchange_states(
        back_local, keep_send, sizes, False, (z_pieces.reshape(grid + (dp_rows, cols)),)
    )
    conv_sums, head_sums, dots, dbc, dmix, through, x_pieces = scan.s5(
        dy, x_ext, within, conv_rows, skip_rows, same, dt3, tail3, entry3, cum_g, cumt_g, coupling, bias, bc,
        states, leaving, back_added, keep3, w_x, ext_left
    )
    part, halo, bc_sums, scan_sums, side_pieces = scan.finish(
        dbc, dmix, bc, bc_ext, bc_rows, same, head_sums, dots, keep, dt, sig, head_rows, w_side, through, own_part,
        normed
    )

    grad_normed = part.at[own - HALO :].add(from_later(halo, 1, size))
    scaled_in = grad_normed * norm_in_gain
    input_grad = (
        cotangent.astype(F32)
        + inv_rms * scaled_in
        - rows_in * (inv_rms * inv_rms * inv_rms) * jnp.mean(scaled_in * rows_in, axis=1, keepdims=True)
    )
    grad_in_gain = jnp.sum(grad_normed * rows_in * inv_rms, axis=0)

    grad_skip = jnp.sum(conv_sums[taps + 1].reshape(heads, head_width), axis=1)
    head_sum = jnp.concatenate([scan_sums[0], scan_sums[1], grad_skip])
    row = jnp.concatenate([grad_in_gain, bc_sums[: taps + 1].reshape(-1)])
    small_sum = jnp.concatenate(
        [
            conv_sums[: taps + 1],
            gain_rows[:1],
            jnp.pad(row, (0, inner - row.shape[0]))[None],
            jnp.pad(head_sum, (0, inner - head_sum.shape[0]))[None],
        ],
        0,
    )
    grad_side, grad_wx, small_sum = scatter_gradients(
        [side_pieces.reshape(grid + (-1, dp_rows)), x_pieces.reshape(grid + (dp_rows, cols))], small_sum, sizes
    )
    grad_wzx = jnp.stack([grad_wz, grad_wx], 1)
    grad_side = grad_side.reshape(-1, dp_rows).astype(F32)
    grad_wbc = grad_side[:state2].T
    grad_wdt = lax.dynamic_slice_in_dim(grad_side, state2 + place * heads_own, heads_own, 0).T
    channel_own = lax.dynamic_slice_in_dim(small_sum[: taps + 2], place * cols, cols, 1)
    row = small_sum[taps + 2]
    gain_sum = row[:width]
    taps_sum = row[width : width + taps * state2].reshape(taps, state2)
    bias_sum = row[width + taps * state2 : width + (taps + 1) * state2]
    head_sum = small_sum[taps + 3, : 3 * heads].reshape(3, heads)
    head_own = lax.dynamic_slice_in_dim(head_sum, place * heads_own, heads_own, 1)
    return (
        block_out,
        input_grad,
        gain_sum,
        grad_wzx,
        grad_wbc,
        grad_wdt,
        channel_own[:taps],
        channel_own[taps],
        taps_sum,
        bias_sum,
        head_own[0],
        head_own[1],
        head_own[2],
        channel_own[taps + 1],
        grad_wo,
    )


def solution(mesh):
    rows = P(ALL, None)
    in_specs = (
        rows,
        P("dp", None),
        P(),
        P("dp", None, SEQ),
        P("dp", None),
        P("dp", SEQ),
        P(None, SEQ),
        P(SEQ),
        P(),
        P(),
        P(SEQ),
        P(SEQ),
        P(SEQ),
        P(SEQ),
        P("dp", SEQ),
        rows,
    )
    out_specs = (
        rows,
        rows,
        P(),
        P("dp", None, SEQ),
        P("dp", None),
        P("dp", SEQ),
        P(None, SEQ),
        P(SEQ),
        P(),
        P(),
        P(SEQ),
        P(SEQ),
        P(SEQ),
        P(SEQ),
        P("dp", SEQ),
    )
    return jax.shard_map(
        body, mesh=mesh, in_specs=in_specs, out_specs=out_specs, check_vma=False
    )
```

time: 654 us -> 605 us (0.925)
  Pallas kernels: 367 us -> 522 us
  local copies, waits for them, and re-layouts: 90.7 us -> 28.9 us
  waiting for transfers between devices: 59.5 us -> 6.55 us
  other arithmetic: 57.7 us -> 18.9 us
  starting transfers between devices: 40 us -> 4.18 us
  matrix products: 11.7 us -> 0 us
    pallas_call x2 -> x4, Pallas kernels: 30.7 us -> 194 us  [the longest x2 173 us: exchange_states(): pl.pallas_call(functools.partial(exchange_kernel, sizes, forward, chunks)...]
    ppermute x6 -> x1, waiting for transfers between devices: 29.8 us -> 0.01 us  [from_earlier(): lax.ppermute(values, SEQ, [(i, i + distance) for i in range(size - distan...]
    ppermute x6 -> x1, starting transfers between devices: 30.8 us -> 2.77 us  [from_earlier(): lax.ppermute(values, SEQ, [(i, i + distance) for i in range(size - distan...]
    pallas_call x1, Pallas kernels: 95.8 us -> 69.1 us  [scatter_gradients(): pl.pallas_call(functools.partial(scatter_kernel, sizes, chunks, kinds), o...]
    ppermute x6 -> x1, waiting for transfers between devices: 29.7 us -> 4.58 us  [from_later(): lax.ppermute(values, SEQ, [(i + distance, i) for i in range(size - distan...]
    pallas_call x5, Pallas kernels: 143 us -> 168 us  [call(): pl.pallas_call(kernel, grid=(self.groups,), out_shape=[shape for shape, _...]
    select_n x4 -> x0, other arithmetic: 12.4 us -> none  [the longest x3 11.6 us: to_pair(): jnp.where(core == 0, jnp.stack([v, other]), jnp.stack([other, v]))]
    slice x17 -> x6, local copies, waits for them, and re-layouts: 14.7 us -> 2.38 us  [the longest x1 1.33 us: body(): normed_own = normed[HALO:]]
  transfers between devices with their start and end apart: 17 -> 5, of which waited for: 6 -> 2; matrix products, arithmetic and copies ran while one was open for 23% -> 7% of each run, Pallas kernels for 44% -> 83%
where the time goes in v4:
time: 605 us; the launch traced here: 595 us
  Pallas kernels  522 us (86%)
  local copies, waits for them, and re-layouts  28.9 us (5%)
  other arithmetic  18.9 us (3%)
  between operations  14.6 us (2%)
  waiting for transfers between devices  6.55 us (1%)
    pallas_call x2, Pallas kernels, exchange_states(): pl.pallas_call(functools.partial(exchange_kernel, sizes, forward, chunks)...  173 us
    pallas_call x5, Pallas kernels, call(): pl.pallas_call(kernel, grid=(self.groups,), out_shape=[shape for shape, _...  168 us
    pallas_call x1, Pallas kernels, gather_weights(): pl.pallas_call(functools.partial(gather_kernel, sizes, chunks, kinds), ou...  91.6 us
    pallas_call x1, Pallas kernels, scatter_gradients(): pl.pallas_call(functools.partial(scatter_kernel, sizes, chunks, kinds), o...  69.1 us
    pallas_call x2, Pallas kernels, alone(): pl.pallas_call(kernel, out_shape=outs, in_specs=[whole] * len(ins), out_s...  20.3 us
  transfers between devices with their start and end apart: 5, of which 2 were waited for; matrix products, arithmetic and copies ran while one was open for 7% of the time, Pallas kernels for 83%

profile of v4, /device:TPU:0, one launch (start us, length us, event | category | flops | bytes accessed | tf_op | source)
XLA Modules:
  0.0 595.5 jit_solution(13282873090496174059)
XLA Ops:
  7.3 2.3 fusion.1
  12.8 91.6 %shard_map.271 = (bf16[4,4,2,48,384]{4,3,2,1,0:T(8,128)(2,1)}, bf16[4,4,2,384,384]{4,3,2,1,0:T(8,128)(2,1)}, f32[4,2,16,384]{3,2,1,0:T(8,128)}) custom-call(bf16[48,384]{1,0:T(8,128)(2,1)} %pad.34.refs_0_, bf16[384,384]{1,0:T(8,128)(2,1)} %bitcast.69, f32[16,384]{1,0:T(8,128)} %select_maximum_fusion.refs_2_), custom_call_target="tpu_custom_call" | custom-call | flops 54000001024 | tf_op jit(solution)/shard_map/pallas_call | solution.py:243
  104.5 2.8 collective-permute-start
  115.6 2.2 maximum_convert_fusion
  118.4 10.7 %shard_map.272 = (bf16[4,384,528]{2,1,0:T(8,128)(2,1)}, bf16[4,384,512]{2,1,0:T(8,128)(2,1)}, bf16[4,384,512]{2,1,0:T(8,128)(2,1)}, bf16[384,1536]{1,0:T(8,128)(...) custom-call(bf16[528,1536]{1,0:T(8,128)(2,1)} %copy-done.4, ...), custom_call_target="tpu_custom_call" | custom-call | flops 8999999488 | tf_op jit(solution)/shard_map/pallas_call | solution.py:1159
  129.1 23.0 %shard_map.273 = (f32[528,3072]{1,0:T(8,128)}, f32[512,3072]{1,0:T(8,128)}, f32[512,3072]{1,0:T(8,128)}, f32[4,3072,128]{2,1,0:T(8,128)}, bf16[3072,128]{1,0:T(8,128)(2,1)}) custom-call(bf16[528,1536]{1,0:T(8,128)(2,1)} %copy-done.4, bf16[4,8,384,384]{3,2,1,0:T(8,128)(2,1)} %bitcast.92, f32[8,3072]{1,0:T(8,128)} %bitcast.72, ...), custom_call_target="tpu_custom_call" | custom-call | flops 19800000512 | tf_op jit(solution)/shard_map/pallas_call | solution.py:769
  152.1 54.9 %shard_map.274 = bf16[8,384,128]{2,1,0:T(8,128)(2,1)} custom-call(bf16[8,384,128]{2,1,0:T(8,128)(2,1)} %bitcast.101, bf16[8,16,384]{2,1,0:T(8,128)(2,1)} %get-tuple-element.104.refs_1_), custom_call_target="tpu_custom_call" | custom-call | flops 54000001024 | tf_op jit(solution)/shard_map/pallas_call | solution.py:654
  207.0 21.7 %shard_map.275 = (f32[512,3072]{1,0:T(8,128)}, f32[512,3072]{1,0:T(8,128)}, bf16[4,3072,128]{2,1,0:T(8,128)(2,1)}, f32[512,128]{1,0:T(8,128)}) custom-call(bf16[512,1536]{1,0:T(8,128)(2,1)} %slice.169.normed_ref, bf16[4,8,384,384]{3,2,1,0:T(8,128)(2,1)} %bitcast.89, f32[512,3072]{1,0:T(8,128)} %get-tuple-element.100.within_ref, ...), custom_call_target="tpu_custom_call" | custom-call | flops 19800000512 | tf_op jit(solution)/shard_map/pallas_call | solution.py:769
  228.7 1.9 all-gather.7.cloned.1.call-done
  230.6 29.5 %shard_map.276 = (f32[512,3072]{1,0:T(8,128)}, f32[512,128]{1,0:T(8,128)}, f32[8,3072]{1,0:T(8,128)}, bf16[512,1536]{1,0:T(8,128)(2,1)}, bf16[4,8,384,384]{3,2,1,0:T(8,128)(2,1)}) custom-call(f32[512,3072]{1,0:T(8,128)} %get-tuple-element.106.y_ref, f32[512,3072]{1,0:T(8,128)} %get-tuple-element.107.z_ref, f32[512,128]{1,0:T(8,128)} %get-tuple-element.108.squares_ref, ...), custom_call_target="tpu_custom_call" | custom-call | flops 19800000512 | tf_op jit(solution)/shard_map/pallas_call | solution.py:769
  260.1 29.5 %shard_map.277 = (f32[512,3072]{1,0:T(8,128)}, f32[4,3072,128]{2,1,0:T(8,128)}, bf16[3072,128]{1,0:T(8,128)(2,1)}, f32[512,1536]{1,0:T(8,128)}, bf16[4,8,384,384]{3,2,1,0:T(8,128)(2,1)}) custom-call(f32[512,3072]{1,0:T(8,128)} %get-tuple-element.106.y_ref, f32[512,3072]{1,0:T(8,128)} %get-tuple-element.107.z_ref, f32[512,128]{1,0:T(8,128)} %get-tuple-element.108.squares_ref, ...), custom_call_target="tpu_custom_call" | custom-call | flops 19800000512 | tf_op jit(solution)/shard_map/pallas_call | solution.py:769
  289.7 118.6 %shard_map.278 = (bf16[8,384,128]{2,1,0:T(8,128)(2,1)}, f32[384,384]{1,0:T(8,128)}) custom-call(bf16[8,384,128]{2,1,0:T(8,128)(2,1)} %bitcast.99, bf16[8,16,384]{2,1,0:T(8,128)(2,1)} %get-tuple-element.104.refs_1_, bf16[4,4,2,384,384]{4,3,2,1,0:T(8,128)(2,1)} %bitcast.95), custom_call_target="tpu_custom_call" | custom-call | flops 54000001024 | tf_op jit(solution)/shard_map/pallas_call | solution.py:654
  409.2 64.2 %shard_map.279 = (f32[8,3072]{1,0:T(8,128)}, f32[3,512,128]{2,1,0:T(8,128)}, f32[4,128,128]{2,1,0:T(8,128)}, f32[512,256]{1,0:T(8,128)}, f32[4,128,128]{2,1,0:T(...) custom-call(f32[512,3072]{1,0:T(8,128)} %get-tuple-element.115.dy_ref, ...), custom_call_target="tpu_custom_call" | custom-call | flops 19800000512 | tf_op jit(solution)/shard_map/pallas_call | solution.py:769
  473.4 9.6 %shard_map.280 = (f32[512,1536]{1,0:T(8,128)}, f32[16,1536]{1,0:T(8,128)}, f32[8,256]{1,0:T(8,128)}, f32[8,48]{1,0:T(8,128)}, bf16[4,384,384]{2,1,0:T(8,128)(2,1)}) custom-call(f32[512,256]{1,0:T(8,128)} %get-tuple-element.123.dbc_ref, f32[4,128,128]{2,1,0:T(8,128)} %get-tuple-element.124.dmix_ref, bf16[512,256]{1,0:T(8,128)(2,1)} %get-tuple-element.98.bc_ref, ...), custom_call_target="tpu_custom_call" | custom-call | flops 10800000000 | tf_op jit(solution)/shard_map/pallas_call | solution.py:1159
  486.1 4.6 collective-permute-done.1
  490.6 1.5 add_dynamic-update-slice_fusion
  492.2 2.7 multiply_reduce_fusion.1
  495.6 69.1 %shard_map.281 = (bf16[4,2,48,384]{3,2,1,0:T(8,128)(2,1)}, f32[384,384]{1,0:T(8,128)}, f32[8,3072]{1,0:T(8,128)}) custom-call(bf16[4,4,2,48,384]{4,3,2,1,0:T(8,128)(2,1)} %bitcast.97, bf16[4,4,2,384,384]{4,3,2,1,0:T(8,128)(2,1)} %bitcast.94, f32[8,3072]{1,0:T(8,128)} %pad_maximum_fusion.1.refs_2_), custom_call_target="tpu_custom_call" | custom-call | flops 54000001024 | tf_op jit(solution)/shard_map/pallas_call | solution.py:541
  565.8 1.9 copy.41
  573.8 1.9 copy.42
  575.7 1.5 dynamic-slice_reduce_fusion
  579.9 1.4 slice_reduce_fusion.1
  581.8 4.9 multiply_subtract_fusion
  586.7 1.8 bitcast_convert_fusion
  (112 shorter events, 27.2 us)
Async XLA Ops:
  7.2 3.3 copy-start
  7.2 4.3 copy-start.15
  7.2 4.9 copy-start.20
  7.2 4.9 copy-start.21
  7.2 4.9 copy-start.22
  7.3 4.9 copy-start.14
  7.3 199.7 %all-gather.5.cloned.1.call-start = ((), (), s32[]{:S(2)}) async-start(), calls=%async_computation.2 | async-start | bytes 9732096 | tf_op jit(solution)/shard_map/all_gather | solution.py:1402
  10.4 220.2 %all-gather.7.cloned.1.call-start = ((), (), s32[]{:S(2)}) async-start(), calls=%async_computation.3 | async-start | bytes 9732096 | tf_op jit(solution)/shard_map/all_gather | solution.py:1402
  12.8 91.7 %copy-start.3 = (bf16[512,1536]{1,0:T(8,128)(2,1)S(1)}, bf16[512,1536]{1,0:T(8,128)(2,1)}, u32[]{:S(2)}) copy-start(bf16[512,1536]{1,0:T(8,128)(2,1)} %residual_ref.1) | copy-start | bytes 4718596
  12.8 95.5 %copy-start.16 = (f32[4,256]{1,0:T(4,128)S(1)}, f32[4,256]{1,0:T(4,128)}, u32[]{:S(2)}) copy-start(f32[4,256]{1,0:T(4,128)} %param.26) | copy-start | bytes 12292
  12.8 95.5 %copy-start.19 = (f32[256]{0:T(256)S(1)}, f32[256]{0:T(256)}, u32[]{:S(2)}) copy-start(f32[256]{0:T(256)} %param.27) | copy-start | bytes 3076
  12.8 96.1 %copy-start.12 = (s32[1,4096]{1,0:T(1,128)S(1)}, s32[1,4096]{1,0:T(1,128)}, u32[]{:S(2)}) copy-start(s32[1,4096]{1,0:T(1,128)} %param.19) | copy-start | bytes 49156
  104.4 8.8 %copy-start.8 = (f32[1536]{0:T(1024)S(1)}, f32[1536]{0:T(1024)}, u32[]{:S(2)}) copy-start(f32[1536]{0:T(1024)} %param.20) | copy-start | bytes 18436
  104.4 482.2 %reduce-scatter.2.cloned.1.call-start = ((), (), s32[]{:S(2)}) async-start(), calls=%async_computation.1 | async-start | bytes 9732096 | tf_op jit(solution)/shard_map/reduce_scatter | solution.py:1451
  104.5 8.2 %collective-permute-start = (bf16[16,1536]{1,0:T(8,128)(2,1)S(1)}, bf16[16,1536]{1,0:T(8,128)(2,1)S(1)}, u32[]{:S(2)}, u32[]{:S(2)}) collective-permute-start(bf16[16,1536]{1,0:T(8,128)(2,1)S(1)} %slice.133), channel_id=1, source_target_pairs={{0,1},{1,2},{2,3},{3,4},{4,5},{5,6},{6,7},{8,9},{9,10},{10,11},{11... | collective-permute-start | bytes 147464 | tf_op jit(solution)/shard_map/ppermute | solution.py:1354
  113.7 4.1 copy-start.4
  473.3 10.3 %copy-start.7 = (f32[8,3072]{1,0:T(8,128)S(1)}, f32[8,3072]{1,0:T(8,128)}, u32[]{:S(2)}) copy-start(f32[8,3072]{1,0:T(8,128)} %get-tuple-element.138) | copy-start | bytes 294916
  473.4 18.8 %copy-start.2 = (f32[528,1536]{1,0:T(8,128)S(1)}, f32[528,1536]{1,0:T(8,128)}, u32[]{:S(2)}) copy-start(f32[528,1536]{1,0:T(8,128)} %maximum_convert_fusion) | copy-start | bytes 9732100
  473.4 18.8 %copy-start.9 = (f32[1536]{0:T(1024)S(1)}, f32[1536]{0:T(1024)}, u32[]{:S(2)}) copy-start(f32[1536]{0:T(1024)} %param.20) | copy-start | bytes 18436
  473.4 18.8 %copy-start.11 = (f32[512]{0:T(512)S(1)}, f32[512]{0:T(512)}, u32[]{:S(2)}) copy-start(f32[512]{0:T(512)} %copy-done.10) | copy-start | bytes 6148
  483.9 6.7 %collective-permute-start.1 = (f32[16,1536]{1,0:T(8,128)}, f32[16,1536]{1,0:T(8,128)S(1)}, u32[]{:S(2)}, u32[]{:S(2)}) collective-permute-start(f32[16,1536]{1,0:T(8,128)} %get-tuple-element.135), channel_id=1, source_target_pairs={{1,0},{2,1},{3,2},{4,3},{5,4},{6,5},{7,6},{9,8},{10,9},{11,10},{12... | collective-permute-start | bytes 294920 | tf_op jit(solution)/shard_map/ppermute | solution.py:1358
  495.6 69.1 %copy-start.6 = (f32[384,384]{1,0:T(8,128)S(1)}, f32[384,384]{1,0:T(8,128)}, u32[]{:S(2)}) copy-start(f32[384,384]{1,0:T(8,128)} %get-tuple-element.143) | copy-start | bytes 1769476
  564.7 17.1 %copy-start.13 = (f32[512,1]{0,1:T(1,128)S(1)}, f32[512,1]{0,1:T(1,128)}, u32[]{:S(2)}) copy-start(f32[512,1]{0,1:T(1,128)} %multiply_multiply_fusion) | copy-start | bytes 6148
  581.8 6.7 %copy-start.1 = (bf16[384,256]{1,0:T(8,128)(2,1)S(1)}, bf16[384,256]{1,0:T(8,128)(2,1)}, u32[]{:S(2)}) copy-start(bf16[384,256]{1,0:T(8,128)(2,1)} %param.22) | copy-start | bytes 589828
  (4 other events, 9.2 us)
Sparse Core Ops, SparseCore 0:
  11.6 107.5 all-gather.4
  122.1 108.4 all-gather.6
  260.3 185.0 reduce-scatter.1

commit v5 on v4

--- a/solution.py
+++ b/solution.py
@@ -12,6 +12,8 @@
 HALO = 16
 AHEAD = 2
 LAGS = (0, 1, 3, 5)
+HOSTED_LAGS = (0, 4, 6, 8)
+SLOTS = 2
 CHUNK_ROWS = 48
 MASKED = -1e30
 HIGHEST = lax.Precision.HIGHEST
@@ -258,7 +260,7 @@
     )(*parts, small)
 
 
-def reducer(sizes, chunks, parts, bufs, sems, put):
+def reducer(sizes, chunks, parts, bufs, sems, put, lags=LAGS):
     xs, hs, ts = sizes
     send, recv, own_sem = sems
     x, core, head, tensor = coordinates()
@@ -322,41 +324,43 @@
         kind, start, length, x_first = chunks[index]
         held = bufs[5 * index]
         into = bufs[5 * index + 1 + number]
+        def plus(own, others):
+            if len(others) == 1:
+                return own + others[0]
+            value = own.astype(F32)
+            for one in others:
+                value = value + one.astype(F32)
+            return value.astype(BF16)
+
         if number == 0:
 
             @pl.loop(0, xs * hs)
             def _(both):
                 one, two = lax.div(both, hs), lax.rem(both, hs)
-                value = held[one, two].astype(F32) + into[one, two].astype(F32)
-                held[one, two] = value.astype(BF16)
+                held[one, two] = plus(held[one, two], [into[one, two]])
 
         elif number == 1 and x_first:
 
             @pl.loop(0, hs)
             def _(one):
-                value = held[x, one].astype(F32)
-                for step in range(xs - 1):
-                    value = value + into[step, one].astype(F32)
-                held[x, one] = value.astype(BF16)
+                held[x, one] = plus(held[x, one], [into[step, one] for step in range(xs - 1)])
 
         elif number == 1:
 
             @pl.loop(0, xs * hs)
             def _(both):
                 one, two = lax.div(both, hs), lax.rem(both, hs)
-                value = held[one, two, tensor].astype(F32)
-                for step in range(ts - 1):
-                    value = value + into[step, one, two].astype(F32)
-                held[one, two, tensor] = value.astype(BF16)
+                held[one, two, tensor] = plus(
+                    held[one, two, tensor], [into[step, one, two] for step in range(ts - 1)]
+                )
 
         elif number == 2:
 
             @pl.loop(0, hs)
             def _(one):
-                value = held[x, one, tensor].astype(F32)
-                for step in range(into.shape[0]):
-                    value = value + into[step, one].astype(F32)
-                held[x, one, tensor] = value.astype(BF16)
+                held[x, one, tensor] = plus(
+                    held[x, one, tensor], [into[step, one] for step in range(into.shape[0])]
+                )
 
         else:
             value = held[x, head, tensor].astype(F32)
@@ -374,7 +378,7 @@
                     one.start()
 
     def tick(at):
-        for number, lag in enumerate(LAGS):
+        for number, lag in enumerate(lags):
             index = at - lag
             if 0 <= index < total:
                 for one in stage(index, number):
@@ -396,7 +400,7 @@
                 for one in stage(index, number):
                     one.wait_send()
 
-    return start, tick, end, total + LAGS[3]
+    return start, tick, end, total + lags[3]
 
 
 def reducer_scratch(sizes, chunks, parts):
@@ -682,6 +686,12 @@
     return pl.CostEstimate(flops=microseconds * 900_000_000, bytes_accessed=0, transcendentals=0)
 
 
+def remote_params(collective):
+    return pltpu.CompilerParams(
+        collective_id=collective, has_side_effects=True, vmem_limit_bytes=VMEM_BYTES
+    )
+
+
 def local_params():
     return pltpu.CompilerParams(vmem_limit_bytes=VMEM_BYTES)
 
@@ -721,13 +731,21 @@
     return hit.astype(F32).astype(BF16)
 
 
-def conv_pre(ext_ref, taps_ref, same_ref, own, width):
-    total = taps_ref[width : width + 1] + taps_ref[width - 1 : width] * ext_ref[HALO:]
+def tiles(count, step=32):
+    return [slice(at, min(at + step, count)) for at in range(0, count, step)]
+
+
+def moved(rows, by):
+    return slice(rows.start + by, rows.stop + by)
+
+
+def conv_pre(ext_ref, taps_ref, same_ref, rows, width):
+    total = taps_ref[width : width + 1] + taps_ref[width - 1 : width] * ext_ref[moved(rows, HALO)]
     for back in range(1, width):
         total = total + (
             taps_ref[width - 1 - back : width - back]
-            * ext_ref[HALO - back : HALO - back + own]
-            * same_ref[:, back - 1 : back]
+            * ext_ref[moved(rows, HALO - back)]
+            * same_ref[moved(rows, HALO), back - 1 : back]
         )
     return total
 
@@ -764,7 +782,7 @@
         self.inner = self.hts * cols
         self.pairs = self.wide // 128
 
-    def call(self, kernel, ins, outs, scratch=()):
+    def call(self, kernel, ins, outs, scratch=(), collective=None):
         arrays = [array for array, _ in ins]
         return pl.pallas_call(
             kernel,
@@ -773,12 +791,13 @@
             in_specs=[spec for _, spec in ins],
             out_specs=[spec for _, spec in outs],
             scratch_shapes=list(scratch),
-            compiler_params=local_params(),
+            compiler_params=local_params() if collective is None else remote_params(collective),
             cost_estimate=busy(22),
         )(*arrays)
 
     def full(self, array):
-        return (array, pl.BlockSpec(array.shape, lambda j: (0,) * array.ndim))
+        mode = None if isinstance(array, jax.ShapeDtypeStruct) else pl.Buffered(1)
+        return (array, pl.BlockSpec(array.shape, lambda j: (0,) * array.ndim, pipeline_mode=mode))
 
     def pieces(self, array):
         block = (self.dps, self.group, self.rows, self.cols)
@@ -856,15 +875,19 @@
         def kernel(
             normed_ref, w_ref, conv_ref, same_ref, dt_ref, tail_ref, cum_ref, cumt_ref,
             coupling_ref, bias_ref, bc_ref, keep_ref, ext_ref, x_ref, within_ref, added_ref, local_ref, xd_ref, xt_ref,
+            dtw_ref, tailw_ref,
         ):
             self.project(normed_ref[...], w_ref, ext_ref)
             widen = self.widen()
             keep = self.keep_columns(keep_ref, widen)
-            x = silu_of(conv_pre(ext_ref, conv_ref, same_ref, own, self.taps))
-            x_ref[...] = x
-            xd = x * dot_nn(dt_ref[...], widen)
-            xd_ref[...] = xd.astype(BF16)
-            xt_ref[...] = (xd * dot_nn(tail_ref[...], widen)).astype(BF16)
+            dtw_ref[...] = dot_nn(dt_ref[...], widen)
+            tailw_ref[...] = dot_nn(tail_ref[...], widen)
+            for rows in tiles(own):
+                x = silu_of(conv_pre(ext_ref, conv_ref, same_ref, rows, self.taps))
+                x_ref[rows] = x
+                xd = x * dtw_ref[rows]
+                xd_ref[rows] = xd.astype(BF16)
+                xt_ref[rows] = (xd * tailw_ref[rows]).astype(BF16)
             masks = lane_masks()
             held = None
             for c in range(self.chunks):
@@ -893,7 +916,7 @@
                 self.lanes(f((own, self.inner), F32)), self.states(f((self.chunks, self.inner, state), F32)),
                 self.states(f((self.inner, state), BF16)),
             ],
-            [pltpu.VMEM((own, self.wide), BF16), pltpu.VMEM((own, self.wide), BF16)],
+            [pltpu.VMEM((own, self.wide), BF16)] * 2 + [pltpu.VMEM((own, self.wide), F32)] * 2,
         )
 
     def s2(self, normed_own, w_z, within, x, skip_rows, entry3, bc, entering, added, keep3):
@@ -901,31 +924,30 @@
 
         def kernel(
             normed_ref, w_ref, within_ref, x_ref, skip_ref, entry_ref, bc_ref, entering_ref,
-            added_ref, keep_ref, z_ref, y_ref, states_ref, squares_ref,
+            added_ref, keep_ref, z_ref, y_ref, states_ref, squares_ref, entry_wide_ref, carried_ref,
         ):
             self.project(normed_ref[...], w_ref, z_ref)
             widen = self.widen()
             keep = self.keep_columns(keep_ref, widen)
-            entry = dot_nn(entry_ref[...], widen)
+            entry_wide_ref[...] = dot_nn(entry_ref[...], widen)
             held = entering_ref[...].astype(F32)
             for c in range(self.chunks):
                 rows = self.chunk_rows(c)
                 held16 = held.astype(BF16)
                 states_ref[c] = held16
-                carried = dot_nt(bc_ref[rows, state:], held16)
-                y_ref[rows] = within_ref[rows] + carried * entry[rows] + skip_ref[...] * x_ref[rows]
+                carried_ref[rows] = dot_nt(bc_ref[rows, state:], held16)
                 if c + 1 < self.chunks:
                     held = added_ref[c] + keep[:, c : c + 1] * held
-            gated = y_ref[...] * silu_of(z_ref[...])
-            squares = self.lane_sums(gated * gated)
 
             @pl.when(pl.program_id(0) == 0)
             def _():
-                squares_ref[...] = squares
-
-            @pl.when(pl.program_id(0) > 0)
-            def _():
-                squares_ref[...] += squares
+                squares_ref[...] = jnp.zeros_like(squares_ref)
+
+            for rows in tiles(own):
+                y = within_ref[rows] + carried_ref[rows] * entry_wide_ref[rows] + skip_ref[...] * x_ref[rows]
+                y_ref[rows] = y
+                gated = y * silu_of(z_ref[rows])
+                squares_ref[rows] += self.lane_sums(gated * gated)
 
         f = jax.ShapeDtypeStruct
         return self.call(
@@ -939,38 +961,38 @@
                 self.lanes(f((own, self.inner), F32)), self.lanes(f((own, self.inner), F32)),
                 self.states(f((self.chunks, self.inner, state), BF16)), self.full(f((own, 128), F32)),
             ],
+            [pltpu.VMEM((own, self.wide), F32)] * 2,
         )
 
-    def inv_gate(self, squares_ref):
-        return lax.rsqrt(jnp.sum(squares_ref[...], axis=1, keepdims=True) / self.inner + EPSILON)
+    def inv_gate(self, squares_ref, rows):
+        return lax.rsqrt(jnp.sum(squares_ref[rows], axis=1, keepdims=True) / self.inner + EPSILON)
 
     def s3(self, y, z, squares, gain_row, w_o, cotangent, residual, cot_left):
         own = self.own
 
         def kernel(
             y_ref, z_ref, squares_ref, gain_ref, w_ref, cot_ref, residual_ref, left_ref,
-            grad_ref, cross_ref, gain_grad_ref, out_ref, pieces_ref, gated_ref, sum_ref,
+            grad_ref, cross_ref, gain_grad_ref, out_ref, pieces_ref, gated_ref, sum_ref, normal_ref,
         ):
-            inv = self.inv_gate(squares_ref)
-            gated = y_ref[...] * silu_of(z_ref[...])
-            normal = gated * inv
-            gated_ref[...] = (normal * gain_ref[...]).astype(BF16)
+            for rows in tiles(own):
+                normal = y_ref[rows] * silu_of(z_ref[rows]) * self.inv_gate(squares_ref, rows)
+                normal_ref[rows] = normal
+                gated_ref[rows] = (normal * gain_ref[...]).astype(BF16)
             self.project_back(gated_ref, w_ref, sum_ref)
             self.gradient(left_ref, gated_ref, pieces_ref)
             self.project(cot_ref[...], w_ref, grad_ref)
-            grad = grad_ref[...]
-            gain_grad_ref[...] = jnp.broadcast_to(
-                jnp.sum(grad * normal, axis=0, keepdims=True), gain_grad_ref.shape
-            )
-            cross = self.lane_sums(grad * gain_ref[...] * gated)
 
             @pl.when(pl.program_id(0) == 0)
             def _():
-                cross_ref[...] = cross
-
-            @pl.when(pl.program_id(0) > 0)
-            def _():
-                cross_ref[...] += cross
+                cross_ref[...] = jnp.zeros_like(cross_ref)
+
+            gain_grad = None
+            for rows in tiles(own):
+                product = grad_ref[rows] * normal_ref[rows]
+                summed = jnp.sum(product, axis=0, keepdims=True)
+                gain_grad = summed if gain_grad is None else gain_grad + summed
+                cross_ref[rows] += self.lane_sums(product * gain_ref[...])
+            gain_grad_ref[...] = jnp.broadcast_to(gain_grad, gain_grad_ref.shape)
 
             @pl.when(pl.program_id(0) == self.groups - 1)
             def _():
@@ -988,7 +1010,10 @@
                 self.lanes(f((8, self.inner), F32)), self.full(f((own, self.width), BF16)),
                 self.pieces(self.piece_shape()),
             ],
-            [pltpu.VMEM((own, self.wide), BF16), pltpu.VMEM((own, self.width), F32)],
+            [
+                pltpu.VMEM((own, self.wide), BF16), pltpu.VMEM((own, self.width), F32),
+                pltpu.VMEM((own, self.wide), F32),
+            ],
         )
 
     def s4(self, y, z, squares, cross, gain_row, grad_gate, w_z, entry3, bc, keep3, left):
@@ -997,22 +1022,25 @@
         def kernel(
             y_ref, z_ref, squares_ref, cross_ref, gain_ref, grad_ref, w_ref, entry_ref, bc_ref,
             keep_ref, left_ref, dy_ref, back_ref, local_ref, through_ref, pieces_ref, low_ref, dye_ref,
+            entry_wide_ref,
         ):
-            inv = self.inv_gate(squares_ref)
-            cross_mean = jnp.sum(cross_ref[...], axis=1, keepdims=True) / self.inner
-            z = z_ref[...]
-            gate = jax.nn.sigmoid(z)
-            z_gate = z * gate
-            y = y_ref[...]
-            grad_gated = inv * (grad_ref[...] * gain_ref[...]) - (y * z_gate) * (inv * inv * inv * cross_mean)
-            dy = grad_gated * z_gate
-            dy_ref[...] = dy
-            low_ref[...] = (grad_gated * y * (gate * (1.0 + z * (1.0 - gate)))).astype(BF16)
+            widen = self.widen()
+            keep = self.keep_columns(keep_ref, widen)
+            entry_wide_ref[...] = dot_nn(entry_ref[...], widen)
+            for rows in tiles(own):
+                inv = self.inv_gate(squares_ref, rows)
+                cross_mean = jnp.sum(cross_ref[rows], axis=1, keepdims=True) / self.inner
+                z = z_ref[rows]
+                gate = jax.nn.sigmoid(z)
+                z_gate = z * gate
+                y = y_ref[rows]
+                grad_gated = inv * (grad_ref[rows] * gain_ref[...]) - (y * z_gate) * (inv * inv * cross_mean)
+                dy = grad_gated * z_gate
+                dy_ref[rows] = dy
+                low_ref[rows] = (grad_gated * y * (gate * (1.0 + z * (1.0 - gate)))).astype(BF16)
+                dye_ref[rows] = (dy * entry_wide_ref[rows]).astype(BF16)
             self.project_back(low_ref, w_ref, through_ref)
             self.gradient(left_ref, low_ref, pieces_ref)
-            widen = self.widen()
-            keep = self.keep_columns(keep_ref, widen)
-            dye_ref[...] = (dy * dot_nn(entry_ref[...], widen)).astype(BF16)
             held = None
             for c in range(self.chunks - 1, -1, -1):
                 rows = self.chunk_rows(c)
@@ -1034,22 +1062,56 @@
                 self.states(f((self.chunks, self.inner, state), F32)), self.states(f((self.inner, state), BF16)),
                 self.full(f((own, self.width), F32)), self.pieces(self.piece_shape()),
             ],
-            [pltpu.VMEM((own, self.wide), BF16), pltpu.VMEM((own, self.wide), BF16)],
+            [pltpu.VMEM((own, self.wide), BF16)] * 2 + [pltpu.VMEM((own, self.wide), F32)],
         )
 
     def s5(
         self, dy, x_ext, within, conv_rows, skip_rows, same, dt3, tail3, entry3, cum_g, cumt_g, coupling,
-        bias, bc, states, leaving, back_added, keep3, w_x, left,
+        bias, bc, states, leaving, back_added, keep3, w_x, left, others, sizes,
     ):
         own, state = self.own, bc.shape[1] // 2
         taps = self.taps
+        xs, hs, ts = sizes
+        others = [other.reshape((self.dps, hs, ts) + other.shape[2:]) for other in others]
+        kinds = len(others)
+        moving = row_chunks(self.rows, 0, kinds, self.rows // CHUNK_ROWS)
+        buffers = reducer_scratch(sizes, moving, others)
+        anywhere = pl.BlockSpec(memory_space=pl.ANY)
 
         def kernel(
             dy_ref, ext_ref, within_ref, conv_ref, skip_ref, same_ref, dt_ref, tail_ref, entry_ref,
             cum_ref, cumt_ref, coupling_ref, bias_ref, bc_ref, states_ref, leaving_ref, back_ref, keep_ref,
-            w_ref, left_ref, rows_ref, head_ref, dots_ref, dbc_ref, dmix_ref, through_ref, pieces_ref,
-            low_ref, xd_ref, xt_ref, dy16_ref, dye_ref, dxd_ref, shift_ref,
+            w_ref, left_ref, *rest,
         ):
+            other_refs, rest = rest[:kinds], rest[kinds:]
+            rows_ref, head_ref, dots_ref, dbc_ref, dmix_ref, through_ref, pieces_ref = rest[:7]
+            sum_refs, rest = rest[7 : 7 + kinds], rest[7 + kinds :]
+            low_ref, xd_ref, xt_ref, dy16_ref, dye_ref, halves_ref, shift_ref, dxd_ref = rest[:8]
+            dtw_ref, tailw_ref, pre_ref, spread_ref, carried_ref = rest[8:13]
+            bufs = rest[13:]
+            x_at, core, head, tensor = coordinates()
+
+            def put(kind, start, length, value):
+                sum_refs[kind][start : start + length, :] = value
+
+            begin, step_on, end, ticks = reducer(
+                sizes, moving, other_refs, bufs[:-3], bufs[-3:], put, HOSTED_LAGS
+            )
+
+            def scatter_on(slot):
+                for step in range(self.groups):
+                    if slot < SLOTS and SLOTS * step + slot < ticks:
+
+                        @pl.when(pl.program_id(0) == step)
+                        def _(at=SLOTS * step + slot):
+                            step_on(at)
+
+            @pl.when(pl.program_id(0) == 0)
+            def _():
+                begin(True)
+                enter_kernel(x_at, core, head, tensor, xs, hs, ts, True)
+                begin(False)
+
             first_step = pl.program_id(0) == 0
 
             @pl.when(first_step)
@@ -1061,18 +1123,19 @@
 
             widen, heads_of = self.widen(), self.heads_of()
             keep = self.keep_columns(keep_ref, widen)
-            pre = conv_pre(ext_ref, conv_ref, same_ref, own, taps)
-            gate = jax.nn.sigmoid(pre)
-            x = pre * gate
-            dt = dot_nn(dt_ref[...], widen)
-            tail = dot_nn(tail_ref[...], widen)
-            xd = x * dt
-            xd_ref[...] = xd.astype(BF16)
-            xt_ref[...] = (xd * tail).astype(BF16)
-            dy = dy_ref[...]
-            dy16_ref[...] = dy.astype(BF16)
-            entry = dot_nn(entry_ref[...], widen)
-            dye_ref[...] = (dy * entry).astype(BF16)
+            dtw_ref[...] = dot_nn(dt_ref[...], widen)
+            tailw_ref[...] = dot_nn(tail_ref[...], widen)
+            spread_ref[...] = dot_nn(entry_ref[...], widen)
+            for rows in tiles(own):
+                pre = conv_pre(ext_ref, conv_ref, same_ref, rows, taps)
+                pre_ref[rows] = pre
+                xd = silu_of(pre) * dtw_ref[rows]
+                xd_ref[rows] = xd.astype(BF16)
+                xt_ref[rows] = (xd * tailw_ref[rows]).astype(BF16)
+                dy = dy_ref[rows]
+                dy16_ref[rows] = dy.astype(BF16)
+                dye_ref[rows] = (dy * spread_ref[rows]).astype(BF16)
+            scatter_on(0)
             masks = lane_masks()
             held = leaving_ref[...].astype(F32)
             for c in range(self.chunks - 1, -1, -1):
@@ -1082,7 +1145,8 @@
                 product = held * into16.astype(F32)
                 high, low = self.halves(product)
                 dots_ref[c] += dot_tn(high, heads_of) + dot_tn(low, heads_of)
-                spread_back = dot_nt(bc_ref[rows, :state], held16)
+                spread_ref[rows] = dot_nt(bc_ref[rows, :state], held16)
+                carried_ref[rows] = dot_nt(bc_ref[rows, state:], into16)
                 dmix = dmix_ref[c]
                 for pair in range(self.pairs):
                     lanes = slice(pair * 128, (pair + 1) * 128)
@@ -1095,41 +1159,67 @@
                     dkernel = dot_nt(dy_pair, two_apart(xd_ref[rows, lanes], masks))
                     dmix = dmix + dkernel[:, :CHUNK] * first + dkernel[:, CHUNK:] * second
                 dmix_ref[c] = dmix
-                dxd_within = dxd_ref[rows]
-                carried = dot_nt(bc_ref[rows, state:], into16)
-                falls = (
-                    dy16_ref[rows].astype(F32) * within_ref[rows]
-                    + dye_ref[rows].astype(F32) * carried
-                    - xd_ref[rows].astype(F32) * dxd_within
-                )
-                dxd = dxd_within + tail[rows] * spread_back
-                dxd_ref[rows] = dxd
-                head_ref[0, rows] += self.head_sums(falls, heads_of)
-                head_ref[1, rows] += self.head_sums(xt_ref[rows].astype(F32) * spread_back, heads_of)
-                head_ref[2, rows] += self.head_sums(x[rows] * dxd, heads_of)
                 dbc_ref[rows, :state] += dot_nn(xt_ref[rows], held16)
                 dbc_ref[rows, state:] += dot_nn(dye_ref[rows], into16)
                 if c > 0:
                     held = back_ref[c] + keep[:, c : c + 1] * held
-            dx = dxd_ref[...] * dt + skip_ref[...] * dy
-            grad = dx * (gate * (1.0 + pre * (1.0 - gate)))
+            scatter_on(1)
+            halves = (
+                (dy16_ref, dye_ref), (xd_ref, xt_ref), (low_ref.at[:own], halves_ref),
+            )
             shift_ref[:HALO] = jnp.zeros((HALO, self.wide), F32)
             shift_ref[HALO + own :] = jnp.zeros((HALO, self.wide), F32)
-            rows_ref[taps : taps + 1] = jnp.sum(grad, axis=0, keepdims=True)
-            rows_ref[taps + 1 : taps + 2] = jnp.sum(dy * x, axis=0, keepdims=True)
-            total = None
-            for back in range(taps):
-                masked = grad if back == 0 else grad * same_ref[:, back - 1 : back]
-                shift_ref[HALO : HALO + own] = masked
-                tap = conv_ref[taps - 1 - back : taps - back]
-                piece = tap * shift_ref[back : back + own + HALO]
-                total = piece if total is None else total + piece
-                rows_ref[taps - 1 - back : taps - back] = jnp.sum(
-                    masked * ext_ref[HALO - back : HALO - back + own], axis=0, keepdims=True
+            sums = [None] * (taps + 2)
+
+            def add_to(at, v):
+                v = jnp.sum(v, axis=0, keepdims=True)
+                sums[at] = v if sums[at] is None else sums[at] + v
+
+            for rows in tiles(own):
+                dxd_within = dxd_ref[rows]
+                falls = (
+                    dy16_ref[rows].astype(F32) * within_ref[rows]
+                    + dye_ref[rows].astype(F32) * carried_ref[rows]
+                    - xd_ref[rows].astype(F32) * dxd_within
                 )
-            low_ref[...] = total.astype(BF16)
+                dxd = dxd_within + tailw_ref[rows] * spread_ref[rows]
+                pre, dy = pre_ref[rows], dy_ref[rows]
+                gate = jax.nn.sigmoid(pre)
+                x = pre * gate
+                rises = xt_ref[rows].astype(F32) * spread_ref[rows]
+                for part, (high_ref, low_part_ref) in zip((falls, rises, x * dxd), halves):
+                    high_ref[rows], low_part_ref[rows] = self.halves(part)
+                slope = gate * (1.0 + pre * (1.0 - gate))
+                grad = (dxd * dtw_ref[rows] + skip_ref[...] * dy) * slope
+                shift_ref[moved(rows, HALO)] = grad
+                add_to(taps, grad)
+                add_to(taps + 1, dy * x)
+                add_to(taps - 1, grad * ext_ref[moved(rows, HALO)])
+                for back in range(1, taps):
+                    masked = grad * same_ref[moved(rows, HALO), back - 1 : back]
+                    add_to(taps - 1 - back, masked * ext_ref[moved(rows, HALO - back)])
+            for at in range(taps + 2):
+                rows_ref[at : at + 1] = sums[at]
+            for at, (high_ref, low_part_ref) in enumerate(halves):
+                head_ref[at] += dot_nn(high_ref[...], heads_of) + dot_nn(low_part_ref[...], heads_of)
+            for rows in tiles(own + HALO):
+                total = conv_ref[taps - 1 : taps] * shift_ref[rows]
+                for back in range(1, taps):
+                    total = total + (
+                        conv_ref[taps - 1 - back : taps - back]
+                        * shift_ref[moved(rows, back)]
+                        * same_ref[moved(rows, back), back - 1 : back]
+                    )
+                low_ref[rows] = total.astype(BF16)
+            scatter_on(2)
             self.project_back(low_ref, w_ref, through_ref)
             self.gradient(left_ref, low_ref, pieces_ref)
+
+            @pl.when(pl.program_id(0) == self.groups - 1)
+            def _():
+                for at in range(SLOTS * self.groups, ticks):
+                    step_on(at)
+                end()
 
         f = jax.ShapeDtypeStruct
         scratch16 = pltpu.VMEM((own, self.wide), BF16)
@@ -1141,17 +1231,22 @@
                 self.grouped(cum_g), self.grouped(cumt_g), self.full(coupling), self.full(bias),
                 self.full(bc), self.states(states), self.states(leaving), self.states(back_added),
                 self.full(keep3), self.pieces(w_x), self.full(left),
-            ],
+            ]
+            + [(other, anywhere) for other in others],
             [
                 self.lanes(f((8, self.inner), F32)), self.full(f((3, own, 128), F32)),
                 self.full(f((self.chunks, state, 128), F32)),
                 self.full(f((own, 2 * state), F32)), self.full(f((self.chunks, CHUNK, CHUNK), F32)),
                 self.full(f((self.ext, self.width), F32)), self.pieces(self.piece_shape()),
-            ],
+            ]
+            + [self.full(f((self.rows, self.cols), F32))] * kinds,
             [
-                pltpu.VMEM((self.ext, self.wide), BF16), scratch16, scratch16, scratch16, scratch16, pltpu.VMEM((own, self.wide), F32),
-                pltpu.VMEM((own + 2 * HALO, self.wide), F32),
-            ],
+                pltpu.VMEM((self.ext, self.wide), BF16), scratch16, scratch16, scratch16, scratch16,
+                pltpu.VMEM((own, self.wide), BF16), pltpu.VMEM((own + 2 * HALO, self.wide), F32),
+            ]
+            + [pltpu.VMEM((own, self.wide), F32)] * 6
+            + buffers,
+            4,
         )
 
     def alone(self, kernel, ins, outs, scratch, microseconds):
@@ -1200,8 +1295,8 @@
             same_ref[...] = jnp.zeros_like(same_ref)
             for back in range(1, taps):
                 hit = seg_ref[HALO - back : HALO - back + own] == mine
-                same_ref[:, back - 1 : back] = hit.astype(F32)
-            bc_ref[...] = silu_of(conv_pre(bce_ref, bcw_ref, same_ref, own, taps)).astype(BF16)
+                same_ref[HALO : HALO + own, back - 1 : back] = hit.astype(F32)
+            bc_ref[...] = silu_of(conv_pre(bce_ref, bcw_ref, same_ref, slice(0, own), taps)).astype(BF16)
             shifted = raw_ref[:, :heads] + headw_ref[0:1]
             dt = jnp.maximum(shifted, 0.0) + jnp.log1p(jnp.exp(-jnp.abs(shifted)))
             dt_ref[...] = dt
@@ -1257,7 +1352,7 @@
             [
                 f((self.dps, self.rows, self.ext), BF16), f((self.dps, self.rows, own), BF16),
                 f((self.dps, self.rows, own), BF16),
-                f((wide, self.width), BF16), f((self.ext, state2), F32), f((own, state2), BF16), f((own, 8), F32),
+                f((wide, self.width), BF16), f((self.ext, state2), F32), f((own, state2), BF16), f((own + 2 * HALO, 8), F32),
                 f((own, heads), F32), f((own, heads), F32), f((self.groups, own, self.heads), F32),
                 f((self.groups, self.heads, own), F32), f((own, 3 * heads), BF16), f((own, 3 * heads), BF16),
                 f((own, 3 * heads), BF16), f((8, heads), F32), f((3 * heads, 8), BF16),
@@ -1307,7 +1402,7 @@
             heads_ref[...] = jnp.zeros_like(heads_ref)
             heads_ref[0:1] = grad_shift
             heads_ref[1:2] = rate * grad_log
-            pre = conv_pre(bce_ref, bcw_ref, same_ref, own, taps)
+            pre = conv_pre(bce_ref, bcw_ref, same_ref, slice(0, own), taps)
             gate = jax.nn.sigmoid(pre)
             grad = full_ref[...] * (gate * (1.0 + pre * (1.0 - gate)))
             shift_ref[:HALO] = jnp.zeros((HALO, state2), F32)
@@ -1316,7 +1411,7 @@
             taps_ref[taps : taps + 1] = jnp.sum(grad, axis=0, keepdims=True)
             total = None
             for back in range(taps):
-                masked = grad if back == 0 else grad * same_ref[:, back - 1 : back]
+                masked = grad if back == 0 else grad * same_ref[HALO : HALO + own, back - 1 : back]
                 shift_ref[HALO : HALO + own] = masked
                 piece = bcw_ref[taps - 1 - back : taps - back] * shift_ref[back : back + own + HALO]
                 total = piece if total is None else total + piece
@@ -1446,18 +1541,14 @@
         y, z, squares, cross, gain_row, grad_gate, w_z, entry3, bc, keep3, own_left
     )
 
-    def scattered(pieces):
-        pieces = pieces.reshape(dp_size * size, dp_rows, cols)
-        return lax.psum_scatter(pieces, ALL, scatter_dimension=0, tiled=False).astype(F32)
-
     grid = (dp_size,) + sizes[1:]
-    grad_wo = scattered(out_pieces)
-    leaving, grad_wz = exchange_states(
-        back_local, keep_send, sizes, False, (z_pieces.reshape(grid + (dp_rows, cols)),)
+    leaving, grad_wo = exchange_states(
+        back_local, keep_send, sizes, False, (out_pieces.reshape(grid + (dp_rows, cols)),)
     )
-    conv_sums, head_sums, dots, dbc, dmix, through, x_pieces = scan.s5(
+    conv_sums, head_sums, dots, dbc, dmix, through, x_pieces, grad_wz = scan.s5(
         dy, x_ext, within, conv_rows, skip_rows, same, dt3, tail3, entry3, cum_g, cumt_g, coupling, bias, bc,
-        states, leaving, back_added, keep3, w_x, ext_left
+        states, leaving, back_added, keep3, w_x, ext_left,
+        (z_pieces,), sizes
     )
     part, halo, bc_sums, scan_sums, side_pieces = scan.finish(
         dbc, dmix, bc, bc_ext, bc_rows, same, head_sums, dots, keep, dt, sig, head_rows, w_side, through, own_part,

time: 605 us -> 597 us (0.987)
    pallas_call x2, Pallas kernels: 173 us -> 146 us  [exchange_states(): pl.pallas_call(functools.partial(exchange_kernel, sizes, forward, chunks)...]
    pallas_call x5, Pallas kernels: 168 us -> 189 us  [call(): pl.pallas_call(kernel, grid=(self.groups,), out_shape=[shape for shape, _...]
  transfers between devices with their start and end apart: 5 -> 4, of which waited for: 2 -> 2; matrix products, arithmetic and copies ran while one was open for 7% -> 3% of each run, Pallas kernels for 83% -> 34%
where the time goes in v5:
time: 597 us; the launch traced here: 591 us
  Pallas kernels  519 us (87%)
  local copies, waits for them, and re-layouts  29.8 us (5%)
  other arithmetic  16.1 us (3%)
  between operations  14.9 us (2%)
  waiting for transfers between devices  7.04 us (1%)
    pallas_call x5, Pallas kernels, call(): pl.pallas_call(kernel, grid=(self.groups,), out_shape=[shape for shape, _...  189 us
    pallas_call x2, Pallas kernels, exchange_states(): pl.pallas_call(functools.partial(exchange_kernel, sizes, forward, chunks)...  146 us
    pallas_call x1, Pallas kernels, gather_weights(): pl.pallas_call(functools.partial(gather_kernel, sizes, chunks, kinds), ou...  91.6 us
    pallas_call x1, Pallas kernels, scatter_gradients(): pl.pallas_call(functools.partial(scatter_kernel, sizes, chunks, kinds), o...  72 us
    pallas_call x2, Pallas kernels, alone(): pl.pallas_call(kernel, out_shape=outs, in_specs=[whole] * len(ins), out_s...  20.3 us
  transfers between devices with their start and end apart: 4, of which 2 were waited for; matrix products, arithmetic and copies ran while one was open for 3% of the time, Pallas kernels for 34%

profile of v5, /device:TPU:0, one launch (start us, length us, event | category | flops | bytes accessed | tf_op | source)
XLA Modules:
  0.0 590.8 jit_solution(17227474371554427212)
XLA Ops:
  7.3 2.3 fusion.1
  12.8 91.6 %shard_map.271 = (bf16[4,4,2,48,384]{4,3,2,1,0:T(8,128)(2,1)}, bf16[4,4,2,384,384]{4,3,2,1,0:T(8,128)(2,1)}, f32[4,2,16,384]{3,2,1,0:T(8,128)}) custom-call(bf16[48,384]{1,0:T(8,128)(2,1)} %pad.34.refs_0_, bf16[384,384]{1,0:T(8,128)(2,1)} %bitcast.65, f32[16,384]{1,0:T(8,128)} %select_maximum_fusion.refs_2_), custom_call_target="tpu_custom_call" | custom-call | flops 54000001024 | tf_op jit(solution)/shard_map/pallas_call | solution.py:245
  104.4 2.8 collective-permute-start
  113.6 1.3 slice.169.normed_ref
  115.5 2.2 maximum_convert_fusion
  118.3 10.7 %shard_map.272 = (bf16[4,384,528]{2,1,0:T(8,128)(2,1)}, bf16[4,384,512]{2,1,0:T(8,128)(2,1)}, bf16[4,384,512]{2,1,0:T(8,128)(2,1)}, bf16[384,1536]{1,0:T(8,128)(...) custom-call(bf16[528,1536]{1,0:T(8,128)(2,1)} %copy-done.4, ...), custom_call_target="tpu_custom_call" | custom-call | flops 8999999488 | tf_op jit(solution)/shard_map/pallas_call | solution.py:1254
  129.0 23.1 %shard_map.273 = (f32[528,3072]{1,0:T(8,128)}, f32[512,3072]{1,0:T(8,128)}, f32[512,3072]{1,0:T(8,128)}, f32[4,3072,128]{2,1,0:T(8,128)}, bf16[3072,128]{1,0:T(8,128)(2,1)}) custom-call(bf16[528,1536]{1,0:T(8,128)(2,1)} %copy-done.4, bf16[4,8,384,384]{3,2,1,0:T(8,128)(2,1)} %bitcast.88, f32[8,3072]{1,0:T(8,128)} %bitcast.68, ...), custom_call_target="tpu_custom_call" | custom-call | flops 19800000512 | tf_op jit(solution)/shard_map/pallas_call | solution.py:787
  152.2 54.7 %shard_map.274 = bf16[8,384,128]{2,1,0:T(8,128)(2,1)} custom-call(bf16[8,384,128]{2,1,0:T(8,128)(2,1)} %bitcast.98, bf16[8,16,384]{2,1,0:T(8,128)(2,1)} %get-tuple-element.105.refs_1_), custom_call_target="tpu_custom_call" | custom-call | flops 54000001024 | tf_op jit(solution)/shard_map/pallas_call | solution.py:658
  206.9 20.3 %shard_map.275 = (f32[512,3072]{1,0:T(8,128)}, f32[512,3072]{1,0:T(8,128)}, bf16[4,3072,128]{2,1,0:T(8,128)(2,1)}, f32[512,128]{1,0:T(8,128)}) custom-call(bf16[512,1536]{1,0:T(8,128)(2,1)} %slice.169.normed_ref, bf16[4,8,384,384]{3,2,1,0:T(8,128)(2,1)} %bitcast.85, f32[512,3072]{1,0:T(8,128)} %get-tuple-element.101.within_ref, ...), custom_call_target="tpu_custom_call" | custom-call | flops 19800000512 | tf_op jit(solution)/shard_map/pallas_call | solution.py:787
  227.3 3.2 all-gather.7.cloned.1.call-done
  230.5 30.4 %shard_map.276 = (f32[512,3072]{1,0:T(8,128)}, f32[512,128]{1,0:T(8,128)}, f32[8,3072]{1,0:T(8,128)}, bf16[512,1536]{1,0:T(8,128)(2,1)}, bf16[4,8,384,384]{3,2,1,0:T(8,128)(2,1)}) custom-call(f32[512,3072]{1,0:T(8,128)} %get-tuple-element.107.y_ref, f32[512,3072]{1,0:T(8,128)} %get-tuple-element.108.z_ref, f32[512,128]{1,0:T(8,128)} %get-tuple-element.109.squares_ref, ...), custom_call_target="tpu_custom_call" | custom-call | flops 19800000512 | tf_op jit(solution)/shard_map/pallas_call | solution.py:787
  260.9 28.3 %shard_map.277 = (f32[512,3072]{1,0:T(8,128)}, f32[4,3072,128]{2,1,0:T(8,128)}, bf16[3072,128]{1,0:T(8,128)(2,1)}, f32[512,1536]{1,0:T(8,128)}, bf16[4,8,384,384]{3,2,1,0:T(8,128)(2,1)}) custom-call(f32[512,3072]{1,0:T(8,128)} %get-tuple-element.107.y_ref, f32[512,3072]{1,0:T(8,128)} %get-tuple-element.108.z_ref, f32[512,128]{1,0:T(8,128)} %get-tuple-element.109.squares_ref, ...), custom_call_target="tpu_custom_call" | custom-call | flops 19800000512 | tf_op jit(solution)/shard_map/pallas_call | solution.py:787
  289.2 91.0 %shard_map.278 = (bf16[8,384,128]{2,1,0:T(8,128)(2,1)}, f32[384,384]{1,0:T(8,128)}) custom-call(bf16[8,384,128]{2,1,0:T(8,128)(2,1)} %bitcast.96, bf16[8,16,384]{2,1,0:T(8,128)(2,1)} %get-tuple-element.105.refs_1_, bf16[4,4,2,384,384]{4,3,2,1,0:T(8,128)(2,1)} %bitcast.92), custom_call_target="tpu_custom_call" | custom-call | flops 54000001024 | tf_op jit(solution)/shard_map/pallas_call | solution.py:658
  380.3 86.9 %shard_map.279 = (f32[8,3072]{1,0:T(8,128)}, f32[3,512,128]{2,1,0:T(8,128)}, f32[4,128,128]{2,1,0:T(8,128)}, f32[512,256]{1,0:T(8,128)}, f32[4,128,128]{2,1,0:T(...) custom-call(f32[512,3072]{1,0:T(8,128)} %get-tuple-element.116.dy_ref, ...), custom_call_target="tpu_custom_call" | custom-call | flops 19800000512 | tf_op jit(solution)/shard_map/pallas_call | solution.py:787
  467.3 9.6 %shard_map.280 = (f32[512,1536]{1,0:T(8,128)}, f32[16,1536]{1,0:T(8,128)}, f32[8,256]{1,0:T(8,128)}, f32[8,48]{1,0:T(8,128)}, bf16[4,384,384]{2,1,0:T(8,128)(2,1)}) custom-call(f32[512,256]{1,0:T(8,128)} %get-tuple-element.125.dbc_ref, f32[4,128,128]{2,1,0:T(8,128)} %get-tuple-element.126.dmix_ref, bf16[512,256]{1,0:T(8,128)(2,1)} %get-tuple-element.99.bc_ref, ...), custom_call_target="tpu_custom_call" | custom-call | flops 10800000000 | tf_op jit(solution)/shard_map/pallas_call | solution.py:1254
  480.8 3.7 collective-permute-done.1
  484.6 1.5 add_dynamic-update-slice_fusion
  486.1 2.7 multiply_reduce_fusion.1
  489.5 72.0 %shard_map.281 = (bf16[4,2,48,384]{3,2,1,0:T(8,128)(2,1)}, f32[384,384]{1,0:T(8,128)}, f32[8,3072]{1,0:T(8,128)}) custom-call(bf16[4,4,2,48,384]{4,3,2,1,0:T(8,128)(2,1)} %bitcast.94, bf16[4,4,2,384,384]{4,3,2,1,0:T(8,128)(2,1)} %bitcast.90, f32[8,3072]{1,0:T(8,128)} %pad_maximum_fusion.1.refs_2_), custom_call_target="tpu_custom_call" | custom-call | flops 54000001024 | tf_op jit(solution)/shard_map/pallas_call | solution.py:545
  563.1 1.4 slice_reduce_fusion.1
  566.9 1.9 copy.41
  570.5 1.9 copy.42
  576.3 1.5 dynamic-slice_reduce_fusion
  577.8 4.9 multiply_subtract_fusion
  (113 shorter events, 25.7 us)
Async XLA Ops:
  7.2 4.3 copy-start.19
  7.2 4.3 copy-start.20
  7.2 4.9 copy-start.24
  7.2 4.9 copy-start.23
  7.2 4.9 copy-start.22
  7.3 4.9 copy-start.16
  7.3 199.7 %all-gather.5.cloned.1.call-start = ((), (), s32[]{:S(2)}) async-start(), calls=%async_computation | async-start | bytes 9732096 | tf_op jit(solution)/shard_map/all_gather | solution.py:1497
  10.4 220.1 %all-gather.7.cloned.1.call-start = ((), (), s32[]{:S(2)}) async-start(), calls=%async_computation.1 | async-start | bytes 9732096 | tf_op jit(solution)/shard_map/all_gather | solution.py:1497
  12.8 91.6 %copy-start.3 = (bf16[512,1536]{1,0:T(8,128)(2,1)S(1)}, bf16[512,1536]{1,0:T(8,128)(2,1)}, u32[]{:S(2)}) copy-start(bf16[512,1536]{1,0:T(8,128)(2,1)} %residual_ref.1) | copy-start | bytes 4718596
  12.8 95.5 %copy-start.18 = (f32[4,256]{1,0:T(4,128)S(1)}, f32[4,256]{1,0:T(4,128)}, u32[]{:S(2)}) copy-start(f32[4,256]{1,0:T(4,128)} %param.26) | copy-start | bytes 12292
  12.8 95.5 %copy-start.21 = (f32[256]{0:T(256)S(1)}, f32[256]{0:T(256)}, u32[]{:S(2)}) copy-start(f32[256]{0:T(256)} %param.27) | copy-start | bytes 3076
  12.8 96.1 %copy-start.14 = (s32[1,4096]{1,0:T(1,128)S(1)}, s32[1,4096]{1,0:T(1,128)}, u32[]{:S(2)}) copy-start(s32[1,4096]{1,0:T(1,128)} %param.19) | copy-start | bytes 49156
  104.4 8.8 %copy-start.10 = (f32[1536]{0:T(1024)S(1)}, f32[1536]{0:T(1024)}, u32[]{:S(2)}) copy-start(f32[1536]{0:T(1024)} %param.20) | copy-start | bytes 18436
  104.4 8.3 %collective-permute-start = (bf16[16,1536]{1,0:T(8,128)(2,1)S(1)}, bf16[16,1536]{1,0:T(8,128)(2,1)S(1)}, u32[]{:S(2)}, u32[]{:S(2)}) collective-permute-start(bf16[16,1536]{1,0:T(8,128)(2,1)S(1)} %slice.133), channel_id=1, source_target_pairs={{0,1},{1,2},{2,3},{3,4},{4,5},{5,6},{6,7},{8,9},{9,10},{10,11},{11... | collective-permute-start | bytes 147464 | tf_op jit(solution)/shard_map/ppermute | solution.py:1449
  467.2 12.4 %copy-start.9 = (f32[8,3072]{1,0:T(8,128)S(1)}, f32[8,3072]{1,0:T(8,128)}, u32[]{:S(2)}) copy-start(f32[8,3072]{1,0:T(8,128)} %get-tuple-element.140) | copy-start | bytes 294916
  467.2 18.9 %copy-start.2 = (f32[528,1536]{1,0:T(8,128)S(1)}, f32[528,1536]{1,0:T(8,128)}, u32[]{:S(2)}) copy-start(f32[528,1536]{1,0:T(8,128)} %maximum_convert_fusion) | copy-start | bytes 9732100
  467.2 18.9 %copy-start.11 = (f32[1536]{0:T(1024)S(1)}, f32[1536]{0:T(1024)}, u32[]{:S(2)}) copy-start(f32[1536]{0:T(1024)} %param.20) | copy-start | bytes 18436
  467.2 18.9 %copy-start.13 = (f32[512]{0:T(512)S(1)}, f32[512]{0:T(512)}, u32[]{:S(2)}) copy-start(f32[512]{0:T(512)} %copy-done.12) | copy-start | bytes 6148
  476.9 7.7 %collective-permute-start.1 = (f32[16,1536]{1,0:T(8,128)}, f32[16,1536]{1,0:T(8,128)S(1)}, u32[]{:S(2)}, u32[]{:S(2)}) collective-permute-start(f32[16,1536]{1,0:T(8,128)} %get-tuple-element.137), channel_id=1, source_target_pairs={{1,0},{2,1},{3,2},{4,3},{5,4},{6,5},{7,6},{9,8},{10,9},{11,10},{12... | collective-permute-start | bytes 294920 | tf_op jit(solution)/shard_map/ppermute | solution.py:1453
  489.5 76.2 %copy-start.7 = (f32[384,384]{1,0:T(8,128)S(1)}, f32[384,384]{1,0:T(8,128)}, u32[]{:S(2)}) copy-start(f32[384,384]{1,0:T(8,128)} %get-tuple-element.145) | copy-start | bytes 1769476
  561.5 7.3 %copy-start.8 = (bf16[4,2,48,384]{3,2,1,0:T(8,128)(2,1)S(1)}, bf16[4,2,48,384]{3,2,1,0:T(8,128)(2,1)}, u32[]{:S(2)}) copy-start(bf16[4,2,48,384]{3,2,1,0:T(8,128)(2,1)} %get-tuple-element.147) | copy-start | bytes 884740
  565.7 12.0 %copy-start.15 = (f32[512,1]{0,1:T(1,128)S(1)}, f32[512,1]{0,1:T(1,128)}, u32[]{:S(2)}) copy-start(f32[512,1]{0,1:T(1,128)} %multiply_multiply_fusion) | copy-start | bytes 6148
  577.8 4.9 copy-start.6
  577.8 5.7 copy-start.1
  (5 other events, 14.3 us)
Sparse Core Ops, SparseCore 0:
  11.6 107.5 all-gather.4
  122.1 108.3 all-gather.6

commit v6 on v5

--- a/solution.py
+++ b/solution.py
@@ -10,8 +10,8 @@
 EPSILON = 1e-05
 CHUNK = 128
 HALO = 16
-AHEAD = 2
-LAGS = (0, 1, 3, 5)
+AHEAD = 4
+LAGS = (0, 2, 4, 6)
 HOSTED_LAGS = (0, 4, 6, 8)
 SLOTS = 2
 CHUNK_ROWS = 48
@@ -506,12 +506,12 @@
     for one in small_stage(0):
         one.start()
     begin(False)
-    for tick in range(max(ticks, 9)):
+    for tick in range(max(ticks, LAGS[3] + 3)):
         step_on(tick)
-        if tick == 5:
+        if tick == LAGS[3]:
             for one in side_tensor:
                 one.start()
-        if tick == 7:
+        if tick == LAGS[3] + 2:
             for one in side_tensor:
                 one.wait_recv()
             for one in side_head:

time: 597 us -> 594 us (level)
  no operation moved by 1% of the time
where the time goes in v6:
time: 594 us; the launch traced here: 587 us
  Pallas kernels  515 us (87%)
  local copies, waits for them, and re-layouts  29.8 us (5%)
  other arithmetic  16.1 us (3%)
  between operations  14.9 us (3%)
  waiting for transfers between devices  7.04 us (1%)
    pallas_call x5, Pallas kernels, call(): pl.pallas_call(kernel, grid=(self.groups,), out_shape=[shape for shape, _...  188 us
    pallas_call x2, Pallas kernels, exchange_states(): pl.pallas_call(functools.partial(exchange_kernel, sizes, forward, chunks)...  145 us
    pallas_call x1, Pallas kernels, gather_weights(): pl.pallas_call(functools.partial(gather_kernel, sizes, chunks, kinds), ou...  91.6 us
    pallas_call x1, Pallas kernels, scatter_gradients(): pl.pallas_call(functools.partial(scatter_kernel, sizes, chunks, kinds), o...  69.7 us
    pallas_call x2, Pallas kernels, alone(): pl.pallas_call(kernel, out_shape=outs, in_specs=[whole] * len(ins), out_s...  20.3 us
  transfers between devices with their start and end apart: 4, of which 2 were waited for; matrix products, arithmetic and copies ran while one was open for 3% of the time, Pallas kernels for 34%

profile of v6, /device:TPU:0, one launch (start us, length us, event | category | flops | bytes accessed | tf_op | source)
XLA Modules:
  0.0 587.0 jit_solution(15937540158137961224)
XLA Ops:
  7.3 2.3 fusion.1
  12.8 91.6 %shard_map.271 = (bf16[4,4,2,48,384]{4,3,2,1,0:T(8,128)(2,1)}, bf16[4,4,2,384,384]{4,3,2,1,0:T(8,128)(2,1)}, f32[4,2,16,384]{3,2,1,0:T(8,128)}) custom-call(bf16[48,384]{1,0:T(8,128)(2,1)} %pad.34.refs_0_, bf16[384,384]{1,0:T(8,128)(2,1)} %bitcast.65, f32[16,384]{1,0:T(8,128)} %select_maximum_fusion.refs_2_), custom_call_target="tpu_custom_call" | custom-call | flops 54000001024 | tf_op jit(solution)/shard_map/pallas_call | solution.py:245
  104.4 2.8 collective-permute-start
  113.6 1.3 slice.169.normed_ref
  115.5 2.2 maximum_convert_fusion
  118.3 10.7 %shard_map.272 = (bf16[4,384,528]{2,1,0:T(8,128)(2,1)}, bf16[4,384,512]{2,1,0:T(8,128)(2,1)}, bf16[4,384,512]{2,1,0:T(8,128)(2,1)}, bf16[384,1536]{1,0:T(8,128)(...) custom-call(bf16[528,1536]{1,0:T(8,128)(2,1)} %copy-done.4, ...), custom_call_target="tpu_custom_call" | custom-call | flops 8999999488 | tf_op jit(solution)/shard_map/pallas_call | solution.py:1254
  129.0 23.1 %shard_map.273 = (f32[528,3072]{1,0:T(8,128)}, f32[512,3072]{1,0:T(8,128)}, f32[512,3072]{1,0:T(8,128)}, f32[4,3072,128]{2,1,0:T(8,128)}, bf16[3072,128]{1,0:T(8,128)(2,1)}) custom-call(bf16[528,1536]{1,0:T(8,128)(2,1)} %copy-done.4, bf16[4,8,384,384]{3,2,1,0:T(8,128)(2,1)} %bitcast.88, f32[8,3072]{1,0:T(8,128)} %bitcast.68, ...), custom_call_target="tpu_custom_call" | custom-call | flops 19800000512 | tf_op jit(solution)/shard_map/pallas_call | solution.py:787
  152.2 54.7 %shard_map.274 = bf16[8,384,128]{2,1,0:T(8,128)(2,1)} custom-call(bf16[8,384,128]{2,1,0:T(8,128)(2,1)} %bitcast.98, bf16[8,16,384]{2,1,0:T(8,128)(2,1)} %get-tuple-element.105.refs_1_), custom_call_target="tpu_custom_call" | custom-call | flops 54000001024 | tf_op jit(solution)/shard_map/pallas_call | solution.py:658
  206.9 20.3 %shard_map.275 = (f32[512,3072]{1,0:T(8,128)}, f32[512,3072]{1,0:T(8,128)}, bf16[4,3072,128]{2,1,0:T(8,128)(2,1)}, f32[512,128]{1,0:T(8,128)}) custom-call(bf16[512,1536]{1,0:T(8,128)(2,1)} %slice.169.normed_ref, bf16[4,8,384,384]{3,2,1,0:T(8,128)(2,1)} %bitcast.85, f32[512,3072]{1,0:T(8,128)} %get-tuple-element.101.within_ref, ...), custom_call_target="tpu_custom_call" | custom-call | flops 19800000512 | tf_op jit(solution)/shard_map/pallas_call | solution.py:787
  227.3 3.2 all-gather.7.cloned.1.call-done
  230.5 30.4 %shard_map.276 = (f32[512,3072]{1,0:T(8,128)}, f32[512,128]{1,0:T(8,128)}, f32[8,3072]{1,0:T(8,128)}, bf16[512,1536]{1,0:T(8,128)(2,1)}, bf16[4,8,384,384]{3,2,1,0:T(8,128)(2,1)}) custom-call(f32[512,3072]{1,0:T(8,128)} %get-tuple-element.107.y_ref, f32[512,3072]{1,0:T(8,128)} %get-tuple-element.108.z_ref, f32[512,128]{1,0:T(8,128)} %get-tuple-element.109.squares_ref, ...), custom_call_target="tpu_custom_call" | custom-call | flops 19800000512 | tf_op jit(solution)/shard_map/pallas_call | solution.py:787
  260.9 28.3 %shard_map.277 = (f32[512,3072]{1,0:T(8,128)}, f32[4,3072,128]{2,1,0:T(8,128)}, bf16[3072,128]{1,0:T(8,128)(2,1)}, f32[512,1536]{1,0:T(8,128)}, bf16[4,8,384,384]{3,2,1,0:T(8,128)(2,1)}) custom-call(f32[512,3072]{1,0:T(8,128)} %get-tuple-element.107.y_ref, f32[512,3072]{1,0:T(8,128)} %get-tuple-element.108.z_ref, f32[512,128]{1,0:T(8,128)} %get-tuple-element.109.squares_ref, ...), custom_call_target="tpu_custom_call" | custom-call | flops 19800000512 | tf_op jit(solution)/shard_map/pallas_call | solution.py:787
  289.2 90.4 %shard_map.278 = (bf16[8,384,128]{2,1,0:T(8,128)(2,1)}, f32[384,384]{1,0:T(8,128)}) custom-call(bf16[8,384,128]{2,1,0:T(8,128)(2,1)} %bitcast.96, bf16[8,16,384]{2,1,0:T(8,128)(2,1)} %get-tuple-element.105.refs_1_, bf16[4,4,2,384,384]{4,3,2,1,0:T(8,128)(2,1)} %bitcast.92), custom_call_target="tpu_custom_call" | custom-call | flops 54000001024 | tf_op jit(solution)/shard_map/pallas_call | solution.py:658
  379.6 86.2 %shard_map.279 = (f32[8,3072]{1,0:T(8,128)}, f32[3,512,128]{2,1,0:T(8,128)}, f32[4,128,128]{2,1,0:T(8,128)}, f32[512,256]{1,0:T(8,128)}, f32[4,128,128]{2,1,0:T(...) custom-call(f32[512,3072]{1,0:T(8,128)} %get-tuple-element.116.dy_ref, ...), custom_call_target="tpu_custom_call" | custom-call | flops 19800000512 | tf_op jit(solution)/shard_map/pallas_call | solution.py:787
  465.8 9.6 %shard_map.280 = (f32[512,1536]{1,0:T(8,128)}, f32[16,1536]{1,0:T(8,128)}, f32[8,256]{1,0:T(8,128)}, f32[8,48]{1,0:T(8,128)}, bf16[4,384,384]{2,1,0:T(8,128)(2,1)}) custom-call(f32[512,256]{1,0:T(8,128)} %get-tuple-element.125.dbc_ref, f32[4,128,128]{2,1,0:T(8,128)} %get-tuple-element.126.dmix_ref, bf16[512,256]{1,0:T(8,128)(2,1)} %get-tuple-element.99.bc_ref, ...), custom_call_target="tpu_custom_call" | custom-call | flops 10800000000 | tf_op jit(solution)/shard_map/pallas_call | solution.py:1254
  479.4 3.7 collective-permute-done.1
  483.1 1.5 add_dynamic-update-slice_fusion
  484.7 2.7 multiply_reduce_fusion.1
  488.0 69.7 %shard_map.281 = (bf16[4,2,48,384]{3,2,1,0:T(8,128)(2,1)}, f32[384,384]{1,0:T(8,128)}, f32[8,3072]{1,0:T(8,128)}) custom-call(bf16[4,4,2,48,384]{4,3,2,1,0:T(8,128)(2,1)} %bitcast.94, bf16[4,4,2,384,384]{4,3,2,1,0:T(8,128)(2,1)} %bitcast.90, f32[8,3072]{1,0:T(8,128)} %pad_maximum_fusion.1.refs_2_), custom_call_target="tpu_custom_call" | custom-call | flops 54000001024 | tf_op jit(solution)/shard_map/pallas_call | solution.py:545
  559.3 1.4 slice_reduce_fusion.1
  563.1 1.9 copy.41
  566.7 1.9 copy.42
  572.5 1.5 dynamic-slice_reduce_fusion
  574.0 4.9 multiply_subtract_fusion
  (113 shorter events, 25.7 us)
Async XLA Ops:
  7.2 4.3 copy-start.19
  7.2 4.3 copy-start.20
  7.2 4.9 copy-start.24
  7.2 4.9 copy-start.23
  7.2 4.9 copy-start.22
  7.3 4.9 copy-start.16
  7.3 199.7 %all-gather.5.cloned.1.call-start = ((), (), s32[]{:S(2)}) async-start(), calls=%async_computation | async-start | bytes 9732096 | tf_op jit(solution)/shard_map/all_gather | solution.py:1497
  10.4 220.1 %all-gather.7.cloned.1.call-start = ((), (), s32[]{:S(2)}) async-start(), calls=%async_computation.1 | async-start | bytes 9732096 | tf_op jit(solution)/shard_map/all_gather | solution.py:1497
  12.8 91.6 %copy-start.3 = (bf16[512,1536]{1,0:T(8,128)(2,1)S(1)}, bf16[512,1536]{1,0:T(8,128)(2,1)}, u32[]{:S(2)}) copy-start(bf16[512,1536]{1,0:T(8,128)(2,1)} %residual_ref.1) | copy-start | bytes 4718596
  12.8 95.5 %copy-start.18 = (f32[4,256]{1,0:T(4,128)S(1)}, f32[4,256]{1,0:T(4,128)}, u32[]{:S(2)}) copy-start(f32[4,256]{1,0:T(4,128)} %param.26) | copy-start | bytes 12292
  12.8 95.5 %copy-start.21 = (f32[256]{0:T(256)S(1)}, f32[256]{0:T(256)}, u32[]{:S(2)}) copy-start(f32[256]{0:T(256)} %param.27) | copy-start | bytes 3076
  12.8 96.1 %copy-start.14 = (s32[1,4096]{1,0:T(1,128)S(1)}, s32[1,4096]{1,0:T(1,128)}, u32[]{:S(2)}) copy-start(s32[1,4096]{1,0:T(1,128)} %param.19) | copy-start | bytes 49156
  104.4 8.8 %copy-start.10 = (f32[1536]{0:T(1024)S(1)}, f32[1536]{0:T(1024)}, u32[]{:S(2)}) copy-start(f32[1536]{0:T(1024)} %param.20) | copy-start | bytes 18436
  104.4 8.3 %collective-permute-start = (bf16[16,1536]{1,0:T(8,128)(2,1)S(1)}, bf16[16,1536]{1,0:T(8,128)(2,1)S(1)}, u32[]{:S(2)}, u32[]{:S(2)}) collective-permute-start(bf16[16,1536]{1,0:T(8,128)(2,1)S(1)} %slice.133), channel_id=1, source_target_pairs={{0,1},{1,2},{2,3},{3,4},{4,5},{5,6},{6,7},{8,9},{9,10},{10,11},{11... | collective-permute-start | bytes 147464 | tf_op jit(solution)/shard_map/ppermute | solution.py:1449
  465.8 12.4 %copy-start.9 = (f32[8,3072]{1,0:T(8,128)S(1)}, f32[8,3072]{1,0:T(8,128)}, u32[]{:S(2)}) copy-start(f32[8,3072]{1,0:T(8,128)} %get-tuple-element.140) | copy-start | bytes 294916
  465.8 18.9 %copy-start.2 = (f32[528,1536]{1,0:T(8,128)S(1)}, f32[528,1536]{1,0:T(8,128)}, u32[]{:S(2)}) copy-start(f32[528,1536]{1,0:T(8,128)} %maximum_convert_fusion) | copy-start | bytes 9732100
  465.8 18.9 %copy-start.11 = (f32[1536]{0:T(1024)S(1)}, f32[1536]{0:T(1024)}, u32[]{:S(2)}) copy-start(f32[1536]{0:T(1024)} %param.20) | copy-start | bytes 18436
  465.8 18.9 %copy-start.13 = (f32[512]{0:T(512)S(1)}, f32[512]{0:T(512)}, u32[]{:S(2)}) copy-start(f32[512]{0:T(512)} %copy-done.12) | copy-start | bytes 6148
  475.4 7.7 %collective-permute-start.1 = (f32[16,1536]{1,0:T(8,128)}, f32[16,1536]{1,0:T(8,128)S(1)}, u32[]{:S(2)}, u32[]{:S(2)}) collective-permute-start(f32[16,1536]{1,0:T(8,128)} %get-tuple-element.137), channel_id=1, source_target_pairs={{1,0},{2,1},{3,2},{4,3},{5,4},{6,5},{7,6},{9,8},{10,9},{11,10},{12... | collective-permute-start | bytes 294920 | tf_op jit(solution)/shard_map/ppermute | solution.py:1453
  488.0 73.9 %copy-start.7 = (f32[384,384]{1,0:T(8,128)S(1)}, f32[384,384]{1,0:T(8,128)}, u32[]{:S(2)}) copy-start(f32[384,384]{1,0:T(8,128)} %get-tuple-element.145) | copy-start | bytes 1769476
  557.7 7.3 %copy-start.8 = (bf16[4,2,48,384]{3,2,1,0:T(8,128)(2,1)S(1)}, bf16[4,2,48,384]{3,2,1,0:T(8,128)(2,1)}, u32[]{:S(2)}) copy-start(bf16[4,2,48,384]{3,2,1,0:T(8,128)(2,1)} %get-tuple-element.147) | copy-start | bytes 884740
  561.9 12.0 %copy-start.15 = (f32[512,1]{0,1:T(1,128)S(1)}, f32[512,1]{0,1:T(1,128)}, u32[]{:S(2)}) copy-start(f32[512,1]{0,1:T(1,128)} %multiply_multiply_fusion) | copy-start | bytes 6148
  574.0 4.9 copy-start.6
  574.0 5.7 copy-start.1
  (5 other events, 14.3 us)
Sparse Core Ops, SparseCore 0:
  11.6 107.5 all-gather.4
  122.1 108.3 all-gather.6
